TPU v7x, 32 devices: a whole 2x2x4 slice. The times are simulated.
32 devices in a mesh: dp: 8 (over y, x, core), tensor: 4 (over z).
Axes of the slice: x: 2, y: 2, z: 4, core: 2. Of those that a mesh axis runs over, the one named last changes fastest.
Arguments:
- inputs: bfloat16 [16384, 512], P(('dp', 'tensor')), may hold values from -6 to 6
- segment_ids: int32 [16384], P('dp'), may hold values from -1 to 7, as said below
- query_weight: bfloat16 [512, 512], P(None, 'tensor'), may hold values from -0.25 to 0.25
- query_bias: float32 [512], P('tensor'), may hold values from -3 to 3
- key_weight: bfloat16 [512, 512], P(None, 'tensor'), may hold values from -0.25 to 0.25
- value_weight: bfloat16 [512, 512], P(None, 'tensor'), may hold values from -0.25 to 0.25
- value_bias: float32 [512], P('tensor'), may hold values from -3 to 3
- out_weight: bfloat16 [512, 512], P('tensor'), may hold values from -1 to 1
- out_bias: float32 [512], replicated, may hold values from -2 to 2
- first_gain: float32 [512], replicated, may hold values from 0.5 to 1.5
- first_shift: float32 [512], replicated, may hold values from -2 to 2
- up_weight: bfloat16 [512, 2048], P(None, 'tensor'), may hold values from -0.25 to 0.25
- up_bias: float32 [2048], P('tensor'), may hold values from -2 to 2
- down_weight: bfloat16 [2048, 512], P('tensor'), may hold values from -0.1875 to 0.1875
- down_bias: float32 [512], replicated, may hold values from -2 to 2
- second_gain: float32 [512], replicated, may hold values from 0.5 to 1.5
- second_shift: float32 [512], replicated, may hold values from -2 to 2
- cotangent: bfloat16 [16384, 512], P(('dp', 'tensor')), may hold values from -6 to 6
Outputs:
- result: bfloat16 [16384, 512], P(('dp', 'tensor'))
- input_grad: float32 [16384, 512], P(('dp', 'tensor'))
- query_weight_grad: float32 [512, 512], P(None, 'tensor')
- query_bias_grad: float32 [512], P('tensor')
- key_weight_grad: float32 [512, 512], P(None, 'tensor')
- value_weight_grad: float32 [512, 512], P(None, 'tensor')
- value_bias_grad: float32 [512], P('tensor')
- out_weight_grad: float32 [512, 512], P('tensor')
- out_bias_grad: float32 [512], replicated
- first_gain_grad: float32 [512], replicated
- first_shift_grad: float32 [512], replicated
- up_weight_grad: float32 [512, 2048], P(None, 'tensor')
- up_bias_grad: float32 [2048], P('tensor')
- down_weight_grad: float32 [2048, 512], P('tensor')
- down_bias_grad: float32 [512], replicated
- second_gain_grad: float32 [512], replicated
- second_shift_grad: float32 [512], replicated
Inputs may be any that keep to these rules, and one draw needn't show every extreme that they name: `segment_ids`: each packed sequence of 1024 tokens holds documents numbered 0 to 7 in order (some may be empty), then 1024 / 16 to 128 tokens of padding numbered -1.
All inputs are finite; a program needn't handle non-finite values.
Results may differ from a plain program's by a relative error of at most 0.03.
Values may be sent and summed in bfloat16 or wider, within the bound.
No kernel may reach another device: no remote copies, remote signals or barrier semaphores. Data moves between devices by JAX's collectives and lax.ppermute only.
A program may use at most 128 MiB of HBM per device.

v0:
```python
import math

import jax
import jax.numpy as jnp
from jax import lax
from jax.sharding import PartitionSpec as P

HEAD_DIM = 64
LEN = 1024


epsilon = 1e-05


def layer_norm(hidden, norm_gain, norm_shift):
    center = hidden - jnp.mean(hidden, -1, keepdims=True)
    spread = jnp.mean(center * center, -1, keepdims=True)
    return center * lax.rsqrt(spread + epsilon) * norm_gain + norm_shift


def contract_first(operand, weight):
    return lax.dot_general(
        operand, weight, (((0,), (0,)), ((), ())), preferred_element_type=jnp.float32
    )


def contract_last(operand, weight):
    return lax.dot_general(
        operand, weight, (((1,), (1,)), ((), ())), preferred_element_type=jnp.float32
    )


def gather_rows(shard):
    return lax.all_gather(shard, "tensor", axis=0, tiled=True)


def scatter_rows(operand, weight, row_count):

    def partial_value(first_row, span):
        return jnp.dot(operand, weight, preferred_element_type=jnp.float32)

    return lax.psum_scatter(
        partial_value(jnp.int32(0), row_count * lax.axis_size("tensor")).astype(jnp.bfloat16),
        "tensor",
        scatter_dimension=0,
        tiled=True,
    ).astype(jnp.float32)


def gather_grads(shard):
    return lax.all_gather(shard, "tensor", axis=0, tiled=True)


def scatter_grads(operand, weight, row_count):

    def partial_value(first_row, span):
        return contract_last(operand, weight)

    return lax.psum_scatter(
        partial_value(jnp.int32(0), row_count * lax.axis_size("tensor")).astype(jnp.bfloat16),
        "tensor",
        scatter_dimension=0,
        tiled=True,
    ).astype(jnp.float32)


def masked_scores(queries, key_heads, labels):
    scores = jnp.einsum("qhd,khd->hqk", queries, key_heads, preferred_element_type=jnp.float32) * (
        1.0 / math.sqrt(HEAD_DIM)
    )
    allowed = (labels[:, None] == labels[None, :])[None]
    return jnp.where(allowed, scores, -1000000000.0)


def attend(pieces):
    queries, key_heads, values, labels = pieces
    scores = masked_scores(queries, key_heads, labels)
    row_max = jnp.max(scores, -1, keepdims=True)
    exponent = jnp.exp(scores - row_max)
    row_sum = jnp.sum(exponent, -1, keepdims=True)
    attn_probs = (exponent / row_sum).astype(jnp.bfloat16)
    attended = jnp.einsum(
        "hqk,khd->qhd", attn_probs, values, preferred_element_type=jnp.float32
    ).astype(jnp.bfloat16)
    return (attended, (row_max + jnp.log(row_sum))[..., 0])


def attend_back(pieces):
    queries, key_heads, values, labels, log_total, grad_mixed = pieces
    scores = masked_scores(queries, key_heads, labels)
    attn_probs = jnp.exp(scores - log_total[..., None])
    grad_probs = jnp.einsum("qhd,khd->hqk", grad_mixed, values, preferred_element_type=jnp.float32)
    row_dot = jnp.sum(attn_probs * grad_probs, -1, keepdims=True)
    grad_scores = (attn_probs * (grad_probs - row_dot)).astype(jnp.bfloat16)
    inv_scale = 1.0 / math.sqrt(HEAD_DIM)
    grad_queries = (
        jnp.einsum("hqk,khd->qhd", grad_scores, key_heads, preferred_element_type=jnp.float32)
        * inv_scale
    ).astype(jnp.bfloat16)
    grad_key_heads = (
        jnp.einsum("hqk,qhd->khd", grad_scores, queries, preferred_element_type=jnp.float32)
        * inv_scale
    ).astype(jnp.bfloat16)
    grad_values = jnp.einsum(
        "hqk,qhd->khd",
        attn_probs.astype(jnp.bfloat16),
        grad_mixed,
        preferred_element_type=jnp.float32,
    ).astype(jnp.bfloat16)
    return (grad_queries, grad_key_heads, grad_values)


def forward_layer(layer_in, labels, weights):
    (
        stacked,
        stacked_bias,
        out_weight,
        out_bias,
        first_gain,
        first_shift,
        up_weight,
        up_bias,
        down_weight,
        down_bias,
        second_gain,
        second_shift,
    ) = weights
    row_count = layer_in.shape[0]
    gathered = gather_rows(layer_in.astype(jnp.bfloat16))
    total_rows = gathered.shape[0]
    seq_count = total_rows // LEN
    head_width = stacked.shape[1] // 3
    head_count = head_width // HEAD_DIM
    proj_low = (
        jnp.dot(gathered, stacked, preferred_element_type=jnp.float32) + stacked_bias
    ).astype(jnp.bfloat16)
    queries = proj_low[:, :head_width].reshape(seq_count, LEN, head_count, HEAD_DIM)
    key_heads = proj_low[:, head_width : 2 * head_width].reshape(
        seq_count, LEN, head_count, HEAD_DIM
    )
    values = proj_low[:, 2 * head_width :].reshape(seq_count, LEN, head_count, HEAD_DIM)
    attended, log_total = lax.map(
        attend, (queries, key_heads, values, labels.reshape(seq_count, LEN))
    )
    attended = attended.reshape(total_rows, head_width)
    pre_one = layer_in + scatter_rows(attended, out_weight, row_count) + out_bias
    middle = layer_norm(pre_one, first_gain, first_shift)
    middle_low = middle.astype(jnp.bfloat16)
    ffn_rows = gather_rows(middle_low)
    hidden_pre = jnp.dot(ffn_rows, up_weight, preferred_element_type=jnp.float32) + up_bias
    activated = jax.nn.gelu(hidden_pre).astype(jnp.bfloat16)
    branch_two = scatter_rows(activated, down_weight, row_count)
    pre_two = middle + branch_two + down_bias
    layer_out = layer_norm(pre_two, second_gain, second_shift)
    saved = (
        gathered,
        proj_low,
        attended,
        log_total,
        pre_one,
        ffn_rows,
        hidden_pre,
        activated,
        pre_two,
    )
    return (layer_out, saved)


def backward_layer(saved, grad_out, labels, weights):
    (
        stacked,
        stacked_bias,
        out_weight,
        out_bias,
        first_gain,
        first_shift,
        up_weight,
        up_bias,
        down_weight,
        down_bias,
        second_gain,
        second_shift,
    ) = weights
    gathered, proj_low, attended, log_total, pre_one, ffn_rows, hidden_pre, activated, pre_two = (
        saved
    )
    row_count = grad_out.shape[0]
    total_rows = gathered.shape[0]
    seq_count = total_rows // LEN
    head_width = stacked.shape[1] // 3
    head_count = head_width // HEAD_DIM
    unused, pull_two = jax.vjp(layer_norm, pre_two, second_gain, second_shift)
    grad_pre_two, grad_second_gain, grad_second_shift = pull_two(grad_out)
    grad_branch_two = grad_pre_two.astype(jnp.bfloat16)
    grad_down_bias = jnp.sum(grad_branch_two.astype(jnp.float32), 0)
    grad_rows_two = gather_grads(grad_branch_two)
    grad_down = contract_first(activated, grad_rows_two)
    grad_act = contract_last(grad_rows_two, down_weight)
    unused_gelu, pull_gelu = jax.vjp(jax.nn.gelu, hidden_pre)
    grad_hidden = pull_gelu(grad_act)[0].astype(jnp.bfloat16)
    grad_up_bias = jnp.sum(grad_hidden.astype(jnp.float32), 0)
    grad_up = contract_first(ffn_rows, grad_hidden)
    grad_middle = grad_pre_two + scatter_grads(grad_hidden, up_weight, row_count)
    unused_one, pull_one = jax.vjp(layer_norm, pre_one, first_gain, first_shift)
    grad_pre_one, grad_first_gain, grad_first_shift = pull_one(grad_middle)
    grad_branch_one = grad_pre_one.astype(jnp.bfloat16)
    grad_out_bias = jnp.sum(grad_branch_one.astype(jnp.float32), 0)
    grad_rows_one = gather_grads(grad_branch_one)
    grad_out_weight = contract_first(attended, grad_rows_one)
    grad_attended = contract_last(grad_rows_one, out_weight).astype(jnp.bfloat16)
    queries = proj_low[:, :head_width].reshape(seq_count, LEN, head_count, HEAD_DIM)
    key_heads = proj_low[:, head_width : 2 * head_width].reshape(
        seq_count, LEN, head_count, HEAD_DIM
    )
    values = proj_low[:, 2 * head_width :].reshape(seq_count, LEN, head_count, HEAD_DIM)
    grad_queries, grad_key_heads, grad_values = lax.map(
        attend_back,
        (
            queries,
            key_heads,
            values,
            labels.reshape(seq_count, LEN),
            log_total,
            grad_attended.reshape(seq_count, LEN, head_count, HEAD_DIM),
        ),
    )
    grad_proj = jnp.concatenate(
        (
            grad_queries.reshape(total_rows, head_width),
            grad_key_heads.reshape(total_rows, head_width),
            grad_values.reshape(total_rows, head_width),
        ),
        1,
    )
    grad_stacked = contract_first(gathered, grad_proj)
    grad_query_bias = jnp.sum(grad_proj[:, :head_width].astype(jnp.float32), 0)
    grad_value_bias = jnp.sum(grad_proj[:, 2 * head_width :].astype(jnp.float32), 0)
    grad_in = grad_pre_one + scatter_grads(grad_proj, stacked, row_count)
    split_terms = (
        grad_stacked,
        grad_query_bias,
        grad_value_bias,
        grad_out_weight,
        grad_up,
        grad_up_bias,
        grad_down,
    )
    shared_terms = (
        grad_out_bias,
        grad_first_gain,
        grad_first_shift,
        grad_down_bias,
        grad_second_gain,
        grad_second_shift,
    )
    return (grad_in, split_terms, shared_terms)


def per_device(
    inputs,
    segment_ids,
    query_weight,
    query_bias,
    key_weight,
    value_weight,
    value_bias,
    out_weight,
    out_bias,
    first_gain,
    first_shift,
    up_weight,
    up_bias,
    down_weight,
    down_bias,
    second_gain,
    second_shift,
    cotangent,
):
    stacked = jnp.concatenate((query_weight, key_weight, value_weight), 1)
    stacked_bias = jnp.concatenate((query_bias, jnp.zeros_like(query_bias), value_bias))
    weights = (
        stacked,
        stacked_bias,
        out_weight,
        out_bias,
        first_gain,
        first_shift,
        up_weight,
        up_bias,
        down_weight,
        down_bias,
        second_gain,
        second_shift,
    )
    layer_one_in = inputs.astype(jnp.float32)
    layer_two_in, saved_one = forward_layer(layer_one_in, segment_ids, weights)
    final_out, saved_two = forward_layer(layer_two_in, segment_ids, weights)
    layer_inputs = (layer_one_in, layer_two_in)
    grad_flow = cotangent.astype(jnp.float32)
    split_total = None
    shared_total = None
    for position in (1, 0):
        kept = forward_layer(layer_inputs[position], segment_ids, weights)[1]
        grad_flow, split_terms, shared_terms = backward_layer(kept, grad_flow, segment_ids, weights)
        if position == 1:
            split_total = split_terms
            shared_total = shared_terms
        else:
            split_total = jax.tree.map(jnp.add, split_total, split_terms)
            shared_total = jax.tree.map(jnp.add, shared_total, shared_terms)
    split_total = lax.psum(
        (
            split_total[0],
            split_total[1],
            split_total[2],
            split_total[3],
            split_total[4],
            split_total[5],
            split_total[6],
        ),
        "dp",
    )
    shared_total = lax.psum(
        (
            shared_total[0],
            shared_total[1],
            shared_total[2],
            shared_total[3],
            shared_total[4],
            shared_total[5],
        ),
        ("dp", "tensor"),
    )
    (
        grad_stacked,
        grad_query_bias,
        grad_value_bias,
        grad_out_weight,
        grad_up,
        grad_up_bias,
        grad_down,
    ) = split_total
    (
        grad_out_bias,
        grad_first_gain,
        grad_first_shift,
        grad_down_bias,
        grad_second_gain,
        grad_second_shift,
    ) = shared_total
    head_width = stacked.shape[1] // 3
    return (
        final_out.astype(jnp.bfloat16),
        grad_flow,
        grad_stacked[:, :head_width],
        grad_query_bias,
        grad_stacked[:, head_width : 2 * head_width],
        grad_stacked[:, 2 * head_width :],
        grad_value_bias,
        grad_out_weight,
        grad_out_bias,
        grad_first_gain,
        grad_first_shift,
        grad_up,
        grad_up_bias,
        grad_down,
        grad_down_bias,
        grad_second_gain,
        grad_second_shift,
    )


def solution(mesh):
    placed = (
        P(("dp", "tensor"), None),
        P("dp"),
        P(None, "tensor"),
        P("tensor"),
        P(None, "tensor"),
        P(None, "tensor"),
        P("tensor"),
        P("tensor", None),
        P(),
        P(),
        P(),
        P(None, "tensor"),
        P("tensor"),
        P("tensor", None),
        P(),
        P(),
        P(),
        P(("dp", "tensor"), None),
    )
    return jax.shard_map(
        per_device,
        mesh=mesh,
        in_specs=placed,
        out_specs=(
            P(("dp", "tensor"), None),
            P(("dp", "tensor"), None),
            P(None, "tensor"),
            P("tensor"),
            P(None, "tensor"),
            P(None, "tensor"),
            P("tensor"),
            P("tensor", None),
            P(),
            P(),
            P(),
            P(None, "tensor"),
            P("tensor"),
            P("tensor", None),
            P(),
            P(),
            P(),
        ),
        check_vma=False,
    )
```

profile of v0, /device:TPU:1, one launch (start us, length us, event | category | flops | bytes accessed | tf_op | source)
XLA Modules:
  0.0 1302.0 jit_solution(14768318015421609500)
XLA Ops:
  12.2 45.5 %all-gather.11.cloned.1.call-done = bf16[2048,512]{1,0:T(8,128)(2,1)} async-done(((bf16[512,512]{1,0:T(8,128)(2,1)}), bf16[2048,512]{1,0:T(8,128)(2,1)}) %all-gather.11.cloned.1.call-update) | async-done | bytes 2097168 | tf_op jit(solution)/shard_map/all_gather | solution.py:34
  130.8 45.6 %reduce-scatter.29.cloned.1.call-done = bf16[512,512]{1,0:T(8,128)(2,1)} async-done(((bf16[2048,512]{1,0:T(8,128)(2,1)}), bf16[512,512]{1,0:T(8,128)(2,1)}) %reduce-scatter.29.cloned.1.call-update) | async-done | bytes 524304 | tf_op jit(solution)/shard_map/reduce_scatter | solution.py:42
  183.6 45.0 %all-gather.13.cloned.1.call-done = bf16[2048,512]{1,0:T(8,128)(2,1)} async-done(((bf16[512,512]{1,0:T(8,128)(2,1)}), bf16[2048,512]{1,0:T(8,128)(2,1)}) %all-gather.13.cloned.1.call-update) | async-done | bytes 2097168 | tf_op jit(solution)/shard_map/all_gather | solution.py:34
  234.9 40.3 %all-gather.25.cloned.1.call-done = bf16[2048,512]{1,0:T(8,128)(2,1)} async-done(((bf16[512,512]{1,0:T(8,128)(2,1)}), bf16[2048,512]{1,0:T(8,128)(2,1)}) %all-gather.25.cloned.1.call-update) | async-done | bytes 2097168 | tf_op jit(solution)/shard_map/all_gather | solution.py:34
  283.2 36.5 %reduce-scatter.15.cloned.1.call-done = bf16[512,512]{1,0:T(8,128)(2,1)} async-done(((bf16[2048,512]{1,0:T(8,128)(2,1)}), bf16[512,512]{1,0:T(8,128)(2,1)}) %reduce-scatter.15.cloned.1.call-update) | async-done | bytes 524304 | tf_op jit(solution)/shard_map/reduce_scatter | solution.py:42
  319.8 45.6 %reduce-scatter.31.cloned.1.call-done = bf16[512,512]{1,0:T(8,128)(2,1)} async-done(((bf16[2048,512]{1,0:T(8,128)(2,1)}), bf16[512,512]{1,0:T(8,128)(2,1)}) %reduce-scatter.31.cloned.1.call-update) | async-done | bytes 524304 | tf_op jit(solution)/shard_map/reduce_scatter | solution.py:42
  371.2 45.5 %all-gather.15.cloned.1.call-done = bf16[2048,512]{1,0:T(8,128)(2,1)} async-done(((bf16[512,512]{1,0:T(8,128)(2,1)}), bf16[2048,512]{1,0:T(8,128)(2,1)}) %all-gather.15.cloned.1.call-update) | async-done | bytes 2097168 | tf_op jit(solution)/shard_map/all_gather | solution.py:34
  470.5 24.1 %reduce-scatter.17.cloned.1.call-done = bf16[512,512]{1,0:T(8,128)(2,1)} async-done(((bf16[2048,512]{1,0:T(8,128)(2,1)}), bf16[512,512]{1,0:T(8,128)(2,1)}) %reduce-scatter.17.cloned.1.call-update) | async-done | bytes 524304 | tf_op jit(solution)/shard_map/reduce_scatter | solution.py:42
  494.6 45.8 %reduce-scatter.21.cloned.1.call-done = bf16[512,512]{1,0:T(8,128)(2,1)} async-done(((bf16[2048,512]{1,0:T(8,128)(2,1)}), bf16[512,512]{1,0:T(8,128)(2,1)}) %reduce-scatter.21.cloned.1.call-update) | async-done | bytes 524304 | tf_op jit(solution)/shard_map/reduce_scatter | solution.py:42
  545.5 45.0 %all-gather.17.cloned.1.call-done = bf16[2048,512]{1,0:T(8,128)(2,1)} async-done(((bf16[512,512]{1,0:T(8,128)(2,1)}), bf16[2048,512]{1,0:T(8,128)(2,1)}) %all-gather.17.cloned.1.call-update) | async-done | bytes 2097168 | tf_op jit(solution)/shard_map/all_gather | solution.py:34
  596.7 40.5 %all-gather.19.cloned.1.call-done = bf16[2048,512]{1,0:T(8,128)(2,1)} async-done(((bf16[512,512]{1,0:T(8,128)(2,1)}), bf16[2048,512]{1,0:T(8,128)(2,1)}) %all-gather.19.cloned.1.call-update) | async-done | bytes 2097168 | tf_op jit(solution)/shard_map/all_gather | solution.py:34
  646.9 35.0 %reduce-scatter.19.cloned.1.call-done = bf16[512,512]{1,0:T(8,128)(2,1)} async-done(((bf16[2048,512]{1,0:T(8,128)(2,1)}), bf16[512,512]{1,0:T(8,128)(2,1)}) %reduce-scatter.19.cloned.1.call-update) | async-done | bytes 524304 | tf_op jit(solution)/shard_map/reduce_scatter | solution.py:42
  681.9 45.5 %reduce-scatter.23.cloned.1.call-done = bf16[512,512]{1,0:T(8,128)(2,1)} async-done(((bf16[2048,512]{1,0:T(8,128)(2,1)}), bf16[512,512]{1,0:T(8,128)(2,1)}) %reduce-scatter.23.cloned.1.call-update) | async-done | bytes 524304 | tf_op jit(solution)/shard_map/reduce_scatter | solution.py:42
  734.9 45.6 %all-gather.21.cloned.1.call-done = bf16[2048,512]{1,0:T(8,128)(2,1)} async-done(((bf16[512,512]{1,0:T(8,128)(2,1)}), bf16[2048,512]{1,0:T(8,128)(2,1)}) %all-gather.21.cloned.1.call-update) | async-done | bytes 2097168 | tf_op jit(solution)/shard_map/all_gather | solution.py:51
  792.0 42.5 %reduce-scatter.25.cloned.1.call-done = bf16[512,512]{1,0:T(8,128)(2,1)} async-done(((bf16[2048,512]{1,0:T(8,128)(2,1)}), bf16[512,512]{1,0:T(8,128)(2,1)}) %reduce-scatter.25.cloned.1.call-update) | async-done | bytes 524304 | tf_op jit(solution)/shard_map/reduce_scatter | solution.py:59
  842.0 45.1 %all-gather.23.cloned.1.call-done = bf16[2048,512]{1,0:T(8,128)(2,1)} async-done(((bf16[512,512]{1,0:T(8,128)(2,1)}), bf16[2048,512]{1,0:T(8,128)(2,1)}) %all-gather.23.cloned.1.call-update) | async-done | bytes 2097168 | tf_op jit(solution)/shard_map/all_gather | solution.py:51
  895.0 26.8 %while.75 = (s32[]{:T(128)}, bf16[2,1024,2,64]{1,3,2,0:T(8,128)(2,1)}, bf16[2,1024,2,64]{1,3,2,0:T(8,128)(2,1)}, bf16[2,1024,2,64]{1,3,2,0:T(8,128)(2,1)S(1)}, b...) while((s32[]{:T(128)}, ...), condition=%wide.region_37.38_spmd, body=%wide.region_35.37_spmd.sunk | while | flops 1375336448 | bytes 78193896 | solution.py:216
  931.0 40.7 %reduce-scatter.27.cloned.1.call-done = bf16[512,512]{1,0:T(8,128)(2,1)} async-done(((bf16[2048,512]{1,0:T(8,128)(2,1)}), bf16[512,512]{1,0:T(8,128)(2,1)}) %reduce-scatter.27.cloned.1.call-update) | async-done | bytes 524304 | tf_op jit(solution)/shard_map/reduce_scatter | solution.py:59
  978.8 45.5 %all-gather.27.cloned.1.call-done = bf16[2048,512]{1,0:T(8,128)(2,1)} async-done(((bf16[512,512]{1,0:T(8,128)(2,1)}), bf16[2048,512]{1,0:T(8,128)(2,1)}) %all-gather.27.cloned.1.call-update) | async-done | bytes 2097168 | tf_op jit(solution)/shard_map/all_gather | solution.py:51
  1034.9 42.5 %reduce-scatter.33.cloned.1.call-done = bf16[512,512]{1,0:T(8,128)(2,1)} async-done(((bf16[2048,512]{1,0:T(8,128)(2,1)}), bf16[512,512]{1,0:T(8,128)(2,1)}) %reduce-scatter.33.cloned.1.call-update) | async-done | bytes 524304 | tf_op jit(solution)/shard_map/reduce_scatter | solution.py:59
  1099.2 30.4 %all-gather.29.cloned.1.call-done = bf16[2048,512]{1,0:T(8,128)(2,1)} async-done(((bf16[512,512]{1,0:T(8,128)(2,1)}), bf16[2048,512]{1,0:T(8,128)(2,1)}) %all-gather.29.cloned.1.call-update) | async-done | bytes 2097168 | tf_op jit(solution)/shard_map/all_gather | solution.py:51
  1137.7 28.3 %while.77 = (s32[]{:T(128)}, bf16[2,1024,2,64]{1,3,2,0:T(8,128)(2,1)}, bf16[2,1024,2,64]{1,3,2,0:T(8,128)(2,1)}, bf16[2,1024,2,64]{1,3,2,0:T(8,128)(2,1)S(1)}, b...) while((s32[]{:T(128)}, ...), condition=%wide.region_56.57_spmd, body=%wide.region_54.56_spmd.sunk | while | flops 1375336448 | bytes 78193896 | solution.py:216
  1179.0 39.7 %all-reduce = (f32[512]{0:T(512)}, f32[512]{0:T(512)}, f32[512]{0:T(512)}, f32[512]{0:T(512)}, f32[512]{0:T(512)}, /*index=5*/f32[512]{0:T(512)}) all-reduce(f32[512]{0:T(512)S(1)} %add.487, f32[512]{0:T(512)S(1)} %add.488, f32[512]{0:T(512)S(1)} %add.489, f32[512]{0:T(512)S(1)} %add.493, ...), channel_id=1, replica_groups=mesh['dp'=8,'tensor'=4] {'dp','tensor'}, use_global_device_ids=true, to_apply=%region_68.69 | all-reduce | flops 3072 | bytes 24576 | tf_op jit(solution)/shard_map/psum | solution.py:323
  1244.8 44.1 %reduce-scatter.35.cloned.1.call-done = bf16[512,512]{1,0:T(8,128)(2,1)} async-done(((bf16[2048,512]{1,0:T(8,128)(2,1)}), bf16[512,512]{1,0:T(8,128)(2,1)}) %reduce-scatter.35.cloned.1.call-update) | async-done | bytes 524304 | tf_op jit(solution)/shard_map/reduce_scatter | solution.py:59
  (524 shorter events, 443.3 us)
Async XLA Ops:
  7.2 221.3 %copy-start = (bf16[512,512]{1,0:T(8,128)(2,1)S(1)}, bf16[512,512]{1,0:T(8,128)(2,1)}, u32[]{:S(2)}) copy-start(bf16[512,512]{1,0:T(8,128)(2,1)} %param.41) | copy-start | bytes 1572868
  7.2 50.5 %all-gather.11.cloned.1.call-start = ((), (), s32[]{:S(2)}) async-start(), calls=%async_computation.12 | async-start | bytes 2621440 | tf_op jit(solution)/shard_map/all_gather | solution.py:34
  7.9 122.9 %reduce-scatter.13.cloned.1.call-start = ((), (), s32[]{:S(2)}) async-start(), calls=%async_computation.13 | async-start | bytes 2621440 | tf_op jit(solution)/shard_map/reduce_scatter | solution.py:42
  88.2 88.2 %reduce-scatter.29.cloned.1.call-start = ((), (), s32[]{:S(2)}) async-start(), calls=%async_computation.27 | async-start | bytes 2621440 | tf_op jit(solution)/shard_map/reduce_scatter | solution.py:42
  108.0 120.5 %all-gather.13.cloned.1.call-start = ((), (), s32[]{:S(2)}) async-start(), calls=%async_computation.14 | async-start | bytes 2621440 | tf_op jit(solution)/shard_map/all_gather | solution.py:34
  182.9 92.3 %all-gather.25.cloned.1.call-start = ((), (), s32[]{:S(2)}) async-start(), calls=%async_computation.28 | async-start | bytes 2621440 | tf_op jit(solution)/shard_map/all_gather | solution.py:34
  183.5 136.3 %reduce-scatter.15.cloned.1.call-start = ((), (), s32[]{:S(2)}) async-start(), calls=%async_computation.15 | async-start | bytes 2621440 | tf_op jit(solution)/shard_map/reduce_scatter | solution.py:42
  234.4 131.0 %reduce-scatter.31.cloned.1.call-start = ((), (), s32[]{:S(2)}) async-start(), calls=%async_computation.29 | async-start | bytes 2621440 | tf_op jit(solution)/shard_map/reduce_scatter | solution.py:42
  283.2 133.5 %all-gather.15.cloned.1.call-start = ((), (), s32[]{:S(2)}) async-start(), calls=%async_computation.16 | async-start | bytes 2621440 | tf_op jit(solution)/shard_map/all_gather | solution.py:34
  371.1 123.5 %reduce-scatter.17.cloned.1.call-start = ((), (), s32[]{:S(2)}) async-start(), calls=%async_computation.17 | async-start | bytes 2621440 | tf_op jit(solution)/shard_map/reduce_scatter | solution.py:42
  452.4 88.0 %reduce-scatter.21.cloned.1.call-start = ((), (), s32[]{:S(2)}) async-start(), calls=%async_computation.20 | async-start | bytes 2621440 | tf_op jit(solution)/shard_map/reduce_scatter | solution.py:42
  470.4 120.0 %all-gather.17.cloned.1.call-start = ((), (), s32[]{:S(2)}) async-start(), calls=%async_computation.18 | async-start | bytes 2621440 | tf_op jit(solution)/shard_map/all_gather | solution.py:34
  544.9 92.3 %all-gather.19.cloned.1.call-start = ((), (), s32[]{:S(2)}) async-start(), calls=%async_computation.21 | async-start | bytes 2621440 | tf_op jit(solution)/shard_map/all_gather | solution.py:34
  545.4 136.4 %reduce-scatter.19.cloned.1.call-start = ((), (), s32[]{:S(2)}) async-start(), calls=%async_computation.19 | async-start | bytes 2621440 | tf_op jit(solution)/shard_map/reduce_scatter | solution.py:42
  596.4 130.9 %reduce-scatter.23.cloned.1.call-start = ((), (), s32[]{:S(2)}) async-start(), calls=%async_computation.22 | async-start | bytes 2621440 | tf_op jit(solution)/shard_map/reduce_scatter | solution.py:42
  646.9 133.6 %all-gather.21.cloned.1.call-start = ((), (), s32[]{:S(2)}) async-start(), calls=%async_computation.23 | async-start | bytes 2621440 | tf_op jit(solution)/shard_map/all_gather | solution.py:51
  734.9 99.6 %reduce-scatter.25.cloned.1.call-start = ((), (), s32[]{:S(2)}) async-start(), calls=%async_computation.24 | async-start | bytes 2621440 | tf_op jit(solution)/shard_map/reduce_scatter | solution.py:59
  792.0 95.2 %all-gather.23.cloned.1.call-start = ((), (), s32[]{:S(2)}) async-start(), calls=%async_computation.25 | async-start | bytes 2621440 | tf_op jit(solution)/shard_map/all_gather | solution.py:51
  841.6 130.2 %reduce-scatter.27.cloned.1.call-start = ((), (), s32[]{:S(2)}) async-start(), calls=%async_computation.26 | async-start | bytes 2621440 | tf_op jit(solution)/shard_map/reduce_scatter | solution.py:59
  929.2 95.1 %all-gather.27.cloned.1.call-start = ((), (), s32[]{:S(2)}) async-start(), calls=%async_computation.30 | async-start | bytes 2621440 | tf_op jit(solution)/shard_map/all_gather | solution.py:51
  978.7 98.7 %reduce-scatter.33.cloned.1.call-start = ((), (), s32[]{:S(2)}) async-start(), calls=%async_computation.31 | async-start | bytes 2621440 | tf_op jit(solution)/shard_map/reduce_scatter | solution.py:59
  1034.9 94.7 %all-gather.29.cloned.1.call-start = ((), (), s32[]{:S(2)}) async-start(), calls=%async_computation.32 | async-start | bytes 2621440 | tf_op jit(solution)/shard_map/all_gather | solution.py:51
  1084.0 158.7 %all-reduce.5.cloned.1.call-start = ((), (), s32[]{:S(2)}) async-start(), calls=%async_computation.34 | async-start | bytes 6291456 | tf_op jit(solution)/shard_map/psum | solution.py:311
  1172.9 115.9 %reduce-scatter.35.cloned.1.call-start = ((), (), s32[]{:S(2)}) async-start(), calls=%async_computation.33 | async-start | bytes 2621440 | tf_op jit(solution)/shard_map/reduce_scatter | solution.py:59
  (117 other events, 3735.8 us)
Sparse Core Ops, SparseCore 0:
  9.6 48.0 all-gather.10
  88.3 42.4 reduce-scatter.12
  133.2 43.1 reduce-scatter.28
  183.0 45.4 all-gather.12
  230.5 44.6 all-gather.24
  277.3 42.4 reduce-scatter.14
  322.2 43.1 reduce-scatter.30
  371.2 45.4 all-gather.14
  452.5 41.9 reduce-scatter.16
  496.8 43.5 reduce-scatter.20
  545.0 45.4 all-gather.16
  592.4 44.6 all-gather.18
  639.4 42.4 reduce-scatter.18
  684.1 43.1 reduce-scatter.22
  735.0 45.4 all-gather.20
  792.1 42.3 reduce-scatter.24
  841.7 45.4 all-gather.22
  929.3 42.4 reduce-scatter.26
  978.9 45.3 all-gather.26
  1035.0 42.4 reduce-scatter.32
  1084.1 45.4 all-gather.28
  1172.9 69.7 all-reduce.4
  1245.0 43.8 reduce-scatter.34
where the time goes:
time: 1310 us; the launch traced here: 1300 us
  waiting for transfers between devices  912 us (70%)
  matrix products  182 us (14%)
  other arithmetic  74 us (6%)
  local copies, waits for them, and re-layouts  62.3 us (5%)
  blocking collectives  52.1 us (4%)
  between operations  15.9 us (1%)
    reduce_scatter x8, waiting for transfers between devices, scatter_rows(): lax.psum_scatter(partial_value(jnp.int32(0), row_count * lax.axis_size('t...  301 us
    all_gather x6, waiting for transfers between devices, gather_rows(): return lax.all_gather(shard, 'tensor', axis=0, tiled=True)  262 us
    reduce_scatter x4, waiting for transfers between devices, scatter_grads(): lax.psum_scatter(partial_value(jnp.int32(0), row_count * lax.axis_size('t...  170 us
    all_gather x4, waiting for transfers between devices, gather_grads(): return lax.all_gather(shard, 'tensor', axis=0, tiled=True)  167 us
    psum x1, blocking collectives, per_device(): lax.psum((shared_total[0], shared_total[1], shared_total[2], shared_total...  39.7 us
    dot_general x8, matrix products, attend(): jnp.einsum('hqk,khd->qhd', attn_probs, values, preferred_element_type=jnp...  31 us
    dot_general x8, matrix products, contract_last(): lax.dot_general(operand, weight, (((1,), (1,)), ((), ())), preferred_elem...  30.6 us
  transfers between devices with their start and end apart: 23, of which 23 were waited for; matrix products, arithmetic and copies ran while one was open for 7% of the time, Pallas kernels for 0%

commit v1 on v0

v1 whole, which is shorter than its diff:
```python
import math

import jax
import jax.numpy as jnp
from jax import lax
from jax.sharding import PartitionSpec as P

HEAD_DIM = 64
LEN = 1024
EPS = 1e-05
LOW = jnp.bfloat16
F32 = jnp.float32


def swap_dp(value, bit):
    count = lax.axis_size("dp")
    return lax.ppermute(value, "dp", [(i, i ^ bit) for i in range(count)])


def swap_tensor(value, step):
    count = lax.axis_size("tensor")
    return lax.ppermute(value, "tensor", [(i, i ^ step) for i in range(count)])


def regroup(block):
    dp, tensor = lax.axis_size("dp"), lax.axis_size("tensor")
    pairs = [
        ((2 * k + c) * tensor + 2 * a + b, (2 * k + b) * tensor + 2 * a + c)
        for k in range(dp // 2)
        for c in range(2)
        for a in range(tensor // 2)
        for b in range(2)
        if b != c
    ]
    moved = lax.ppermute(block, ("dp", "tensor"), pairs)
    stays = (lax.axis_index("dp") % 2) == (lax.axis_index("tensor") % 2)
    return jnp.where(stays, block, moved)


def gather_units(piece):
    kinds, rows, width = piece.shape
    near = jnp.stack((piece, swap_tensor(piece, 1)), 1)
    far = jnp.stack((swap_tensor(piece, 2), swap_tensor(piece, 3)), 1)
    near = near.reshape(kinds, 2, 1, 1, 1, rows, width)
    far = far.reshape(kinds, 2, 1, 1, 1, rows, width)
    near = jnp.concatenate((near, swap_dp(near, 2)), 3)
    far = jnp.concatenate((far, swap_dp(far, 4)), 2)
    near = jnp.concatenate((near, swap_dp(near, 4)), 2)
    far = jnp.concatenate((far, swap_dp(far, 2)), 3)
    near = jnp.concatenate((near, swap_dp(near, 1)), 4)
    far = jnp.concatenate((far, swap_dp(far, 1)), 4)
    return jnp.concatenate((near, far), 1).reshape(kinds, 32 * rows, width)


def add_half(value, axis, bit):
    first, second = jnp.split(value, 2, axis)
    return (first.astype(F32) + swap_dp(second, bit).astype(F32)).astype(LOW)


def reduce_units(total):
    kinds, rows, width = total.shape
    rows //= 32
    total = total.reshape(kinds, 4, 2, 2, 2, rows, width)
    total = add_half(total, 4, 1)
    near, far = total[:, :2], total[:, 2:]
    near = add_half(near, 3, 2)
    far = add_half(far, 2, 4)
    near = add_half(near, 2, 4)
    far = add_half(far, 3, 2)
    near = near.reshape(kinds, 2, rows, width)
    far = far.reshape(kinds, 2, rows, width)
    own = (
        near[:, 0].astype(F32)
        + swap_tensor(near[:, 1], 1).astype(F32)
        + swap_tensor(far[:, 0], 2).astype(F32)
        + swap_tensor(far[:, 1], 3).astype(F32)
    )
    bit = 8
    while bit < lax.axis_size("dp"):
        own = own + swap_dp(own.astype(LOW), bit).astype(F32)
        bit *= 2
    own = own.astype(LOW).reshape(kinds, 1, 1, 1, rows, width)
    left, right = own[..., : width // 2], own[..., width // 2 :]
    left = both(left, 2, 2)
    right = both(right, 1, 4)
    left = both(left, 1, 4)
    right = both(right, 2, 2)
    left = both(left, 3, 1)
    right = both(right, 3, 1)
    return jnp.concatenate((left, right), -1).reshape(kinds, 8 * rows, width).astype(F32)


def both(value, axis, bit):
    other = swap_dp(value, bit)
    upper = (lax.axis_index("dp") & bit) != 0
    return jnp.where(
        upper, jnp.concatenate((other, value), axis), jnp.concatenate((value, other), axis)
    )


def relative(value, axis, bit_of):
    return jnp.where(bit_of, jnp.flip(value, axis), value)


def unit_flips(value):
    dp, tensor = lax.axis_index("dp"), lax.axis_index("tensor")
    rows = value.shape[-1]
    value = relative(value, 1, (dp & 4) != 0)
    value = relative(value, 2, (dp & 2) != 0)
    value = relative(value, 3, (dp & 1) != 0)
    value = value.reshape(2, 2, 8, rows)
    value = relative(value, 0, (tensor & 2) != 0)
    value = relative(value, 1, (tensor & 1) != 0)
    return value.reshape(4, 2, 2, 2, rows)


def gather_bias(shard):
    rows = shard.shape[0] // 8
    dp = lax.axis_index("dp")
    blocks = shard.reshape(2, 2, 2, rows)
    blocks = relative(blocks, 0, (dp & 4) != 0)
    blocks = relative(blocks, 1, (dp & 2) != 0)
    blocks = relative(blocks, 2, (dp & 1) != 0)
    flat = blocks.reshape(8 * rows)
    return flat


def dot_nt(a, b):
    return lax.dot_general(a, b, (((1,), (1,)), ((), ())), preferred_element_type=F32)


def dot_tn(a, b):
    return lax.dot_general(a, b, (((0,), (0,)), ((), ())), preferred_element_type=F32)


def dot_nn(a, b):
    return jnp.dot(a, b, preferred_element_type=F32)


def norm(value):
    center = value - jnp.mean(value, -1, keepdims=True)
    scale = lax.rsqrt(jnp.mean(center * center, -1, keepdims=True) + EPS)
    return center * scale, scale


def norm_back(grad, gain, unit, scale):
    scaled = grad * gain
    mean_a = jnp.mean(scaled, -1, keepdims=True)
    mean_b = jnp.mean(scaled * unit, -1, keepdims=True)
    return (scaled - mean_a - unit * mean_b) * scale


def split_heads(value):
    return value.reshape(value.shape[0], -1, HEAD_DIM)


def attention_forward(layer_in, low_all, labels_own, labels_all, w):
    rows = layer_in.shape[0]
    low_own = low_all[:rows]
    queries = (dot_nt(low_own, w["q"]) + w["qb"]).astype(LOW)
    keys = dot_nt(low_all, w["k"]).astype(LOW)
    values = (dot_nt(low_all, w["v"]) + w["vb"]).astype(LOW)
    scores = jnp.einsum(
        "qhd,khd->hqk", split_heads(queries), split_heads(keys), preferred_element_type=F32
    ) * (1.0 / math.sqrt(HEAD_DIM))
    scores = jnp.where((labels_own[:, None] == labels_all[None, :])[None], scores, -1e9)
    exponent = jnp.exp(scores - jnp.max(scores, -1, keepdims=True))
    probs = (exponent / jnp.sum(exponent, -1, keepdims=True)).astype(LOW)
    inv_total = 1.0 / jnp.sum(probs.astype(F32), -1, keepdims=True)
    attended = (
        jnp.einsum("hqk,khd->qhd", probs, split_heads(values), preferred_element_type=F32)
        .astype(LOW)
        .reshape(rows, -1)
    )
    pre_one = layer_in + dot_nn(attended, w["o"]) + w["ob"]
    unit_one, scale_one = norm(pre_one)
    middle = unit_one * w["g1"] + w["s1"]
    return middle, (queries, keys, values, probs, inv_total, attended, unit_one, scale_one)


def ffn_forward(middle, w):
    hidden = dot_nt(middle.astype(LOW), w["up"]) + w["upb"]
    active, pull = jax.vjp(jax.nn.gelu, hidden)
    slope = pull(jnp.ones_like(hidden))[0].astype(LOW)
    active = active.astype(LOW)
    pre_two = middle + dot_nn(active, w["down"]) + w["db"]
    unit_two, scale_two = norm(pre_two)
    return unit_two * w["g2"] + w["s2"], (middle.astype(LOW), active, slope, unit_two, scale_two)


def ffn_backward(grad_out, kept, w):
    middle_low, active, slope, unit_two, scale_two = kept
    grad_gain = jnp.sum(grad_out * unit_two, 0)
    grad_shift = jnp.sum(grad_out, 0)
    grad_pre = norm_back(grad_out, w["g2"], unit_two, scale_two)
    grad_branch = grad_pre.astype(LOW)
    grad_db = jnp.sum(grad_branch.astype(F32), 0)
    grad_hidden = (dot_nt(grad_branch, w["down"]) * slope.astype(F32)).astype(LOW)
    grad_upb = jnp.sum(grad_hidden.astype(F32), 0)
    grad_middle = grad_pre + dot_nn(grad_hidden, w["up"])
    return grad_middle, (grad_branch, grad_hidden), (grad_db, grad_gain, grad_shift, grad_upb)


def attention_backward(grad_middle, kept, w):
    queries, keys, values, probs, inv_total, attended, unit_one, scale_one = kept
    rows = grad_middle.shape[0]
    grad_gain = jnp.sum(grad_middle * unit_one, 0)
    grad_shift = jnp.sum(grad_middle, 0)
    grad_pre = norm_back(grad_middle, w["g1"], unit_one, scale_one)
    grad_branch = grad_pre.astype(LOW)
    grad_ob = jnp.sum(grad_branch.astype(F32), 0)
    grad_att = dot_nt(grad_branch, w["o"]).astype(LOW)
    grad_heads = split_heads(grad_att)
    grad_probs = jnp.einsum(
        "qhd,khd->hqk", grad_heads, split_heads(values), preferred_element_type=F32
    )
    inv = 1.0 / math.sqrt(HEAD_DIM)
    delta = jnp.sum(probs.astype(F32) * grad_probs, -1, keepdims=True)
    grad_scores = (probs.astype(F32) * (grad_probs - delta * inv_total)).astype(LOW)
    grad_q = (
        jnp.einsum("hqk,khd->qhd", grad_scores, split_heads(keys), preferred_element_type=F32) * inv
    ).astype(LOW).reshape(rows, -1)
    grad_k = (
        jnp.einsum("hqk,qhd->khd", grad_scores, split_heads(queries), preferred_element_type=F32)
        * inv
    ).astype(LOW).reshape(2 * rows, -1)
    grad_v = jnp.einsum(
        "hqk,qhd->khd", probs, grad_heads, preferred_element_type=F32
    ).astype(LOW).reshape(2 * rows, -1)
    grad_qb = jnp.sum(grad_q.astype(F32), 0)
    grad_vb = jnp.sum(grad_v.astype(F32), 0)
    both_halves = dot_nn(grad_k, w["k"]) + dot_nn(grad_v, w["v"])
    grad_in = grad_pre + dot_nn(grad_q, w["q"]) + both_halves[:rows]
    sent = both_halves[rows:].astype(LOW)
    return (
        grad_in,
        sent,
        (grad_branch, grad_q, grad_k, grad_v),
        (grad_ob, grad_gain, grad_shift, grad_qb, grad_vb),
    )


def per_device(
    inputs, segment_ids, query_weight, query_bias, key_weight, value_weight, value_bias, out_weight, out_bias,
    first_gain, first_shift, up_weight, up_bias, down_weight, down_bias, second_gain, second_shift, cotangent,
):
    rows, width = inputs.shape
    dp, tensor = lax.axis_index("dp"), lax.axis_index("tensor")
    core = dp % 2
    slice_at = dp % 8
    head_rows = query_weight.shape[1] // 8
    unit_rows = up_weight.shape[1] // 8

    def columns(weight, count):
        return lax.dynamic_slice_in_dim(weight, slice_at * count, count, 1).T

    qkv = jnp.stack([columns(v, head_rows) for v in (query_weight, key_weight, value_weight)])
    first_in = regroup(inputs)
    grad_flow = regroup(cotangent).astype(F32)
    qkv = gather_units(qkv)
    out_all = gather_units(lax.dynamic_slice_in_dim(out_weight, slice_at * head_rows, head_rows, 0)[None])[0]
    up_all = gather_units(columns(up_weight, unit_rows)[None])[0]
    down_all = gather_units(
        lax.dynamic_slice_in_dim(down_weight, slice_at * unit_rows, unit_rows, 0)[None]
    )[0]
    flat = jnp.concatenate((gather_bias(query_bias), gather_bias(value_bias), gather_bias(up_bias)))
    flat = jnp.stack([flat] + [swap_tensor(flat, j) for j in (1, 2, 3)])
    heads = query_bias.shape[0]
    w = {
        "q": qkv[0], "k": qkv[1], "v": qkv[2], "o": out_all, "up": up_all, "down": down_all,
        "qb": flat[:, :heads].reshape(-1), "vb": flat[:, heads : 2 * heads].reshape(-1),
        "upb": flat[:, 2 * heads :].reshape(-1),
        "ob": out_bias, "g1": first_gain, "s1": first_shift, "db": down_bias, "g2": second_gain, "s2": second_shift,
    }

    seq = lax.dynamic_slice_in_dim(segment_ids, (tensor // 2) * LEN, LEN)
    seq = jnp.where(core == tensor % 2, seq, swap_dp(seq, 1))
    labels_own = lax.dynamic_slice_in_dim(seq, core * rows, rows)
    labels_all = jnp.concatenate((labels_own, lax.dynamic_slice_in_dim(seq, (1 - core) * rows, rows)))

    kept = []
    layer_in = first_in.astype(F32)
    for _ in range(2):
        low = layer_in.astype(LOW)
        low_all = jnp.concatenate((low, swap_dp(low, 1)))
        middle, kept_attention = attention_forward(layer_in, low_all, labels_own, labels_all, w)
        layer_in, kept_ffn = ffn_forward(middle, w)
        kept.append((low_all, kept_attention, kept_ffn))
    result = regroup(layer_in.astype(LOW))

    pairs_list, sums = [], []
    for position in (1, 0):
        low_all, kept_attention, kept_ffn = kept[position]
        grad_middle, ffn_pairs, ffn_sums = ffn_backward(grad_flow, kept_ffn, w)
        grad_flow, sent, att_pairs, att_sums = attention_backward(grad_middle, kept_attention, w)
        grad_flow = grad_flow + swap_dp(sent, 1).astype(F32)
        pairs_list.append(
            (
                (kept_ffn[1], ffn_pairs[0]),
                (ffn_pairs[1], kept_ffn[0]),
                (kept_attention[5], att_pairs[0]),
                (att_pairs[1], low_all[:rows]),
                (att_pairs[2], low_all),
                (att_pairs[3], low_all),
            )
        )
        sums.append(att_sums + ffn_sums)
    grads = [
        dot_tn(jnp.concatenate((second[0], first[0])), jnp.concatenate((second[1], first[1]))).astype(LOW)
        for second, first in zip(*pairs_list)
    ]
    down_grad = reduce_units(grads[0][None])[0]
    up_grad = reduce_units(grads[1][None])[0].T
    out_grad, q_grad, k_grad, v_grad = reduce_units(jnp.stack(grads[2:]))
    ob, g1, s1, qb, vb, db, g2, s2, upb = (a + b for a, b in zip(*sums))

    def absolute(value):
        return unit_flips(value.reshape(4, 2, 2, 2, -1)).reshape(4, -1)

    small = jnp.concatenate(
        [ob, g1, s1, db, g2, s2]
        + [absolute(v).reshape(-1) for v in (qb, vb, upb)]
    ).reshape(-1, width)
    small = lax.psum(small, ("dp", "tensor")).reshape(-1)
    ob, g1, s1, db, g2, s2 = jnp.split(small[: 6 * width], 6)

    def own(start, count):
        return lax.dynamic_slice_in_dim(small[start : start + 4 * count], tensor * count, count)

    units = up_bias.shape[0]
    qb = own(6 * width, heads)
    vb = own(6 * width + 4 * heads, heads)
    upb = own(6 * width + 8 * heads, units)
    input_grad = regroup(grad_flow.astype(LOW)).astype(F32)
    return (
        result, input_grad, q_grad.T, qb, k_grad.T, v_grad.T, vb, out_grad, ob, g1, s1, up_grad, upb, down_grad, db, g2, s2,
    )


def solution(mesh):
    split = P(("dp", "tensor"), None)
    columns, rows, part = P(None, "tensor"), P("tensor", None), P("tensor")
    return jax.shard_map(
        per_device,
        mesh=mesh,
        in_specs=(
            split, P("dp"), columns, part, columns, columns, part, rows, P(), P(), P(), columns, part, rows, P(), P(),
            P(), split,
        ),
        out_specs=(
            split, split, columns, part, columns, columns, part, rows, P(), P(), P(), columns, part, rows, P(), P(), P(),
        ),
        check_vma=False,
    )
```

time: 1310 us -> 376 us (0.29)
  waiting for transfers between devices: 912 us -> 34.7 us
  starting transfers between devices: 2.56 us -> 106 us
  matrix products: 182 us -> 107 us
  local copies, waits for them, and re-layouts: 62.3 us -> 22.5 us
  other arithmetic: 74 us -> 58 us
  blocking collectives: 52.1 us -> 38.3 us
    reduce_scatter x12 -> x0, waiting for transfers between devices: 471 us -> none  [the longest x8 301 us: scatter_rows(): lax.psum_scatter(partial_value(jnp.int32(0), row_count * lax.axis_size('t...]
    all_gather x10 -> x0, waiting for transfers between devices: 428 us -> none  [the longest x6 262 us: gather_rows(): return lax.all_gather(shard, 'tensor', axis=0, tiled=True)]
    ppermute x0 -> x90, starting transfers between devices: none -> 106 us  [the longest x62 61.5 us: swap_dp(): return lax.ppermute(value, 'dp', [(i, i ^ bit) for i in range(count)])]
    dot_general x60 -> x40, matrix products: 161 us -> 85.8 us  [the longest x12 25.2 us: dot_nt(): lax.dot_general(a, b, (((1,), (1,)), ((), ())), preferred_element_type=F32)]
    reduce_sum x31 -> x9, other arithmetic: 45.9 us -> 6.19 us  [the longest x2 1.74 us: attention_backward(): grad_ob = jnp.sum(grad_branch.astype(F32), 0)]
    ppermute x0 -> x90, waiting for transfers between devices: none -> 34.7 us  [the longest x62 30.7 us: swap_dp(): return lax.ppermute(value, 'dp', [(i, i ^ bit) for i in range(count)])]
    convert_element_type x7 -> x19, other arithmetic: 15.9 us -> 42.7 us  [the longest x2 23.3 us: attention_backward(): (probs.astype(F32) * (grad_probs - delta * inv_total)).astype(LOW)]
    while x50 -> x0, local copies, waits for them, and re-layouts: 20.7 us -> none  [the longest x8 10.6 us: backward_layer(): lax.map(attend_back, (queries, key_heads, values, labels.reshape(seq_coun...]
  transfers between devices with their start and end apart: 23 -> 90, of which waited for: 23 -> 20; matrix products, arithmetic and copies ran while one was open for 7% -> 35% of each run, Pallas kernels for 0% -> 0%
where the time goes in v1:
time: 376 us; the launch traced here: 370 us
  matrix products  107 us (28%)
  starting transfers between devices  106 us (28%)
  other arithmetic  58 us (15%)
  blocking collectives  38.3 us (10%)
  waiting for transfers between devices  34.7 us (9%)
  local copies, waits for them, and re-layouts  22.5 us (6%)
    ppermute x62, starting transfers between devices, swap_dp(): return lax.ppermute(value, 'dp', [(i, i ^ bit) for i in range(count)])  61.5 us
    psum x1, blocking collectives, per_device(): small = lax.psum(small, ('dp', 'tensor')).reshape(-1)  38.3 us
    ppermute x62, waiting for transfers between devices, swap_dp(): return lax.ppermute(value, 'dp', [(i, i ^ bit) for i in range(count)])  30.7 us
    ppermute x24, starting transfers between devices, swap_tensor(): return lax.ppermute(value, 'tensor', [(i, i ^ step) for i in range(count)])  28.9 us
    dot_general x12, matrix products, dot_nt(): lax.dot_general(a, b, (((1,), (1,)), ((), ())), preferred_element_type=F32)  25.2 us
    convert_element_type x2, other arithmetic, attention_backward(): (probs.astype(F32) * (grad_probs - delta * inv_total)).astype(LOW)  23.3 us
    sub x2, matrix products, attention_forward(): exponent = jnp.exp(scores - jnp.max(scores, -1, keepdims=True))  21.1 us
    ppermute x4, starting transfers between devices, regroup(): moved = lax.ppermute(block, ('dp', 'tensor'), pairs)  15.9 us
  transfers between devices with their start and end apart: 90, of which 20 were waited for; matrix products, arithmetic and copies ran while one was open for 35% of the time, Pallas kernels for 0%

profile of v1, /device:TPU:1, one launch (start us, length us, event | category | flops | bytes accessed | tf_op | source)
XLA Modules:
  0.0 370.4 jit_solution(17218495146412474730)
XLA Ops:
  3.5 4.2 %collective-permute-start.13 = (f32[768]{0:T(1024)S(1)}, f32[768]{0:T(1024)S(1)}, u32[]{:S(2)}, u32[]{:S(2)}) collective-permute-start(f32[768]{0:T(1024)S(1)} %constant_dynamic-update-slice_fusion.2), channel_id=1, source_target_pairs={{0,3},{1,2},{2,1},{3,0},{4,7},{5,6},{6,5},{7,4},{8,11},{9,10},{10,... | collective-permute-start | bytes 9224 | tf_op jit(solution)/shard_map/ppermute | solution.py:22
  39.1 6.9 %collective-permute-start = (bf16[512,512]{1,0:T(8,128)(2,1)}, bf16[512,512]{1,0:T(8,128)(2,1)S(1)}, u32[]{:S(2)}, u32[]{:S(2)}) collective-permute-start(bf16[512,512]{1,0:T(8,128)(2,1)} %param.18), channel_id=1, source_target_pairs={{1,4},{3,6},{4,1},{6,3},{9,12},{11,14},{12,9},{14,11},{17,20},{19,... | collective-permute-start | bytes 1572872 | tf_op jit(solution)/shard_map/ppermute | solution.py:35
  55.0 5.0 %collective-permute-done.30 = bf16[1,2,1,1,1,64,512]{6,5,4,3,2,1,0:T(8,128)(2,1)S(1)} collective-permute-done((bf16[1,2,1,1,1,64,512]{6,5,4,3,2,1,0:T(8,128)(2,1)S(1)}, bf16[1,2,1,1,1,64,512]{6,5,4,3,2,1,0:T(8,128)(2,1)S(1)}, u32[]{:S(2)}, u32[]{:S(2)}) %collective-permute-start.30) | collective-permute-done | bytes 131104 | tf_op jit(solution)/shard_map/ppermute | solution.py:17
  68.9 4.0 %collective-permute-done.31 = bf16[1,2,2,1,1,64,512]{6,5,4,3,2,1,0:T(8,128)(2,1)S(1)} collective-permute-done((bf16[1,2,2,1,1,64,512]{6,5,4,3,2,1,0:T(8,128)(2,1)S(1)}, bf16[1,2,2,1,1,64,512]{6,5,4,3,2,1,0:T(8,128)(2,1)S(1)}, u32[]{:S(2)}, u32[]{:S(2)}) %collective-permute-start.31) | collective-permute-done | bytes 262176 | tf_op jit(solution)/shard_map/ppermute | solution.py:17
  87.1 10.5 %fusion.154 = (f32[8,512]{1,0:T(8,128)S(1)}, f32[8,512,1024]{2,1,0:T(8,128)}) fusion(pred[512,1024]{1,0:T(8,128)(4,1)} %broadcast_compare_fusion, bf16[512,8,64]{0,2,1:T(8,128)(2,1)S(1)} %bitcast.372, bf16[1024,8,64]{0,2,1:T(8,128)(2,1)} %bitcast.376), kind=kOutput, calls=%fused_computation.413 | convolution fusion | flops 553649152 | bytes 18890752 | tf_op jit(solution)/shard_map/sub | solution.py:167
  97.6 7.0 %divide_convert_fusion.1 = bf16[8,512,1024]{2,1,0:T(8,128)(2,1)S(1)} fusion(f32[8,512,1024]{2,1,0:T(8,128)} %get-tuple-element.138, f32[8,512]{1,0:T(8,128)S(1)} %get-tuple-element.137), kind=kLoop, calls=%fused_computation.15 | loop fusion | flops 8388608 | bytes 25182208 | tf_op jit(solution)/shard_map/convert_element_type | solution.py:168
  110.2 4.0 %multiply_convert_fusion.3 = (bf16[512,2048]{1,0:T(8,128)(2,1)S(1)}, f32[512,2048]{1,0:T(8,128)}) fusion(f32[2048]{0:T(1024)S(1)} %bitcast.422, bf16[512,512]{1,0:T(8,128)(2,1)S(1)} %fusion.91, bf16[2048,512]{1,0:T(8,128)(2,1)S(1)} %bitcast.364), kind=kOutput, calls=%fused_computation.57 | convolution fusion | flops 1084227584 | bytes 8921088 | tf_op jit(solution)/shard_map/dot_general | solution.py:129
  124.8 10.6 %fusion.156 = (f32[8,512]{1,0:T(8,128)S(1)}, f32[8,512,1024]{2,1,0:T(8,128)}) fusion(pred[512,1024]{1,0:T(8,128)(4,1)} %broadcast_compare_fusion, bf16[512,8,64]{0,2,1:T(8,128)(2,1)} %bitcast.374, bf16[1024,8,64]{0,2,1:T(8,128)(2,1)} %bitcast.378), kind=kOutput, calls=%fused_computation.415 | convolution fusion | flops 553649152 | bytes 18890752 | tf_op jit(solution)/shard_map/sub | solution.py:167
  135.4 7.0 %divide_convert_fusion = bf16[8,512,1024]{2,1,0:T(8,128)(2,1)S(1)} fusion(f32[8,512,1024]{2,1,0:T(8,128)} %get-tuple-element.144, f32[8,512]{1,0:T(8,128)S(1)} %get-tuple-element.143), kind=kLoop, calls=%fused_computation.12 | loop fusion | flops 8388608 | bytes 25182208 | tf_op jit(solution)/shard_map/convert_element_type | solution.py:168
  155.7 4.0 %convert_reduce_fusion.3 = (f32[2048]{0:T(1024)S(1)}, bf16[512,2048]{1,0:T(8,128)(2,1)S(1)}) fusion(f32[512,2048]{1,0:T(8,128)S(1)} %get-tuple-element.148, f32[2048]{0:T(1024)S(1)} %bitcast.424, bf16[512,512]{1,0:T(8,128)(2,1)S(1)} %get-tuple-element.75, bf16[2048,512]{1,0:T(8,128)(2,1)S(1)} %bitcast.362), kind=kOutput, calls=%fused_computation.53 | convolution fusion | flops 1098905600 | bytes 8929280 | tf_op jit(solution)/shard_map/dot_general | solution.py:129
  164.4 7.8 %convert_reduce_fusion.1 = (f32[8,512]{1,0:T(8,128)S(1)}, f32[8,512]{1,0:T(8,128)S(1)}, f32[8,512,1024]{2,1,0:T(8,128)}) fusion(bf16[8,512,1024]{2,1,0:T(8,128)(2,1)S(1)} %divide_convert_fusion, bf16[512,8,64]{0,2,1:T(8,128)(2,1)S(1)} %bitcast.339, bf16[1024,8,64]{0,2,1:T(8,128)(2,1)S(1)} %bitcast.355), kind=kOutput, calls=%fused_computation.6 | convolution fusion | flops 553639936 | bytes 26771456 | tf_op jit(solution)/shard_map/qhd,khd->hqk/dot_general | solution.py:214
  172.2 3.5 collective-permute-start.43
  175.8 11.7 %fusion.3 = bf16[8,512,1024]{2,1,0:T(8,128)(2,1)S(1)} fusion(f32[8,512,1024]{2,1,0:T(8,128)} %get-tuple-element.152, f32[8,512]{1,0:T(8,128)S(1)} %divide_multiply_fusion.1, f32[8,512,1024]{2,1,0:T(8,128)} %get-tuple-element.144, f32[8,512]{1,0:T(8,128)S(1)} %get-tuple-element.143), kind=kLoop, calls=%fused_computation.9 | loop fusion | flops 25165824 | bytes 41975808 | tf_op jit(solution)/shard_map/convert_element_type | solution.py:219
  196.2 3.7 %fusion.36 = bf16[2048,512]{1,0:T(8,128)(2,1)} fusion(bf16[512,2048]{1,0:T(8,128)(2,1)S(1)} %copy-done.55, bf16[512,2048]{1,0:T(8,128)(2,1)S(1)} %copy-done.57, bf16[512,512]{1,0:T(8,128)(2,1)S(1)} %get-tuple-element.72, bf16[512,512]{1,0:T(8,128)(2,1)S(1)} %get-tuple-element.75), kind=kOutput, calls=%fused_computation.58 | convolution fusion | flops 2159017984 | bytes 7340032 | tf_op jit(solution)/shard_map/dot_general | solution.py:133
  200.0 3.9 %convert_reduce_fusion.2 = (f32[2048]{0:T(1024)S(1)}, bf16[512,2048]{1,0:T(8,128)(2,1)S(1)}) fusion(f32[512,2048]{1,0:T(8,128)S(1)} %copy-done.58, f32[2048]{0:T(1024)S(1)} %bitcast.425, bf16[512,512]{1,0:T(8,128)(2,1)S(1)} %get-tuple-element.72, bf16[2048,512]{1,0:T(8,128)(2,1)S(1)} %bitcast.363), kind=kOutput, calls=%fused_computation.52 | convolution fusion | flops 1098905600 | bytes 8929280 | tf_op jit(solution)/shard_map/dot_general | solution.py:129
  203.9 3.8 %fusion.39 = bf16[2048,512]{1,0:T(8,128)(2,1)} fusion(bf16[512,2048]{1,0:T(8,128)(2,1)S(1)} %get-tuple-element.167, bf16[512,2048]{1,0:T(8,128)(2,1)S(1)} %copy-done.53, bf16[512,512]{1,0:T(8,128)(2,1)S(1)} %copy-done.41, bf16[512,512]{1,0:T(8,128)(2,1)S(1)} %fusion.93), kind=kOutput, calls=%fused_computation.59 | convolution fusion | flops 2159017984 | bytes 7340032 | tf_op jit(solution)/shard_map/dot_general | solution.py:133
  213.1 7.7 %convert_reduce_fusion = (f32[8,512]{1,0:T(8,128)S(1)}, f32[8,512]{1,0:T(8,128)S(1)}, f32[8,512,1024]{2,1,0:T(8,128)}) fusion(bf16[8,512,1024]{2,1,0:T(8,128)(2,1)S(1)} %bitcast.323, bf16[512,8,64]{0,2,1:T(8,128)(2,1)S(1)} %bitcast.337, bf16[1024,8,64]{0,2,1:T(8,128)(2,1)S(1)} %bitcast.353), kind=kOutput, calls=%fused_computation.3 | convolution fusion | flops 553639936 | bytes 26771456 | tf_op jit(solution)/shard_map/qhd,khd->hqk/dot_general | solution.py:214
  220.9 11.6 %fusion.5 = bf16[8,512,1024]{2,1,0:T(8,128)(2,1)S(1)} fusion(f32[8,512,1024]{2,1,0:T(8,128)} %get-tuple-element.155, f32[8,512]{1,0:T(8,128)S(1)} %divide_multiply_fusion, f32[8,512,1024]{2,1,0:T(8,128)} %get-tuple-element.138, f32[8,512]{1,0:T(8,128)S(1)} %get-tuple-element.137), kind=kLoop, calls=%fused_computation.11 | loop fusion | flops 25165824 | bytes 41975808 | tf_op jit(solution)/shard_map/convert_element_type | solution.py:219
  232.5 3.5 convert_reduce_fusion.7
  238.6 38.3 %psum.7 = f32[12,512]{1,0:T(8,128)S(1)} all-reduce(f32[12,512]{1,0:T(8,128)S(1)} %reshape.2031), channel_id=1, replica_groups=mesh['dp'=8,'tensor'=4] {'dp','tensor'}, use_global_device_ids=true, to_apply=%region_42.43 | all-reduce | flops 6144 | bytes 49152 | tf_op jit(solution)/shard_map/psum | solution.py:324
  296.2 3.2 collective-permute-start.47
  317.6 4.3 %collective-permute-done.52 = bf16[4,2,1,2,1,16,512]{6,5,4,3,2,1,0:T(8,128)(2,1)S(1)} collective-permute-done((bf16[4,2,1,2,1,16,512]{6,5,4,3,2,1,0:T(8,128)(2,1)S(1)}, bf16[4,2,1,2,1,16,512]{6,5,4,3,2,1,0:T(8,128)(2,1)S(1)}, u32[]{:S(2)}, u32[]{:S(2)}) %collective-permute-start.52) | collective-permute-done | bytes 262176 | tf_op jit(solution)/shard_map/ppermute | solution.py:17
  338.3 5.1 %collective-permute-start.84 = (bf16[1,1,1,1,64,256]{5,4,3,2,1,0:T(8,128)(2,1)S(1)}, bf16[1,1,1,1,64,256]{5,4,3,2,1,0:T(8,128)(2,1)S(1)}, u32[]{:S(2)}, u32[]{:S(2)}) collective-permute-start(bf16[1,1,1,1,64,256]{5,4,3,2,1,0:T(8,128)(2,1)S(1)} %get-tuple-element.114), channel_id=1, source_target_pairs={{0,8},{4,12},{8,0},{12,4},{16,24},{20,28},{24,16},{28,20},{1,9},{5... | collective-permute-start | bytes 98312 | tf_op jit(solution)/shard_map/ppermute | solution.py:17
  353.6 4.5 %collective-permute-start.89 = (bf16[1,2,2,1,64,256]{5,4,3,2,1,0:T(8,128)(2,1)S(1)}, bf16[1,2,2,1,64,256]{5,4,3,2,1,0:T(8,128)(2,1)S(1)}, u32[]{:S(2)}, u32[]{:S(2)}) collective-permute-start(bf16[1,2,2,1,64,256]{5,4,3,2,1,0:T(8,128)(2,1)S(1)} %maximum_select_fusion.10), channel_id=1, source_target_pairs={{0,4},{4,0},{8,12},{12,8},{16,20},{20,16},{24,28},{28,24},{1,5},{5... | collective-permute-start | bytes 393224 | tf_op jit(solution)/shard_map/ppermute | solution.py:17
  (558 shorter events, 190.9 us)
Async XLA Ops:
  3.5 13.7 %collective-permute-start.13 = (f32[768]{0:T(1024)S(1)}, f32[768]{0:T(1024)S(1)}, u32[]{:S(2)}, u32[]{:S(2)}) collective-permute-start(f32[768]{0:T(1024)S(1)} %constant_dynamic-update-slice_fusion.2), channel_id=1, source_target_pairs={{0,3},{1,2},{2,1},{3,0},{4,7},{5,6},{6,5},{7,4},{8,11},{9,10},{10,... | collective-permute-start | bytes 9224 | tf_op jit(solution)/shard_map/ppermute | solution.py:22
  7.7 11.9 %collective-permute-start.11 = (f32[768]{0:T(1024)S(1)}, f32[768]{0:T(1024)S(1)}, u32[]{:S(2)}, u32[]{:S(2)}) collective-permute-start(f32[768]{0:T(1024)S(1)} %constant_dynamic-update-slice_fusion.2), channel_id=1, source_target_pairs={{0,1},{1,0},{2,3},{3,2},{4,5},{5,4},{6,7},{7,6},{8,9},{9,8},{10,11... | collective-permute-start | bytes 9224 | tf_op jit(solution)/shard_map/ppermute | solution.py:22
  8.8 16.6 %collective-permute-start.20 = (bf16[1,16,512]{2,1,0:T(8,128)(2,1)S(1)}, bf16[1,16,512]{2,1,0:T(8,128)(2,1)S(1)}, u32[]{:S(2)}, u32[]{:S(2)}) collective-permute-start(bf16[1,16,512]{2,1,0:T(8,128)(2,1)S(1)} %get-tuple-element.108), channel_id=1, source_target_pairs={{0,3},{1,2},{2,1},{3,0},{4,7},{5,6},{6,5},{7,4},{8,11},{9,10},{10,... | collective-permute-start | bytes 49160 | tf_op jit(solution)/shard_map/ppermute | solution.py:22
  11.9 13.9 %collective-permute-start.19 = (bf16[1,16,512]{2,1,0:T(8,128)(2,1)S(1)}, bf16[1,16,512]{2,1,0:T(8,128)(2,1)S(1)}, u32[]{:S(2)}, u32[]{:S(2)}) collective-permute-start(bf16[1,16,512]{2,1,0:T(8,128)(2,1)S(1)} %get-tuple-element.108), channel_id=1, source_target_pairs={{0,2},{1,3},{2,0},{3,1},{4,6},{5,7},{6,4},{7,5},{8,10},{9,11},{10,... | collective-permute-start | bytes 49160 | tf_op jit(solution)/shard_map/ppermute | solution.py:22
  19.6 15.8 %collective-permute-start.6 = (bf16[3,16,512]{2,1,0:T(8,128)(2,1)S(1)}, bf16[3,16,512]{2,1,0:T(8,128)(2,1)S(1)}, u32[]{:S(2)}, u32[]{:S(2)}) collective-permute-start(bf16[3,16,512]{2,1,0:T(8,128)(2,1)S(1)} %get-tuple-element.124), channel_id=1, source_target_pairs={{0,2},{1,3},{2,0},{3,1},{4,6},{5,7},{6,4},{7,5},{8,10},{9,11},{10,... | collective-permute-start | bytes 147464 | tf_op jit(solution)/shard_map/ppermute | solution.py:22
  21.7 12.9 %collective-permute-start.2 = (bf16[3,16,512]{2,1,0:T(8,128)(2,1)S(1)}, bf16[3,16,512]{2,1,0:T(8,128)(2,1)S(1)}, u32[]{:S(2)}, u32[]{:S(2)}) collective-permute-start(bf16[3,16,512]{2,1,0:T(8,128)(2,1)S(1)} %get-tuple-element.124), channel_id=1, source_target_pairs={{0,1},{1,0},{2,3},{3,2},{4,5},{5,4},{6,7},{7,6},{8,9},{9,8},{10,11... | collective-permute-start | bytes 147464 | tf_op jit(solution)/shard_map/ppermute | solution.py:22
  25.4 12.9 %collective-permute-start.7 = (bf16[3,16,512]{2,1,0:T(8,128)(2,1)S(1)}, bf16[3,16,512]{2,1,0:T(8,128)(2,1)S(1)}, u32[]{:S(2)}, u32[]{:S(2)}) collective-permute-start(bf16[3,16,512]{2,1,0:T(8,128)(2,1)S(1)} %get-tuple-element.124), channel_id=1, source_target_pairs={{0,3},{1,2},{2,1},{3,0},{4,7},{5,6},{6,5},{7,4},{8,11},{9,10},{10,... | collective-permute-start | bytes 147464 | tf_op jit(solution)/shard_map/ppermute | solution.py:22
  25.8 12.5 %collective-permute-start.29 = (bf16[1,64,512]{2,1,0:T(8,128)(2,1)S(1)}, bf16[1,64,512]{2,1,0:T(8,128)(2,1)S(1)}, u32[]{:S(2)}, u32[]{:S(2)}) collective-permute-start(bf16[1,64,512]{2,1,0:T(8,128)(2,1)S(1)} %bitcast.392), channel_id=1, source_target_pairs={{0,3},{1,2},{2,1},{3,0},{4,7},{5,6},{6,5},{7,4},{8,11},{9,10},{10,... | collective-permute-start | bytes 196616 | tf_op jit(solution)/shard_map/ppermute | solution.py:22
  35.4 12.0 %collective-permute-start.38 = (bf16[1,64,512]{2,1,0:T(8,128)(2,1)S(1)}, bf16[1,64,512]{2,1,0:T(8,128)(2,1)S(1)}, u32[]{:S(2)}, u32[]{:S(2)}) collective-permute-start(bf16[1,64,512]{2,1,0:T(8,128)(2,1)S(1)} %get-tuple-element.100), channel_id=1, source_target_pairs={{0,3},{1,2},{2,1},{3,0},{4,7},{5,6},{6,5},{7,4},{8,11},{9,10},{10,... | collective-permute-start | bytes 196616 | tf_op jit(solution)/shard_map/ppermute | solution.py:22
  39.1 41.0 %collective-permute-start = (bf16[512,512]{1,0:T(8,128)(2,1)}, bf16[512,512]{1,0:T(8,128)(2,1)S(1)}, u32[]{:S(2)}, u32[]{:S(2)}) collective-permute-start(bf16[512,512]{1,0:T(8,128)(2,1)} %param.18), channel_id=1, source_target_pairs={{1,4},{3,6},{4,1},{6,3},{9,12},{11,14},{12,9},{14,11},{17,20},{19,... | collective-permute-start | bytes 1572872 | tf_op jit(solution)/shard_map/ppermute | solution.py:35
  62.1 13.2 %collective-permute-start.35 = (bf16[1,2,1,2,1,64,512]{6,5,1,4,3,2,0:T(8,128)(2,1)S(1)}, bf16[1,2,1,2,1,64,512]{6,5,1,4,3,2,0:T(8,128)(2,1)S(1)}, u32[]{:S(2)}, u32[]{:S(2)}) collective-permute-start(bf16[1,2,1,2,1,64,512]{6,5,1,4,3,2,0:T(8,128)(2,1)S(1)} %pad_maximum_fusion.24), channel_id=1, source_target_pairs={{0,16},{4,20},{8,24},{12,28},{16,0},{20,4},{24,8},{28,12},{1,17},{... | collective-permute-start | bytes 786440 | tf_op jit(solution)/shard_map/ppermute | solution.py:17
  117.1 35.5 %collective-permute-start.44 = (bf16[512,512]{1,0:T(8,128)(2,1)}, bf16[512,512]{1,0:T(8,128)(2,1)}, u32[]{:S(2)}, u32[]{:S(2)}) collective-permute-start(bf16[512,512]{1,0:T(8,128)(2,1)} %param.35), channel_id=1, source_target_pairs={{1,4},{3,6},{4,1},{6,3},{9,12},{11,14},{12,9},{14,11},{17,20},{19,... | collective-permute-start | bytes 1572872 | tf_op jit(solution)/shard_map/ppermute | solution.py:35
  172.2 121.0 %collective-permute-start.43 = (bf16[512,512]{1,0:T(8,128)(2,1)}, bf16[512,512]{1,0:T(8,128)(2,1)}, u32[]{:S(2)}, u32[]{:S(2)}) collective-permute-start(bf16[512,512]{1,0:T(8,128)(2,1)} %get-tuple-element.92), channel_id=1, source_target_pairs={{1,4},{3,6},{4,1},{6,3},{9,12},{11,14},{12,9},{14,11},{17,20},{19,... | collective-permute-start | bytes 1572872 | tf_op jit(solution)/shard_map/ppermute | solution.py:35
  279.6 19.8 %collective-permute-start.76 = (bf16[1,4,2,2,1,64,512]{6,5,1,4,3,2,0:T(8,128)(2,1)S(1)}, bf16[1,4,2,2,1,64,512]{6,5,1,4,3,2,0:T(8,128)(2,1)S(1)}, u32[]{:S(2)}, u32[]{:S(2)}) collective-permute-start(bf16[1,4,2,2,1,64,512]{6,5,1,4,3,2,0:T(8,128)(2,1)S(1)} %copy.106), channel_id=1, source_target_pairs={{0,4},{4,0},{8,12},{12,8},{16,20},{20,16},{24,28},{28,24},{1,5},{5... | collective-permute-start | bytes 3145736 | tf_op jit(solution)/shard_map/ppermute | solution.py:17
  281.1 18.7 %collective-permute-start.62 = (bf16[1,4,2,2,1,64,512]{6,5,1,4,3,2,0:T(8,128)(2,1)S(1)}, bf16[1,4,2,2,1,64,512]{6,5,1,4,3,2,0:T(8,128)(2,1)S(1)}, u32[]{:S(2)}, u32[]{:S(2)}) collective-permute-start(bf16[1,4,2,2,1,64,512]{6,5,1,4,3,2,0:T(8,128)(2,1)S(1)} %copy.104), channel_id=1, source_target_pairs={{0,4},{4,0},{8,12},{12,8},{16,20},{20,16},{24,28},{28,24},{1,5},{5... | collective-permute-start | bytes 3145736 | tf_op jit(solution)/shard_map/ppermute | solution.py:17
  282.8 12.8 %collective-permute-start.46 = (bf16[512,512]{1,0:T(8,128)(2,1)S(1)}, bf16[512,512]{1,0:T(8,128)(2,1)S(1)}, u32[]{:S(2)}, u32[]{:S(2)}) collective-permute-start(bf16[512,512]{1,0:T(8,128)(2,1)S(1)} %slice.225), channel_id=1, source_target_pairs={{0,4},{4,0},{8,12},{12,8},{16,20},{20,16},{24,28},{28,24},{1,5},{5... | collective-permute-start | bytes 1572872 | tf_op jit(solution)/shard_map/ppermute | solution.py:17
  291.6 12.2 %collective-permute-start.48 = (bf16[4,4,2,2,1,16,512]{6,5,4,3,2,1,0:T(8,128)(2,1)S(1)}, bf16[4,4,2,2,1,16,512]{6,5,4,3,2,1,0:T(8,128)(2,1)S(1)}, u32[]{:S(2)}, u32[]{:S(2)}) collective-permute-start(bf16[4,4,2,2,1,16,512]{6,5,4,3,2,1,0:T(8,128)(2,1)S(1)} %split.163), channel_id=1, source_target_pairs={{0,4},{4,0},{8,12},{12,8},{16,20},{20,16},{24,28},{28,24},{1,5},{5... | collective-permute-start | bytes 3145736 | tf_op jit(solution)/shard_map/ppermute | solution.py:17
  303.8 12.6 %collective-permute-start.66 = (bf16[1,2,1,2,1,64,512]{6,5,1,4,3,2,0:T(8,128)(2,1)S(1)}, bf16[1,2,1,2,1,64,512]{6,5,1,4,3,2,0:T(8,128)(2,1)S(1)}, u32[]{:S(2)}, u32[]{:S(2)}) collective-permute-start(bf16[1,2,1,2,1,64,512]{6,5,1,4,3,2,0:T(8,128)(2,1)S(1)} %split.182), channel_id=1, source_target_pairs={{0,16},{4,20},{8,24},{12,28},{16,0},{20,4},{24,8},{28,12},{1,17},{... | collective-permute-start | bytes 786440 | tf_op jit(solution)/shard_map/ppermute | solution.py:17
  307.0 14.9 %collective-permute-start.52 = (bf16[4,2,1,2,1,16,512]{6,5,4,3,2,1,0:T(8,128)(2,1)S(1)}, bf16[4,2,1,2,1,16,512]{6,5,4,3,2,1,0:T(8,128)(2,1)S(1)}, u32[]{:S(2)}, u32[]{:S(2)}) collective-permute-start(bf16[4,2,1,2,1,16,512]{6,5,4,3,2,1,0:T(8,128)(2,1)S(1)} %split.169), channel_id=1, source_target_pairs={{0,16},{4,20},{8,24},{12,28},{16,0},{20,4},{24,8},{28,12},{1,17},{... | collective-permute-start | bytes 786440 | tf_op jit(solution)/shard_map/ppermute | solution.py:17
  310.0 12.1 %collective-permute-start.49 = (bf16[4,2,2,1,1,16,512]{6,5,0,1,4,3,2:T(8,128)(2,1)S(1)}, bf16[4,2,2,1,1,16,512]{6,5,0,1,4,3,2:T(8,128)(2,1)S(1)}, u32[]{:S(2)}, u32[]{:S(2)}) collective-permute-start(bf16[4,2,2,1,1,16,512]{6,5,0,1,4,3,2:T(8,128)(2,1)S(1)} %copy.101), channel_id=1, source_target_pairs={{0,8},{4,12},{8,0},{12,4},{16,24},{20,28},{24,16},{28,20},{1,9},{5... | collective-permute-start | bytes 786440 | tf_op jit(solution)/shard_map/ppermute | solution.py:17
  311.5 13.2 %collective-permute-start.78 = (bf16[1,2,1,1,1,64,512]{6,5,1,4,3,2,0:T(8,128)(2,1)S(1)}, bf16[1,2,1,1,1,64,512]{6,5,1,4,3,2,0:T(8,128)(2,1)S(1)}, u32[]{:S(2)}, u32[]{:S(2)}) collective-permute-start(bf16[1,2,1,1,1,64,512]{6,5,1,4,3,2,0:T(8,128)(2,1)S(1)} %split.190), channel_id=1, source_target_pairs={{0,16},{4,20},{8,24},{12,28},{16,0},{20,4},{24,8},{28,12},{1,17},{... | collective-permute-start | bytes 393224 | tf_op jit(solution)/shard_map/ppermute | solution.py:17
  316.4 12.2 %collective-permute-start.64 = (bf16[1,2,1,1,1,64,512]{6,5,1,4,3,2,0:T(8,128)(2,1)S(1)}, bf16[1,2,1,1,1,64,512]{6,5,1,4,3,2,0:T(8,128)(2,1)S(1)}, u32[]{:S(2)}, u32[]{:S(2)}) collective-permute-start(bf16[1,2,1,1,1,64,512]{6,5,1,4,3,2,0:T(8,128)(2,1)S(1)} %split.180), channel_id=1, source_target_pairs={{0,16},{4,20},{8,24},{12,28},{16,0},{20,4},{24,8},{28,12},{1,17},{... | collective-permute-start | bytes 393224 | tf_op jit(solution)/shard_map/ppermute | solution.py:17
  350.2 11.9 %collective-permute-start.74 = (bf16[1,2,1,1,64,256]{5,4,3,2,1,0:T(8,128)(2,1)S(1)}, bf16[1,2,1,1,64,256]{5,4,3,2,1,0:T(8,128)(2,1)S(1)}, u32[]{:S(2)}, u32[]{:S(2)}) collective-permute-start(bf16[1,2,1,1,64,256]{5,4,3,2,1,0:T(8,128)(2,1)S(1)} %maximum_select_fusion.17), channel_id=1, source_target_pairs={{0,8},{4,12},{8,0},{12,4},{16,24},{20,28},{24,16},{28,20},{1,9},{5... | collective-permute-start | bytes 196616 | tf_op jit(solution)/shard_map/ppermute | solution.py:17
  353.6 15.1 %collective-permute-start.89 = (bf16[1,2,2,1,64,256]{5,4,3,2,1,0:T(8,128)(2,1)S(1)}, bf16[1,2,2,1,64,256]{5,4,3,2,1,0:T(8,128)(2,1)S(1)}, u32[]{:S(2)}, u32[]{:S(2)}) collective-permute-start(bf16[1,2,2,1,64,256]{5,4,3,2,1,0:T(8,128)(2,1)S(1)} %maximum_select_fusion.10), channel_id=1, source_target_pairs={{0,4},{4,0},{8,12},{12,8},{16,20},{20,16},{24,28},{28,24},{1,5},{5... | collective-permute-start | bytes 393224 | tf_op jit(solution)/shard_map/ppermute | solution.py:17
  (127 other events, 736.5 us)

commit v2 on v1

v2 whole, which is shorter than its diff:
```python
import functools
import math

import jax
import jax.numpy as jnp
from jax import lax
from jax.experimental import pallas as pl
from jax.experimental.pallas import tpu as pltpu
from jax.sharding import PartitionSpec as P

HEAD_DIM = 64
LEN = 1024
EPS = 1e-05
LANES = 128
LOW = jnp.bfloat16
F32 = jnp.float32
EXP2_SCALE = math.log2(math.e) / math.sqrt(HEAD_DIM)
INV_SCALE = 1.0 / math.sqrt(HEAD_DIM)
BARRED = -1e9


def swap_dp(value, bits):
    count = lax.axis_size("dp")
    return lax.ppermute(value, "dp", [(i, i ^ bits) for i in range(count)])


def swap_tensor(value, step):
    count = lax.axis_size("tensor")
    return lax.ppermute(value, "tensor", [(i, i ^ step) for i in range(count)])


def regroup(block):
    dp, tensor = lax.axis_size("dp"), lax.axis_size("tensor")
    pairs = [
        ((2 * k + c) * tensor + 2 * a + b, (2 * k + b) * tensor + 2 * a + c)
        for k in range(dp // 2)
        for c in range(2)
        for a in range(tensor // 2)
        for b in range(2)
        if b != c
    ]
    moved = lax.ppermute(block, ("dp", "tensor"), pairs)
    stays = (lax.axis_index("dp") % 2) == (lax.axis_index("tensor") % 2)
    return jnp.where(stays, block, moved)


def gather_units(piece):
    return spread(join_shards(piece))


def join_shards(piece):
    return jnp.stack([piece] + [swap_tensor(piece, step) for step in (1, 2, 3)], 1)


def spread(piece):
    own = [piece] + [swap_dp(piece, bits) for bits in (2, 4, 6)]
    return own, [swap_dp(block, 1) for block in own]


def sum_parts(parts):
    total = parts[0].astype(F32)
    for part in parts[1:]:
        total = total + part.astype(F32)
    return total


def reduce_core(keep, send):
    other = swap_dp(send, 1)
    return [sum_parts((keep[i], other[i])).astype(LOW) for i in range(4)]


def reduce_plane(parts):
    parts = [parts[0]] + [swap_dp(parts[i], 2 * i) for i in (1, 2, 3)]
    return [sum_parts([part[j] for part in parts]).astype(LOW) for j in range(4)]


def reduce_shards(parts):
    total = sum_parts([parts[0]] + [swap_tensor(parts[j], j) for j in (1, 2, 3)])
    bits = 8
    while bits < lax.axis_size("dp"):
        total = total + swap_dp(total.astype(LOW), bits).astype(F32)
        bits *= 2
    return total.astype(LOW)


def sum_everywhere(value):
    for step in (2, 1):
        value = value + swap_tensor(value, step)
    bits = 1
    while bits < lax.axis_size("dp"):
        value = value + swap_dp(value, bits)
        bits *= 2
    return value


def flip(value, axis, wanted):
    return jnp.where(wanted, jnp.flip(value, axis), value)


def relative_bias(shard):
    dp = lax.axis_index("dp")
    blocks = shard.reshape(2, 2, 2, -1)
    blocks = flip(flip(flip(blocks, 2, (dp & 1) != 0), 1, (dp & 2) != 0), 0, (dp & 4) != 0)
    return blocks.reshape(-1)


def dot_nt(a, b):
    return lax.dot_general(a, b, (((1,), (1,)), ((), ())), preferred_element_type=F32)


def dot_tn(a, b):
    return lax.dot_general(a, b, (((0,), (0,)), ((), ())), preferred_element_type=F32)


def dot_nn(a, b):
    return jnp.dot(a, b, preferred_element_type=F32)


def norm(value):
    center = value - jnp.mean(value, -1, keepdims=True)
    scale = lax.rsqrt(jnp.mean(center * center, -1, keepdims=True) + EPS)
    return center * scale, scale


def norm_back(grad, gain, unit, scale):
    scaled = grad * gain
    mean_a = jnp.mean(scaled, -1, keepdims=True)
    mean_b = jnp.mean(scaled * unit, -1, keepdims=True)
    return (scaled - mean_a - unit * mean_b) * scale


def lane_half(which):
    first = lax.broadcasted_iota(jnp.int32, (1, LANES), 1) < HEAD_DIM
    return first if which == 0 else jnp.logical_not(first)


VMEM_LIMIT = 14 * 2**20


def call(kernel, name, micros, outs, scratch, *operands, scalars=0):
    return pl.pallas_call(
        kernel,
        in_specs=[pl.BlockSpec(memory_space=pltpu.SMEM)] * scalars
        + [pl.BlockSpec(memory_space=pltpu.VMEM)] * (len(operands) - scalars),
        out_shape=[jax.ShapeDtypeStruct(shape, dtype) for shape, dtype in outs],
        scratch_shapes=[pltpu.VMEM(shape, dtype) for shape, dtype in scratch],
        compiler_params=pltpu.CompilerParams(vmem_limit_bytes=VMEM_LIMIT),
        cost_estimate=pl.CostEstimate(flops=int(micros * 1.1e9), bytes_accessed=0, transcendentals=0),
        name=name,
    )(*operands)


def attention_first_kernel(*refs):
    blocks, w_ref, rest = refs[:8], refs[-3], refs[8:-3] + refs[-2:]
    rows = blocks[0].shape[2]
    for at, block in enumerate(blocks):
        c, i = divmod(at, 4)
        for kind in range(4):
            for j in range(4):
                w_ref[kind, pl.ds(j * LANES + (2 * i + c) * rows, rows)] = block[kind, j]
    attention_forward_kernel(*rest[:5], w_ref, *rest[5:])


def attention_forward_kernel(
    in_ref, low_ref, other_ref, mark_ref, barred_ref, w_ref, qb, vb, ob, gain, shift,
    q_out, k_out, v_out, e_out, inv_out, o_out, att_out, unit_out, scale_out, mid_out, kmask, vmask,
):
    wq, wk, wv, wo = (w_ref.at[kind] for kind in range(4))
    rows = in_ref.shape[0]
    heads = wq.shape[0] // HEAD_DIM
    zero = jnp.zeros((), LOW)
    low = low_ref[...]
    q_out[...] = (dot_nt(low, wq[...]) + qb[...]).astype(LOW)
    for half, part in enumerate((low, other_ref[...])):
        r = slice(half * rows, (half + 1) * rows)
        keys = dot_nt(part, wk[...]).astype(LOW)
        values = (dot_nt(part, wv[...]) + vb[...]).astype(LOW)
        k_out[r] = keys
        v_out[r] = values
        for h in range(heads):
            keep = lane_half(h % 2)
            cols = slice(h // 2 * LANES, (h // 2 + 1) * LANES)
            kmask[h, r, :LANES] = jnp.where(keep, keys[:, cols], barred_ref[r])
            kmask[h, r, LANES:] = jnp.where(keep, keys[:, cols], zero)
            vmask[h, r] = jnp.where(keep, values[:, cols], jnp.ones((), LOW))
    mark = mark_ref[...]
    first = lane_half(0)
    for p in range(heads // 2):
        cols = slice(p * LANES, (p + 1) * LANES)
        scaled = q_out[:, cols].astype(F32) * EXP2_SCALE
        high = scaled.astype(LOW)
        rest = (scaled - high.astype(F32)).astype(LOW)
        mixed = []
        for h in range(2):
            keep = lane_half(h)
            query = jnp.concatenate((jnp.where(keep, high, mark), jnp.where(keep, rest, zero)), 1)
            scores = dot_nt(query, kmask[2 * p + h])
            exponent = jnp.exp2(scores - jnp.max(scores, -1, keepdims=True)).astype(LOW)
            e_out[2 * p + h] = exponent
            mixed.append(dot_nn(exponent, vmask[2 * p + h]))
        inv = 1.0 / pltpu.roll(jnp.where(first, mixed[1], mixed[0]), HEAD_DIM, 1)
        attended = jnp.where(first, mixed[0], mixed[1]) * inv
        inv_out[:, cols] = inv
        o_out[:, cols] = attended
        att_out[:, cols] = attended.astype(LOW)
    unit, scale = norm(in_ref[...].astype(F32) + dot_nn(att_out[...], wo[...]) + ob[...])
    unit_out[...] = unit
    scale_out[...] = jnp.broadcast_to(scale, scale_out.shape)
    mid_out[...] = unit * gain[...] + shift[...]


def attention_forward(layer_in, low, other, mark, barred, w, blocks=None):
    rows, width = layer_in.shape
    units = w["qb"].shape[1]
    heads = units // HEAD_DIM
    outs = [
        ((rows, units), LOW), ((2 * rows, units), LOW), ((2 * rows, units), LOW), ((heads, rows, 2 * rows), LOW),
        ((rows, units), F32), ((rows, units), F32), ((rows, units), LOW), ((rows, width), F32), ((rows, LANES), F32),
        ((rows, width), F32),
    ]
    scratch = [((heads, 2 * rows, 2 * LANES), LOW), ((heads, 2 * rows, LANES), LOW)]
    tail = (w["qb"], w["vb"], w["ob"], w["g1"], w["s1"])
    first = (layer_in, low, other, mark, barred)
    if blocks is None:
        return call(attention_forward_kernel, "attention_forward", 8, outs, scratch, *first, w["heads"], *tail)
    outs.append(((4, units, width), LOW))
    return call(attention_first_kernel, "attention_first", 8, outs, scratch, *blocks, *first, *tail)


GELU_A = math.sqrt(2.0 / math.pi)
GELU_B = 0.044715


def pieces_of(blocks):
    start = 0
    for block in blocks:
        count = block.shape[1] * block.shape[2]
        yield slice(start, start + count), block[0].reshape(count, -1), block[1].reshape(count, -1)
        start += count


def ffn_forward_kernel(*refs):
    blocks, (mid_ref, upb, db, gain, shift) = refs[:8], refs[8:13]
    low_out, act_out, slope_out, unit_out, scale_out, out_out, next_out = refs[13:]
    middle = mid_ref[...]
    low = middle.astype(LOW)
    low_out[...] = low
    total = middle + db[...]
    for r, up, down in pieces_of(blocks):
        hidden = dot_nt(low, up) + upb[:, r]
        square = hidden * hidden
        bent = jnp.tanh(hidden * (GELU_A + GELU_A * GELU_B * square))
        half = 0.5 + 0.5 * bent
        active = (hidden * half).astype(LOW)
        act_out[:, r] = active
        inner = GELU_A + 3.0 * GELU_A * GELU_B * square
        slope_out[:, r] = (half + 0.5 * hidden * (1.0 - bent * bent) * inner).astype(LOW)
        total = total + dot_nn(active, down)
    unit, scale = norm(total)
    unit_out[...] = unit
    scale_out[...] = jnp.broadcast_to(scale, scale_out.shape)
    layer_out = unit * gain[...] + shift[...]
    out_out[...] = layer_out
    next_out[...] = layer_out.astype(LOW)


def ffn_forward(middle, w):
    rows, width = middle.shape
    units = w["upb"].shape[1]
    outs = [
        ((rows, width), LOW), ((rows, units), LOW), ((rows, units), LOW), ((rows, width), F32), ((rows, LANES), F32),
        ((rows, width), F32), ((rows, width), LOW),
    ]
    return call(
        ffn_forward_kernel, "ffn_forward", 5, outs, [], *w["ffn"], middle, w["upb"], w["db"], w["g2"], w["s2"]
    )


def row_sum(value):
    return jnp.sum(value, 0, keepdims=True)


def ffn_backward_kernel(*refs):
    blocks, (grad_ref, unit_two, scale_two, slope, unit_one, scale_one, w_ref, gain_two, gain_one) = refs[:8], refs[8:17]
    branch_two_out, hidden_out, pre_one_out, branch_one_out, att_out, sums_out = refs[17:]
    grad = grad_ref[...].astype(F32)
    unit = unit_two[...]
    sums_out[0:1] = row_sum(grad * unit)
    sums_out[1:2] = row_sum(grad)
    grad_pre = norm_back(grad, gain_two[...], unit, scale_two[:, :1])
    branch = grad_pre.astype(LOW)
    branch_two_out[...] = branch
    sums_out[2:3] = row_sum(branch.astype(F32))
    grad_middle = grad_pre
    for r, up, down in pieces_of(blocks):
        hidden = (dot_nt(branch, down) * slope[:, r].astype(F32)).astype(LOW)
        hidden_out[:, r] = hidden
        grad_middle = grad_middle + dot_nn(hidden, up)
    unit = unit_one[...]
    sums_out[3:4] = row_sum(grad_middle * unit)
    sums_out[4:5] = row_sum(grad_middle)
    grad_pre = norm_back(grad_middle, gain_one[...], unit, scale_one[:, :1])
    pre_one_out[...] = grad_pre
    branch = grad_pre.astype(LOW)
    branch_one_out[...] = branch
    sums_out[5:6] = row_sum(branch.astype(F32))
    sums_out[6:8] = jnp.zeros((2, grad.shape[1]), F32)
    att_out[...] = dot_nt(branch, w_ref[3]).astype(LOW)


def ffn_backward(grad_out, kept_ffn, kept_attention, w):
    rows, width = grad_out.shape
    units = w["upb"].shape[1]
    outs = [
        ((rows, width), LOW), ((rows, units), LOW), ((rows, width), F32), ((rows, width), LOW),
        ((rows, w["qb"].shape[1]), LOW), ((8, width), F32),
    ]
    return call(
        ffn_backward_kernel, "ffn_backward", 4, outs, [], *w["ffn"],
        grad_out, kept_ffn["unit"], kept_ffn["scale"], kept_ffn["slope"], kept_attention["unit"], kept_attention["scale"],
        w["heads"], w["g2"], w["g1"],
    )


def attention_backward_kernel(
    att_ref, pre_ref, q_ref, k_ref, v_ref, e_ref, inv_ref, o_ref, w_ref,
    in_out, sent_out, dq_out, dk_out, dv_out, vmask,
):
    wq, wk, wv = (w_ref.at[kind] for kind in range(3))
    rows = att_ref.shape[0]
    heads = wq.shape[0] // HEAD_DIM
    zero = jnp.zeros((), LOW)
    first = lane_half(0)
    spare = lax.broadcasted_iota(jnp.int32, (1, LANES), 1) % HEAD_DIM
    minus = jnp.where(spare < 3, -1.0, 0.0).astype(LOW)
    for h in range(heads):
        vmask[h] = jnp.where(lane_half(h % 2), v_ref[:, h // 2 * LANES : (h // 2 + 1) * LANES], minus)
    for p in range(heads // 2):
        cols = slice(p * LANES, (p + 1) * LANES)
        queries, keys = q_ref[:, cols], k_ref[:, cols]
        grad = (att_ref[:, cols].astype(F32) * inv_ref[:, cols]).astype(LOW)
        dots = grad.astype(F32) * o_ref[:, cols]
        dq, dk, dv = [], [], []
        for h in range(2):
            keep = lane_half(h)
            dot = jnp.sum(jnp.where(keep, dots, 0.0), -1, keepdims=True)
            top = dot.astype(LOW)
            left = dot - top.astype(F32)
            mid = left.astype(LOW)
            end = (left - mid.astype(F32)).astype(LOW)
            pieces = jnp.where(spare == 0, top, jnp.where(spare == 1, mid, jnp.where(spare == 2, end, zero)))
            exponent = e_ref[2 * p + h]
            centered = dot_nt(jnp.where(keep, grad, pieces), vmask[2 * p + h])
            grad_scores = (exponent.astype(F32) * centered).astype(LOW)
            dq.append(dot_nn(grad_scores, keys))
            dk.append(dot_tn(grad_scores, queries))
            dv.append(dot_tn(exponent, grad))
        dq_out[:, cols] = (jnp.where(first, dq[0], dq[1]) * INV_SCALE).astype(LOW)
        dk_out[:, cols] = (jnp.where(first, dk[0], dk[1]) * INV_SCALE).astype(LOW)
        dv_out[:, cols] = jnp.where(first, dv[0], dv[1]).astype(LOW)
    dq, dk, dv = dq_out[...], dk_out[...], dv_out[...]
    sent_out[...] = (dot_nn(dk[rows:], wk[...]) + dot_nn(dv[rows:], wv[...])).astype(LOW)
    in_out[...] = pre_ref[...] + dot_nn(dq, wq[...]) + dot_nn(dk[:rows], wk[...]) + dot_nn(dv[:rows], wv[...])


def attention_backward(grad_att, grad_pre, kept, w):
    rows, width = grad_pre.shape
    units = w["qb"].shape[1]
    heads = units // HEAD_DIM
    outs = [
        ((rows, width), F32), ((rows, width), LOW), ((rows, units), LOW), ((2 * rows, units), LOW), ((2 * rows, units), LOW),
    ]
    return call(
        attention_backward_kernel, "attention_backward", 12, outs, [((heads, 2 * rows, LANES), LOW)],
        grad_att, grad_pre, kept["q"], kept["k"], kept["v"], kept["e"], kept["inv"], kept["o"], w["heads"],
    )


def both_layers(firsts, seconds):
    return sum(dot_tn(a[...], b[...]) for a, b in zip(firsts, seconds))


def ffn_grads_kernel(*refs):
    actives, branches, hiddens, middles, attendeds, ones_branches = (refs[2 * i : 2 * i + 2] for i in range(6))
    outs = refs[12:]
    rows, units = actives[0].shape
    step = units // 8
    ur = step // 4
    hr = attendeds[0].shape[1] // 32
    one = jnp.ones((rows, LANES), LOW)
    out_grad = both_layers(attendeds, ones_branches).astype(LOW)
    for at in range(8):
        c, i = divmod(at, 4)
        out = outs[c].at[i]
        cols = slice(at * step, (at + 1) * step)
        down = both_layers([a.at[:, cols] for a in actives], branches).astype(LOW)
        up = both_layers([h.at[:, cols] for h in hiddens], middles).astype(LOW)
        bias = sum(dot_tn(h[:, cols], one) for h in hiddens).astype(LOW)
        for j in range(4):
            out[j, :ur] = down[j * ur : (j + 1) * ur]
            out[j, ur : 2 * ur] = up[j * ur : (j + 1) * ur]
            head = j * LANES + (2 * i + c) * hr
            out[j, 2 * ur : 2 * ur + hr] = out_grad[head : head + hr]
            for g in range(4):
                first = j * ur + g * (ur // 4)
                out[j, 2 * ur + hr :, g * LANES : (g + 1) * LANES] = bias[first : first + ur // 4]


def ffn_grads(pairs):
    rows, units = pairs[0][0].shape
    width = pairs[1][0].shape[1]
    ur, hr = units // 32, pairs[4][0].shape[1] // 32
    out = ((4, 4, 2 * ur + hr + ur // 4, width), LOW)
    return call(ffn_grads_kernel, "ffn_grads", 7, [out, out], [], *[v for pair in pairs for v in pair])


def head_grads_kernel(*refs):
    dqs, dks, dvs, lows, others = (refs[2 * i : 2 * i + 2] for i in range(5))
    outs = refs[10:]
    rows, units = dqs[0].shape
    hr = units // 32
    one = jnp.ones((rows, LANES), LOW)

    def halves(grads):
        own = [g.at[:rows] for g in grads]
        return own, [g.at[rows:] for g in grads]

    dk_own, dk_other = halves(dks)
    dv_own, dv_other = halves(dvs)
    grads = [
        both_layers(dqs, lows),
        both_layers(dk_own + dk_other, lows + others),
        both_layers(dv_own + dv_other, lows + others),
    ]
    grads = [g.astype(LOW) for g in grads]
    biases = [sum(dot_tn(g[...], one) for g in part).astype(LOW) for part in (dqs, dv_own + dv_other)]
    rest = jnp.zeros((hr, outs[0].shape[3] - 2 * LANES), LOW)
    for at in range(8):
        c, i = divmod(at, 4)
        for j in range(4):
            out = outs[c].at[i, j]
            first = j * LANES + (2 * i + c) * hr
            for kind in range(3):
                out[kind * hr : (kind + 1) * hr] = grads[kind][first : first + hr]
            for kind in range(2):
                out[3 * hr :, kind * LANES : (kind + 1) * LANES] = biases[kind][first : first + hr]
            out[3 * hr :, 2 * LANES :] = rest


def head_grads(pairs):
    units = pairs[0][0].shape[1]
    width = pairs[3][0].shape[1]
    out = ((4, 4, 4 * (units // 32), width), LOW)
    return call(head_grads_kernel, "head_grads", 5, [out, out], [], *[v for pair in pairs for v in pair])


def first_row(column):
    return column.T[:1]


def ffn_finish_kernel(ur, hr, eighth_ref, *refs):
    blocks, (down_out, up_out, out_out, bias_out, up_all, bias_all) = refs[:8], refs[8:]
    for at, block in enumerate(blocks):
        c, i = divmod(at, 4)
        slot = eighth_ref[0] ^ (2 * i + c)
        units = pl.ds(pl.multiple_of(slot * ur, ur), ur)
        down_out[units] = block[:ur].astype(F32)
        up_all[units] = block[ur : 2 * ur].astype(F32)
        out_out[pl.ds(pl.multiple_of(slot * hr, hr), hr)] = block[2 * ur : 2 * ur + hr].astype(F32)
        for g in range(4):
            some = pl.ds(pl.multiple_of(slot * ur + g * (ur // 4), ur // 4), ur // 4)
            bias_all[some] = block[2 * ur + hr :, g * LANES : (g + 1) * LANES].astype(F32)
    up_out[...] = up_all[...].T
    bias_out[...] = first_row(bias_all[...])


def ffn_finish(own, ur, hr, eighth):
    own, other = spread(own)
    width = own[0].shape[1]
    outs = [((8 * ur, width), F32), ((width, 8 * ur), F32), ((8 * hr, width), F32), ((1, 8 * ur), F32)]
    scratch = [((8 * ur, width), F32), ((8 * ur, LANES), F32)]
    return call(
        functools.partial(ffn_finish_kernel, ur, hr), "ffn_finish", 2, outs, scratch, eighth, *own, *other, scalars=1
    )


def head_finish_kernel(hr, eighth_ref, *refs):
    blocks, outs, biases, scratch = refs[:8], refs[8:11], refs[11:13], refs[13:]
    for at, block in enumerate(blocks):
        c, i = divmod(at, 4)
        slot = eighth_ref[0] ^ (2 * i + c)
        units = pl.ds(pl.multiple_of(slot * hr, hr), hr)
        for kind in range(3):
            scratch[kind][units] = block[kind * hr : (kind + 1) * hr].astype(F32)
        for kind in range(2):
            scratch[3 + kind][units] = block[3 * hr :, kind * LANES : (kind + 1) * LANES].astype(F32)
    for kind in range(3):
        outs[kind][...] = scratch[kind][...].T
    for kind in range(2):
        biases[kind][...] = first_row(scratch[3 + kind][...])


def head_finish(own, hr, eighth):
    own, other = spread(own)
    width = own[0].shape[1]
    outs = [((width, 8 * hr), F32)] * 3 + [((1, 8 * hr), F32)] * 2
    scratch = [((8 * hr, width), F32)] * 3 + [((8 * hr, LANES), F32)] * 2
    return call(
        functools.partial(head_finish_kernel, hr), "head_finish", 2, outs, scratch, eighth, *own, *other, scalars=1
    )


def per_device(
    inputs, segment_ids, query_weight, query_bias, key_weight, value_weight, value_bias, out_weight, out_bias,
    first_gain, first_shift, up_weight, up_bias, down_weight, down_bias, second_gain, second_shift, cotangent,
):
    rows, width = inputs.shape
    dp, tensor = lax.axis_index("dp"), lax.axis_index("tensor")
    core, eighth = dp % 2, dp % 8
    shard_heads, shard_units = query_weight.shape[1], up_weight.shape[1]
    hr, ur = shard_heads // 8, shard_units // 8

    def columns(weight, count):
        return lax.dynamic_slice_in_dim(weight, eighth * count, count, 1).T

    def own_rows(weight, count):
        return lax.dynamic_slice_in_dim(weight, eighth * count, count, 0)

    heads_piece = jnp.stack([columns(v, hr) for v in (query_weight, key_weight, value_weight)] + [own_rows(out_weight, hr)])
    ffn_piece = jnp.stack((columns(up_weight, ur), own_rows(down_weight, ur)))
    first_in = regroup(inputs)
    heads_piece = join_shards(heads_piece)
    heads_piece, ffn_piece = lax.optimization_barrier((heads_piece, ffn_piece))
    own, others = spread(heads_piece)
    head_blocks = own + others
    own, others = gather_units(ffn_piece)
    ffn_blocks = own + others
    seq = lax.dynamic_slice_in_dim(segment_ids, (tensor // 2) * LEN, LEN)
    seq = jnp.where(core == tensor % 2, seq, swap_dp(seq, 1))
    labels_own = lax.dynamic_slice_in_dim(seq, core * rows, rows)
    labels_all = jnp.concatenate((labels_own, lax.dynamic_slice_in_dim(seq, (1 - core) * rows, rows)))
    code = jnp.arange(LANES) % HEAD_DIM - 1
    mark = (labels_own[:, None] == code).astype(LOW)
    barred = jnp.where(labels_all[:, None] == code, 0.0, BARRED).astype(LOW)
    flat = jnp.concatenate((relative_bias(query_bias), relative_bias(value_bias), relative_bias(up_bias)))
    flat = jnp.stack((flat, swap_tensor(flat, 1)))
    flat = jnp.concatenate((flat, swap_tensor(flat, 2)))
    w = {
        "ffn": ffn_blocks,
        "qb": flat[:, :shard_heads].reshape(1, -1), "vb": flat[:, shard_heads : 2 * shard_heads].reshape(1, -1),
        "upb": flat[:, 2 * shard_heads :].reshape(4, 4, 2, ur).transpose(2, 1, 0, 3).reshape(1, -1),
        "ob": out_bias[None], "g1": first_gain[None], "s1": first_shift[None], "db": down_bias[None],
        "g2": second_gain[None], "s2": second_shift[None],
    }

    kept = []
    layer_in, low = first_in, first_in
    for position in range(2):
        other = swap_dp(low, 1)
        made = attention_forward(layer_in, low, other, mark, barred, w, None if position else head_blocks)
        q, k, v, e, inv, o, attended, unit_one, scale_one, middle = made[:10]
        if position == 0:
            w["heads"] = made[10]
        middle_low, active, slope, unit_two, scale_two, layer_out, next_low = ffn_forward(middle, w)
        attention = {"q": q, "k": k, "v": v, "e": e, "inv": inv, "o": o, "unit": unit_one, "scale": scale_one}
        ffn = {"slope": slope, "unit": unit_two, "scale": scale_two}
        kept.append((attention, ffn, low, other, attended, middle_low, active))
        layer_in, low = layer_out, next_low
    result = regroup(low)

    grad_flow = regroup(cotangent)
    ffn_pairs, head_pairs, sums = [], [], []
    for position in (1, 0):
        attention, ffn, low, other, attended, middle_low, active = kept[position]
        branch_two, grad_hidden, grad_pre, branch_one, grad_att, six = ffn_backward(grad_flow, ffn, attention, w)
        sums.append(six)
        ffn_pairs.append((active, branch_two, grad_hidden, middle_low, attended, branch_one))
        if position == 0:
            ffn_parts = reduce_core(*ffn_grads(list(zip(*ffn_pairs))))
            grad_att, *ffn_parts = lax.optimization_barrier((grad_att, *ffn_parts))
        grad_in, sent, dq, dk, dv = attention_backward(grad_att, grad_pre, attention, w)
        grad_flow = grad_in + swap_dp(sent, 1).astype(F32)
        head_pairs.append((dq, dk, dv, low, other))
    head_parts = reduce_core(*head_grads(list(zip(*head_pairs))))
    ffn_own = reduce_shards(reduce_plane(ffn_parts))
    head_own = reduce_shards(reduce_plane(head_parts))
    at = jnp.reshape(eighth, (1,)).astype(jnp.int32)
    down_grad, up_grad, out_grad, up_bias_grad = ffn_finish(ffn_own, ur, hr, at)
    q_grad, k_grad, v_grad, q_bias_grad, v_bias_grad = head_finish(head_own, hr, at)
    shared = sum_everywhere(sums[0] + sums[1])
    input_grad = regroup(grad_flow.astype(LOW)).astype(F32)
    return (
        result, input_grad, q_grad, q_bias_grad[0], k_grad, v_grad, v_bias_grad[0], out_grad, shared[5], shared[3], shared[4],
        up_grad, up_bias_grad[0], down_grad, shared[2], shared[0], shared[1],
    )


def solution(mesh):
    split = P(("dp", "tensor"), None)
    columns, rows, part = P(None, "tensor"), P("tensor", None), P("tensor")
    return jax.shard_map(
        per_device,
        mesh=mesh,
        in_specs=(
            split, P("dp"), columns, part, columns, columns, part, rows, P(), P(), P(), columns, part, rows, P(), P(),
            P(), split,
        ),
        out_specs=(
            split, split, columns, part, columns, columns, part, rows, P(), P(), P(), columns, part, rows, P(), P(), P(),
        ),
        check_vma=False,
    )
```

time: 376 us -> 255 us (0.68)
  matrix products: 107 us -> 0 us
  Pallas kernels: 0 us -> 74.6 us
  other arithmetic: 58 us -> 6.05 us
  blocking collectives: 38.3 us -> 0 us
  waiting for transfers between devices: 34.7 us -> 51.7 us
  starting transfers between devices: 106 us -> 92.3 us
    dot_general x40 -> x0, matrix products: 85.8 us -> none  [the longest x12 25.2 us: dot_nt(): lax.dot_general(a, b, (((1,), (1,)), ((), ())), preferred_element_type=F32)]
    pallas_call x0 -> x12, Pallas kernels: none -> 74.6 us  [call(): pl.pallas_call(kernel, in_specs=[pl.BlockSpec(memory_space=pltpu.SMEM)] *...]
    convert_element_type x18 -> x6, other arithmetic: 41.6 us -> 1.72 us  [the longest x2 1.18 us: reduce_core(): return [sum_parts((keep[i], other[i])).astype(LOW) for i in range(4)]]
    psum x1 -> x0, blocking collectives: 38.3 us -> none  [per_device(): small = lax.psum(small, ('dp', 'tensor')).reshape(-1)]
    sub x2 -> x0, matrix products: 21.1 us -> none  [attention_forward(): exponent = jnp.exp(scores - jnp.max(scores, -1, keepdims=True))]
    ppermute x24 -> x16, waiting for transfers between devices: 1.4 us -> 16.6 us  [swap_tensor(): return lax.ppermute(value, 'tensor', [(i, i ^ step) for i in range(count)])]
    ppermute x24 -> x16, starting transfers between devices: 28.9 us -> 20.7 us  [swap_tensor(): return lax.ppermute(value, 'tensor', [(i, i ^ step) for i in range(count)])]
    reduce_sum x9 -> x0, other arithmetic: 6.19 us -> none  [the longest x2 1.74 us: attention_backward(): grad_ob = jnp.sum(grad_branch.astype(F32), 0)]
  transfers between devices with their start and end apart: 90 -> 64, of which waited for: 20 -> 17; matrix products, arithmetic and copies ran while one was open for 35% -> 6% of each run, Pallas kernels for 0% -> 12%
where the time goes in v2:
time: 255 us; the launch traced here: 251 us
  starting transfers between devices  92.3 us (36%)
  Pallas kernels  74.6 us (29%)
  waiting for transfers between devices  51.7 us (20%)
  local copies, waits for them, and re-layouts  24.9 us (10%)
  other arithmetic  6.05 us (2%)
    pallas_call x12, Pallas kernels, call(): pl.pallas_call(kernel, in_specs=[pl.BlockSpec(memory_space=pltpu.SMEM)] *...  74.6 us
    ppermute x44, starting transfers between devices, swap_dp(): return lax.ppermute(value, 'dp', [(i, i ^ bits) for i in range(count)])  58.4 us
    ppermute x44, waiting for transfers between devices, swap_dp(): return lax.ppermute(value, 'dp', [(i, i ^ bits) for i in range(count)])  35.1 us
    ppermute x16, starting transfers between devices, swap_tensor(): return lax.ppermute(value, 'tensor', [(i, i ^ step) for i in range(count)])  20.7 us
    ppermute x16, waiting for transfers between devices, swap_tensor(): return lax.ppermute(value, 'tensor', [(i, i ^ step) for i in range(count)])  16.6 us
    unnamed x78, local copies, waits for them, and re-layouts  13.5 us
    ppermute x4, starting transfers between devices, regroup(): moved = lax.ppermute(block, ('dp', 'tensor'), pairs)  13.2 us
  transfers between devices with their start and end apart: 64, of which 17 were waited for; matrix products, arithmetic and copies ran while one was open for 6% of the time, Pallas kernels for 12%

profile of v2, /device:TPU:1, one launch (start us, length us, event | category | flops | bytes accessed | tf_op | source)
XLA Modules:
  0.0 251.3 jit_solution(9680308491752146028)
XLA Ops:
  3.9 3.2 %collective-permute-start.1 = (bf16[4,16,512]{2,1,0:T(8,128)(2,1)S(1)}, bf16[4,16,512]{2,1,0:T(8,128)(2,1)S(1)}, u32[]{:S(2)}, u32[]{:S(2)}) collective-permute-start(bf16[4,16,512]{2,1,0:T(8,128)(2,1)S(1)} %get-tuple-element.184), channel_id=1, source_target_pairs={{0,2},{1,3},{2,0},{3,1},{4,6},{5,7},{6,4},{7,5},{8,10},{9,11},{10,... | collective-permute-start | bytes 196616 | tf_op jit(solution)/shard_map/ppermute | solution.py:29
  15.3 3.1 %collective-permute-start.20 = (bf16[512,512]{1,0:T(8,128)(2,1)S(1)}, bf16[512,512]{1,0:T(8,128)(2,1)S(1)}, u32[]{:S(2)}, u32[]{:S(2)}) collective-permute-start(bf16[512,512]{1,0:T(8,128)(2,1)S(1)} %copy-done.28), channel_id=1, source_target_pairs={{1,4},{3,6},{4,1},{6,3},{9,12},{11,14},{12,9},{14,11},{17,20},{19,... | collective-permute-start | bytes 1572872 | tf_op jit(solution)/shard_map/ppermute | solution.py:42
  18.9 3.1 %collective-permute-start.4 = (bf16[2,64,512]{2,1,0:T(8,128)(2,1)S(1)}, bf16[2,64,512]{2,1,0:T(8,128)(2,1)S(1)}, u32[]{:S(2)}, u32[]{:S(2)}) collective-permute-start(bf16[2,64,512]{2,1,0:T(8,128)(2,1)S(1)} %pad_maximum_fusion.2), channel_id=1, source_target_pairs={{0,2},{1,3},{2,0},{3,1},{4,6},{5,7},{6,4},{7,5},{8,10},{9,11},{10,... | collective-permute-start | bytes 393224 | tf_op jit(solution)/shard_map/ppermute | solution.py:29
  24.5 4.3 %collective-permute-done.5 = bf16[2,64,512]{2,1,0:T(8,128)(2,1)S(1)} collective-permute-done((bf16[2,64,512]{2,1,0:T(8,128)(2,1)S(1)}, bf16[2,64,512]{2,1,0:T(8,128)(2,1)S(1)}, u32[]{:S(2)}, u32[]{:S(2)}) %collective-permute-start.5) | collective-permute-done | bytes 131104 | tf_op jit(solution)/shard_map/ppermute | solution.py:29
  38.0 3.2 %collective-permute-start.19 = (bf16[4,4,16,512]{3,2,1,0:T(8,128)(2,1)S(1)}, bf16[4,4,16,512]{3,2,1,0:T(8,128)(2,1)S(1)}, u32[]{:S(2)}, u32[]{:S(2)}) collective-permute-start(bf16[4,4,16,512]{3,2,1,0:T(8,128)(2,1)S(1)} %collective-permute-done.15.refs_3_), channel_id=1, source_target_pairs={{0,4},{4,0},{8,12},{12,8},{16,20},{20,16},{24,28},{28,24},{1,5},{5... | collective-permute-start | bytes 786440 | tf_op jit(solution)/shard_map/ppermute | solution.py:24
  57.7 9.9 %collective-permute-done.7.refs_2_ = bf16[2,4,64,512]{3,2,1,0:T(8,128)(2,1)S(1)} collective-permute-done((bf16[2,4,64,512]{3,2,1,0:T(8,128)(2,1)S(1)}, bf16[2,4,64,512]{3,2,1,0:T(8,128)(2,1)S(1)}, u32[]{:S(2)}, u32[]{:S(2)}) %collective-permute-start.7) | collective-permute-done | bytes 524320 | tf_op jit(solution)/shard_map/ppermute | solution.py:24
  73.0 8.8 %attention_first.1 = (bf16[512,512]{1,0:T(8,128)(2,1)S(1)}, bf16[1024,512]{1,0:T(8,128)(2,1)S(1)}, bf16[1024,512]{1,0:T(8,128)(2,1)S(1)}, bf16[8,512,1024]{2,1,0...) custom-call(bf16[4,4,16,512]{3,2,1,0:T(8,128)(2,1)S(1)} %pad_maximum, ...), custom_call_target="tpu_custom_call" | custom-call | flops 8800000000 | tf_op jit(solution)/shard_map/attention_first/pallas_call | solution.py:141
  81.8 3.3 %copy-done.17 = bf16[8,512,1024]{2,1,0:T(8,128)(2,1)} copy-done((bf16[8,512,1024]{2,1,0:T(8,128)(2,1)}, bf16[8,512,1024]{2,1,0:T(8,128)(2,1)S(1)}, u32[]{:S(2)}) %copy-start.17) | copy-done | bytes 8388632
  87.0 5.3 %ffn_forward.2 = (bf16[512,512]{1,0:T(8,128)(2,1)S(1)}, bf16[512,2048]{1,0:T(8,128)(2,1)S(1)}, bf16[512,2048]{1,0:T(8,128)(2,1)S(1)}, f32[512,512]{1,0:T(8,128)S...) custom-call(bf16[2,4,64,512]{3,2,1,0:T(8,128)(2,1)S(1)} %pad_maximum_fusion.refs_0_, ...), custom_call_target="tpu_custom_call" | custom-call | flops 5500000256 | tf_op jit(solution)/shard_map/ffn_forward/pallas_call | solution.py:141
  94.3 8.2 %attention_forward.1 = (bf16[512,512]{1,0:T(8,128)(2,1)S(1)}, bf16[1024,512]{1,0:T(8,128)(2,1)S(1)}, bf16[1024,512]{1,0:T(8,128)(2,1)S(1)}, bf16[8,512,1024]{2,1...) custom-call(f32[512,512]{1,0:T(8,128)S(1)} %get-tuple-element.96.in_, ...), custom_call_target="tpu_custom_call" | custom-call | flops 8800000000 | tf_op jit(solution)/shard_map/attention_forward/pallas_call | solution.py:141
  102.6 5.7 %ffn_forward.3 = (bf16[512,512]{1,0:T(8,128)(2,1)S(1)}, bf16[512,2048]{1,0:T(8,128)(2,1)S(1)}, bf16[512,2048]{1,0:T(8,128)(2,1)S(1)}, f32[512,512]{1,0:T(8,128)S...) custom-call(bf16[2,4,64,512]{3,2,1,0:T(8,128)(2,1)S(1)} %pad_maximum_fusion.refs_0_, ...), custom_call_target="tpu_custom_call" | custom-call | flops 5500000256 | tf_op jit(solution)/shard_map/ffn_forward/pallas_call | solution.py:141
  108.3 5.4 %ffn_backward.2 = (bf16[512,512]{1,0:T(8,128)(2,1)S(1)}, bf16[512,2048]{1,0:T(8,128)(2,1)S(1)}, f32[512,512]{1,0:T(8,128)S(1)}, bf16[512,512]{1,0:T(8,128)(2,1)S...) custom-call(bf16[2,4,64,512]{3,2,1,0:T(8,128)(2,1)S(1)} %pad_maximum_fusion.refs_0_, ...), custom_call_target="tpu_custom_call" | custom-call | flops 4400000000 | tf_op jit(solution)/shard_map/ffn_backward/pallas_call | solution.py:141
  113.8 11.5 %attention_backward.2 = (f32[512,512]{1,0:T(8,128)S(1)}, bf16[512,512]{1,0:T(8,128)(2,1)S(1)}, bf16[512,512]{1,0:T(8,128)(2,1)S(1)}, bf16[1024,512]{1,0:T(8,128)(2,1)S(1)}, bf16[1024,512]{1,0:T(8,128)(2,1)S(1)}) custom-call(bf16[512,512]{1,0:T(8,128)(2,1)S(1)} %get-tuple-element.106.att_ref, f32[512,512]{1,0:T(8,128)S(1)} %get-tuple-element.107.pre_ref, ...), custom_call_target="tpu_custom_call" | custom-call | flops 13200000000 | tf_op jit(solution)/shard_map/attention_backward/pallas_call | solution.py:141
  127.4 5.4 %ffn_backward.3 = (bf16[512,512]{1,0:T(8,128)(2,1)S(1)}, bf16[512,2048]{1,0:T(8,128)(2,1)S(1)}, f32[512,512]{1,0:T(8,128)S(1)}, bf16[512,512]{1,0:T(8,128)(2,1)S...) custom-call(bf16[2,4,64,512]{3,2,1,0:T(8,128)(2,1)S(1)} %pad_maximum_fusion.refs_0_, ...), custom_call_target="tpu_custom_call" | custom-call | flops 4400000000 | tf_op jit(solution)/shard_map/ffn_backward/pallas_call | solution.py:141
  132.8 6.2 %ffn_grads.1 = (bf16[4,4,160,512]{3,2,1,0:T(8,128)(2,1)S(1)}, bf16[4,4,160,512]{3,2,1,0:T(8,128)(2,1)S(1)}) custom-call(bf16[512,2048]{1,0:T(8,128)(2,1)S(1)} %get-tuple-element.122.refs_0_, bf16[512,2048]{1,0:T(8,128)(2,1)S(1)} %get-tuple-element.123.refs_1_, bf16[512,512]{1,0:T(8,128)(2,1)S(1)} %get-tuple-element.124.refs_2_, ...), custom_call_target="tpu_custom_call" | custom-call | flops 7699999744 | tf_op jit(solution)/shard_map/ffn_grads/pallas_call | solution.py:141
  146.2 11.2 %attention_backward.3 = (f32[512,512]{1,0:T(8,128)S(1)}, bf16[512,512]{1,0:T(8,128)(2,1)S(1)}, bf16[512,512]{1,0:T(8,128)(2,1)S(1)}, bf16[1024,512]{1,0:T(8,128)(2,1)S(1)}, bf16[1024,512]{1,0:T(8,128)(2,1)S(1)}) custom-call(bf16[512,512]{1,0:T(8,128)(2,1)S(1)} %get-tuple-element.136.att_ref, f32[512,512]{1,0:T(8,128)S(1)} %get-tuple-element.137.pre_ref, ...), custom_call_target="tpu_custom_call" | custom-call | flops 13200000000 | tf_op jit(solution)/shard_map/attention_backward/pallas_call | solution.py:141
  157.5 3.9 %head_grads.1 = (bf16[4,4,64,512]{3,2,1,0:T(8,128)(2,1)S(1)}, bf16[4,4,64,512]{3,2,1,0:T(8,128)(2,1)S(1)}) custom-call(bf16[512,512]{1,0:T(8,128)(2,1)S(1)} %get-tuple-element.146.refs_0_, bf16[512,512]{1,0:T(8,128)(2,1)S(1)} %get-tuple-element.147.refs_1_, bf16[1024,512]{1,0:T(8,128)(2,1)S(1)} %get-tuple-element.148.refs_2_, ...), custom_call_target="tpu_custom_call" | custom-call | flops 5500000256 | tf_op jit(solution)/shard_map/head_grads/pallas_call | solution.py:141
  176.4 12.0 %collective-permute-done.63 = f32[8,512]{1,0:T(8,128)S(1)} collective-permute-done((f32[8,512]{1,0:T(8,128)S(1)}, f32[8,512]{1,0:T(8,128)S(1)}, u32[]{:S(2)}, u32[]{:S(2)}) %collective-permute-start.63) | collective-permute-done | bytes 16416 | tf_op jit(solution)/shard_map/ppermute | solution.py:24
  188.4 14.9 %collective-permute-start.30 = (bf16[512,512]{1,0:T(8,128)(2,1)S(1)}, bf16[512,512]{1,0:T(8,128)(2,1)S(1)}, u32[]{:S(2)}, u32[]{:S(2)}) collective-permute-start(bf16[512,512]{1,0:T(8,128)(2,1)S(1)} %get-tuple-element.145), channel_id=1, source_target_pairs={{0,4},{4,0},{8,12},{12,8},{16,20},{20,16},{24,28},{28,24},{1,5},{5... | collective-permute-start | bytes 1572872 | tf_op jit(solution)/shard_map/ppermute | solution.py:24
  204.5 4.5 %collective-permute-start.51 = (bf16[160,512]{1,0:T(8,128)(2,1)S(1)}, bf16[160,512]{1,0:T(8,128)(2,1)S(1)}, u32[]{:S(2)}, u32[]{:S(2)}) collective-permute-start(bf16[160,512]{1,0:T(8,128)(2,1)S(1)} %get-tuple-element.174), channel_id=1, source_target_pairs={{0,3},{1,2},{2,1},{3,0},{4,7},{5,6},{6,5},{7,4},{8,11},{9,10},{10,... | collective-permute-start | bytes 491528 | tf_op jit(solution)/shard_map/ppermute | solution.py:29
  212.7 4.2 %collective-permute-done.51 = bf16[160,512]{1,0:T(8,128)(2,1)S(1)} collective-permute-done((bf16[160,512]{1,0:T(8,128)(2,1)S(1)}, bf16[160,512]{1,0:T(8,128)(2,1)S(1)}, u32[]{:S(2)}, u32[]{:S(2)}) %collective-permute-start.51) | collective-permute-done | bytes 163872 | tf_op jit(solution)/shard_map/ppermute | solution.py:29
  216.9 4.9 %collective-permute-start.31 = (bf16[512,512]{1,0:T(8,128)(2,1)S(1)}, bf16[512,512]{1,0:T(8,128)(2,1)S(1)}, u32[]{:S(2)}, u32[]{:S(2)}) collective-permute-start(bf16[512,512]{1,0:T(8,128)(2,1)S(1)} %add_convert_fusion.4), channel_id=1, source_target_pairs={{1,4},{3,6},{4,1},{6,3},{9,12},{11,14},{12,9},{14,11},{17,20},{19,... | collective-permute-start | bytes 1572872 | tf_op jit(solution)/shard_map/ppermute | solution.py:42
  222.5 2.9 %collective-permute-start.54 = (bf16[160,512]{1,0:T(8,128)(2,1)S(1)}, bf16[160,512]{1,0:T(8,128)(2,1)S(1)}, u32[]{:S(2)}, u32[]{:S(2)}) collective-permute-start(bf16[160,512]{1,0:T(8,128)(2,1)S(1)} %fusion.6.refs_0_), channel_id=1, source_target_pairs={{0,24},{4,28},{8,16},{12,20},{16,8},{20,12},{24,0},{28,4},{1,25},{... | collective-permute-start | bytes 491528 | tf_op jit(solution)/shard_map/ppermute | solution.py:24
  226.0 3.0 %collective-permute-done.54.refs_3_ = bf16[160,512]{1,0:T(8,128)(2,1)S(1)} collective-permute-done((bf16[160,512]{1,0:T(8,128)(2,1)S(1)}, bf16[160,512]{1,0:T(8,128)(2,1)S(1)}, u32[]{:S(2)}, u32[]{:S(2)}) %collective-permute-start.54) | collective-permute-done | bytes 163872 | tf_op jit(solution)/shard_map/ppermute | solution.py:24
  (257 shorter events, 101.3 us)
Async XLA Ops:
  3.9 14.6 %collective-permute-start.1 = (bf16[4,16,512]{2,1,0:T(8,128)(2,1)S(1)}, bf16[4,16,512]{2,1,0:T(8,128)(2,1)S(1)}, u32[]{:S(2)}, u32[]{:S(2)}) collective-permute-start(bf16[4,16,512]{2,1,0:T(8,128)(2,1)S(1)} %get-tuple-element.184), channel_id=1, source_target_pairs={{0,2},{1,3},{2,0},{3,1},{4,6},{5,7},{6,4},{7,5},{8,10},{9,11},{10,... | collective-permute-start | bytes 196616 | tf_op jit(solution)/shard_map/ppermute | solution.py:29
  15.3 26.0 %collective-permute-start.20 = (bf16[512,512]{1,0:T(8,128)(2,1)S(1)}, bf16[512,512]{1,0:T(8,128)(2,1)S(1)}, u32[]{:S(2)}, u32[]{:S(2)}) collective-permute-start(bf16[512,512]{1,0:T(8,128)(2,1)S(1)} %copy-done.28), channel_id=1, source_target_pairs={{1,4},{3,6},{4,1},{6,3},{9,12},{11,14},{12,9},{14,11},{17,20},{19,... | collective-permute-start | bytes 1572872 | tf_op jit(solution)/shard_map/ppermute | solution.py:42
  18.9 12.7 %collective-permute-start.4 = (bf16[2,64,512]{2,1,0:T(8,128)(2,1)S(1)}, bf16[2,64,512]{2,1,0:T(8,128)(2,1)S(1)}, u32[]{:S(2)}, u32[]{:S(2)}) collective-permute-start(bf16[2,64,512]{2,1,0:T(8,128)(2,1)S(1)} %pad_maximum_fusion.2), channel_id=1, source_target_pairs={{0,2},{1,3},{2,0},{3,1},{4,6},{5,7},{6,4},{7,5},{8,10},{9,11},{10,... | collective-permute-start | bytes 393224 | tf_op jit(solution)/shard_map/ppermute | solution.py:29
  22.3 14.4 %collective-permute-start.15 = (bf16[4,4,16,512]{3,2,1,0:T(8,128)(2,1)S(1)}, bf16[4,4,16,512]{3,2,1,0:T(8,128)(2,1)S(1)}, u32[]{:S(2)}, u32[]{:S(2)}) collective-permute-start(bf16[4,4,16,512]{3,2,1,0:T(8,128)(2,1)S(1)} %pad_maximum_fusion.1.refs_0_), channel_id=1, source_target_pairs={{0,24},{4,28},{8,16},{12,20},{16,8},{20,12},{24,0},{28,4},{1,25},{... | collective-permute-start | bytes 786440 | tf_op jit(solution)/shard_map/ppermute | solution.py:24
  41.4 15.3 %collective-permute-start.8 = (bf16[2,4,64,512]{3,2,1,0:T(8,128)(2,1)S(1)}, bf16[2,4,64,512]{3,2,1,0:T(8,128)(2,1)S(1)}, u32[]{:S(2)}, u32[]{:S(2)}) collective-permute-start(bf16[2,4,64,512]{3,2,1,0:T(8,128)(2,1)S(1)} %pad_maximum_fusion.refs_0_), channel_id=1, source_target_pairs={{0,24},{4,28},{8,16},{12,20},{16,8},{20,12},{24,0},{28,4},{1,25},{... | collective-permute-start | bytes 1572872 | tf_op jit(solution)/shard_map/ppermute | solution.py:24
  44.4 23.2 %collective-permute-start.7 = (bf16[2,4,64,512]{3,2,1,0:T(8,128)(2,1)S(1)}, bf16[2,4,64,512]{3,2,1,0:T(8,128)(2,1)S(1)}, u32[]{:S(2)}, u32[]{:S(2)}) collective-permute-start(bf16[2,4,64,512]{3,2,1,0:T(8,128)(2,1)S(1)} %pad_maximum_fusion.refs_0_), channel_id=1, source_target_pairs={{0,16},{4,20},{8,24},{12,28},{16,0},{20,4},{24,8},{28,12},{1,17},{... | collective-permute-start | bytes 1572872 | tf_op jit(solution)/shard_map/ppermute | solution.py:24
  44.8 23.1 %collective-permute-start.6 = (bf16[2,4,64,512]{3,2,1,0:T(8,128)(2,1)S(1)}, bf16[2,4,64,512]{3,2,1,0:T(8,128)(2,1)}, u32[]{:S(2)}, u32[]{:S(2)}) collective-permute-start(bf16[2,4,64,512]{3,2,1,0:T(8,128)(2,1)S(1)} %pad_maximum_fusion.refs_0_), channel_id=1, source_target_pairs={{0,8},{4,12},{8,0},{12,4},{16,24},{20,28},{24,16},{28,20},{1,9},{5... | collective-permute-start | bytes 1572872 | tf_op jit(solution)/shard_map/ppermute | solution.py:24
  46.7 21.4 %collective-permute-start.21 = (bf16[512,512]{1,0:T(8,128)(2,1)S(1)}, bf16[512,512]{1,0:T(8,128)(2,1)S(1)}, u32[]{:S(2)}, u32[]{:S(2)}) collective-permute-start(bf16[512,512]{1,0:T(8,128)(2,1)S(1)} %broadcast_select_fusion.2.refs_8_.refs_9_.refs_7_), channel_id=1, source_target_pairs={{0,4},{4,0},{8,12},{12,8},{16,20},{20,16},{24,28},{28,24},{1,5},{5... | collective-permute-start | bytes 1572872 | tf_op jit(solution)/shard_map/ppermute | solution.py:24
  53.8 38.8 %collective-permute-start.27 = (bf16[512,512]{1,0:T(8,128)(2,1)}, bf16[512,512]{1,0:T(8,128)(2,1)S(1)}, u32[]{:S(2)}, u32[]{:S(2)}) collective-permute-start(bf16[512,512]{1,0:T(8,128)(2,1)} %param.35), channel_id=1, source_target_pairs={{1,4},{3,6},{4,1},{6,3},{9,12},{11,14},{12,9},{14,11},{17,20},{19,... | collective-permute-start | bytes 1572872 | tf_op jit(solution)/shard_map/ppermute | solution.py:42
  56.7 30.2 %collective-permute-start.9 = (bf16[2,4,64,512]{3,2,1,0:T(8,128)(2,1)S(1)}, bf16[2,4,64,512]{3,2,1,0:T(8,128)(2,1)S(1)}, u32[]{:S(2)}, u32[]{:S(2)}) collective-permute-start(bf16[2,4,64,512]{3,2,1,0:T(8,128)(2,1)S(1)} %pad_maximum_fusion.refs_0_), channel_id=1, source_target_pairs={{0,4},{4,0},{8,12},{12,8},{16,20},{20,16},{24,28},{28,24},{1,5},{5... | collective-permute-start | bytes 1572872 | tf_op jit(solution)/shard_map/ppermute | solution.py:24
  67.6 19.3 %collective-permute-start.12 = (bf16[2,4,64,512]{3,2,1,0:T(8,128)(2,1)S(1)}, bf16[2,4,64,512]{3,2,1,0:T(8,128)(2,1)S(1)}, u32[]{:S(2)}, u32[]{:S(2)}) collective-permute-start(bf16[2,4,64,512]{3,2,1,0:T(8,128)(2,1)S(1)} %collective-permute-done.8.refs_3_), channel_id=1, source_target_pairs={{0,4},{4,0},{8,12},{12,8},{16,20},{20,16},{24,28},{28,24},{1,5},{5... | collective-permute-start | bytes 1572872 | tf_op jit(solution)/shard_map/ppermute | solution.py:24
  68.0 18.9 %collective-permute-start.11 = (bf16[2,4,64,512]{3,2,1,0:T(8,128)(2,1)S(1)}, bf16[2,4,64,512]{3,2,1,0:T(8,128)(2,1)S(1)}, u32[]{:S(2)}, u32[]{:S(2)}) collective-permute-start(bf16[2,4,64,512]{3,2,1,0:T(8,128)(2,1)S(1)} %collective-permute-done.7.refs_2_), channel_id=1, source_target_pairs={{0,4},{4,0},{8,12},{12,8},{16,20},{20,16},{24,28},{28,24},{1,5},{5... | collective-permute-start | bytes 1572872 | tf_op jit(solution)/shard_map/ppermute | solution.py:24
  68.2 18.7 %collective-permute-start.10 = (bf16[2,4,64,512]{3,2,1,0:T(8,128)(2,1)}, bf16[2,4,64,512]{3,2,1,0:T(8,128)(2,1)S(1)}, u32[]{:S(2)}, u32[]{:S(2)}) collective-permute-start(bf16[2,4,64,512]{3,2,1,0:T(8,128)(2,1)} %collective-permute-done.6.refs_1_), channel_id=1, source_target_pairs={{0,4},{4,0},{8,12},{12,8},{16,20},{20,16},{24,28},{28,24},{1,5},{5... | collective-permute-start | bytes 1572872 | tf_op jit(solution)/shard_map/ppermute | solution.py:24
  139.2 36.8 %collective-permute-start.26 = (bf16[512,512]{1,0:T(8,128)(2,1)S(1)}, bf16[512,512]{1,0:T(8,128)(2,1)S(1)}, u32[]{:S(2)}, u32[]{:S(2)}) collective-permute-start(bf16[512,512]{1,0:T(8,128)(2,1)S(1)} %get-tuple-element.100), channel_id=1, source_target_pairs={{1,4},{3,6},{4,1},{6,3},{9,12},{11,14},{12,9},{14,11},{17,20},{19,... | collective-permute-start | bytes 1572872 | tf_op jit(solution)/shard_map/ppermute | solution.py:42
  161.4 47.6 %collective-permute-start.32 = (bf16[4,4,64,512]{3,2,1,0:T(8,128)(2,1)S(1)}, bf16[4,4,64,512]{3,2,1,0:T(8,128)(2,1)S(1)}, u32[]{:S(2)}, u32[]{:S(2)}) collective-permute-start(bf16[4,4,64,512]{3,2,1,0:T(8,128)(2,1)S(1)} %get-tuple-element.153), channel_id=1, source_target_pairs={{0,4},{4,0},{8,12},{12,8},{16,20},{20,16},{24,28},{28,24},{1,5},{5... | collective-permute-start | bytes 3145736 | tf_op jit(solution)/shard_map/ppermute | solution.py:24
  172.4 31.7 %collective-permute-start.46 = (bf16[4,160,512]{2,1,0:T(8,128)(2,1)S(1)}, bf16[4,160,512]{2,1,0:T(8,128)(2,1)S(1)}, u32[]{:S(2)}, u32[]{:S(2)}) collective-permute-start(bf16[4,160,512]{2,1,0:T(8,128)(2,1)S(1)} %get-tuple-element.160), channel_id=1, source_target_pairs={{0,8},{4,12},{8,0},{12,4},{16,24},{20,28},{24,16},{28,20},{1,9},{5... | collective-permute-start | bytes 1966088 | tf_op jit(solution)/shard_map/ppermute | solution.py:24
  172.7 31.5 %collective-permute-start.47 = (bf16[4,160,512]{2,1,0:T(8,128)(2,1)S(1)}, bf16[4,160,512]{2,1,0:T(8,128)(2,1)S(1)}, u32[]{:S(2)}, u32[]{:S(2)}) collective-permute-start(bf16[4,160,512]{2,1,0:T(8,128)(2,1)S(1)} %get-tuple-element.161), channel_id=1, source_target_pairs={{0,16},{4,20},{8,24},{12,28},{16,0},{20,4},{24,8},{28,12},{1,17},{... | collective-permute-start | bytes 1966088 | tf_op jit(solution)/shard_map/ppermute | solution.py:24
  173.9 30.2 %collective-permute-start.48 = (bf16[4,160,512]{2,1,0:T(8,128)(2,1)S(1)}, bf16[4,160,512]{2,1,0:T(8,128)(2,1)S(1)}, u32[]{:S(2)}, u32[]{:S(2)}) collective-permute-start(bf16[4,160,512]{2,1,0:T(8,128)(2,1)S(1)} %get-tuple-element.162), channel_id=1, source_target_pairs={{0,24},{4,28},{8,16},{12,20},{16,8},{20,12},{24,0},{28,4},{1,25},{... | collective-permute-start | bytes 1966088 | tf_op jit(solution)/shard_map/ppermute | solution.py:24
  188.4 22.2 %collective-permute-start.30 = (bf16[512,512]{1,0:T(8,128)(2,1)S(1)}, bf16[512,512]{1,0:T(8,128)(2,1)S(1)}, u32[]{:S(2)}, u32[]{:S(2)}) collective-permute-start(bf16[512,512]{1,0:T(8,128)(2,1)S(1)} %get-tuple-element.145), channel_id=1, source_target_pairs={{0,4},{4,0},{8,12},{12,8},{16,20},{20,16},{24,28},{28,24},{1,5},{5... | collective-permute-start | bytes 1572872 | tf_op jit(solution)/shard_map/ppermute | solution.py:24
  209.0 13.3 %collective-permute-start.50 = (bf16[160,512]{1,0:T(8,128)(2,1)S(1)}, bf16[160,512]{1,0:T(8,128)(2,1)S(1)}, u32[]{:S(2)}, u32[]{:S(2)}) collective-permute-start(bf16[160,512]{1,0:T(8,128)(2,1)S(1)} %get-tuple-element.175), channel_id=1, source_target_pairs={{0,2},{1,3},{2,0},{3,1},{4,6},{5,7},{6,4},{7,5},{8,10},{9,11},{10,... | collective-permute-start | bytes 491528 | tf_op jit(solution)/shard_map/ppermute | solution.py:29
  209.3 16.1 %collective-permute-start.35 = (bf16[4,64,512]{2,1,0:T(8,128)(2,1)S(1)}, bf16[4,64,512]{2,1,0:T(8,128)(2,1)S(1)}, u32[]{:S(2)}, u32[]{:S(2)}) collective-permute-start(bf16[4,64,512]{2,1,0:T(8,128)(2,1)S(1)} %get-tuple-element.177), channel_id=1, source_target_pairs={{0,24},{4,28},{8,16},{12,20},{16,8},{20,12},{24,0},{28,4},{1,25},{... | collective-permute-start | bytes 786440 | tf_op jit(solution)/shard_map/ppermute | solution.py:24
  210.6 14.8 %collective-permute-start.34 = (bf16[4,64,512]{2,1,0:T(8,128)(2,1)S(1)}, bf16[4,64,512]{2,1,0:T(8,128)(2,1)S(1)}, u32[]{:S(2)}, u32[]{:S(2)}) collective-permute-start(bf16[4,64,512]{2,1,0:T(8,128)(2,1)S(1)} %get-tuple-element.178), channel_id=1, source_target_pairs={{0,16},{4,20},{8,24},{12,28},{16,0},{20,4},{24,8},{28,12},{1,17},{... | collective-permute-start | bytes 786440 | tf_op jit(solution)/shard_map/ppermute | solution.py:24
  211.8 14.0 %collective-permute-start.33 = (bf16[4,64,512]{2,1,0:T(8,128)(2,1)S(1)}, bf16[4,64,512]{2,1,0:T(8,128)(2,1)S(1)}, u32[]{:S(2)}, u32[]{:S(2)}) collective-permute-start(bf16[4,64,512]{2,1,0:T(8,128)(2,1)S(1)} %get-tuple-element.179), channel_id=1, source_target_pairs={{0,8},{4,12},{8,0},{12,4},{16,24},{20,28},{24,16},{28,20},{1,9},{5... | collective-permute-start | bytes 786440 | tf_op jit(solution)/shard_map/ppermute | solution.py:24
  216.9 25.0 %collective-permute-start.31 = (bf16[512,512]{1,0:T(8,128)(2,1)S(1)}, bf16[512,512]{1,0:T(8,128)(2,1)S(1)}, u32[]{:S(2)}, u32[]{:S(2)}) collective-permute-start(bf16[512,512]{1,0:T(8,128)(2,1)S(1)} %add_convert_fusion.4), channel_id=1, source_target_pairs={{1,4},{3,6},{4,1},{6,3},{9,12},{11,14},{12,9},{14,11},{17,20},{19,... | collective-permute-start | bytes 1572872 | tf_op jit(solution)/shard_map/ppermute | solution.py:42
  (76 other events, 632.8 us)

commit v3 on v2

v3 whole, which is shorter than its diff:
```python
import functools
import math

import jax
import jax.numpy as jnp
from jax import lax
from jax.experimental import pallas as pl
from jax.experimental.pallas import tpu as pltpu
from jax.sharding import PartitionSpec as P

HEAD_DIM = 64
LEN = 1024
EPS = 1e-05
LANES = 128
LOW = jnp.bfloat16
F32 = jnp.float32
EXP2_SCALE = math.log2(math.e) / math.sqrt(HEAD_DIM)
INV_SCALE = 1.0 / math.sqrt(HEAD_DIM)
BARRED = -1e9


def swap_dp(value, bits):
    count = lax.axis_size("dp")
    return lax.ppermute(value, "dp", [(i, i ^ bits) for i in range(count)])


def swap_tensor(value, step):
    count = lax.axis_size("tensor")
    return lax.ppermute(value, "tensor", [(i, i ^ step) for i in range(count)])


def regroup(block):
    dp, tensor = lax.axis_size("dp"), lax.axis_size("tensor")
    pairs = [
        ((2 * k + c) * tensor + 2 * a + b, (2 * k + b) * tensor + 2 * a + c)
        for k in range(dp // 2)
        for c in range(2)
        for a in range(tensor // 2)
        for b in range(2)
        if b != c
    ]
    moved = lax.ppermute(block, ("dp", "tensor"), pairs)
    stays = (lax.axis_index("dp") % 2) == (lax.axis_index("tensor") % 2)
    return jnp.where(stays, block, moved)


def join_shards(piece):
    pieces = jnp.stack((piece, swap_tensor(piece, 2)))
    other = swap_tensor(pieces, 1)
    return jnp.stack((pieces[0], other[0], pieces[1], other[1]))


def spread_plane(block):
    return [block] + [swap_dp(block, bits) for bits in (2, 4, 6)]


def spread(block):
    own = spread_plane(block)
    return own + [swap_dp(block, 1) for block in own]


def sum_parts(parts):
    total = parts[0].astype(F32)
    for part in parts[1:]:
        total = total + part.astype(F32)
    return total


def pair_halves(keep, send):
    other = swap_dp(send, 1)

    def pair(first, second, shards):
        return jnp.stack([sum_parts((keep[i, shards], other[i, shards])).astype(LOW) for i in (first, second)])

    near, far = slice(0, 2), slice(2, 4)
    return pair(0, 2, near), pair(1, 3, near), pair(0, 1, far), pair(2, 3, far)


def add_halves(kept, got):
    return [sum_parts((kept[i], got[i])).astype(LOW) for i in range(2)]


def add_shards(near, near_got, far, far_got):
    return [sum_parts((a[j], b[j])).astype(LOW) for a, b in ((near, near_got), (far, far_got)) for j in range(2)]


def reduce_shards(parts):
    total = sum_parts([parts[0]] + [swap_tensor(parts[j], j) for j in (1, 2, 3)])
    bits = 8
    while bits < lax.axis_size("dp"):
        total = total + swap_dp(total.astype(LOW), bits).astype(F32)
        bits *= 2
    return total.astype(LOW)


def flip(value, axis, wanted):
    return jnp.where(wanted, jnp.flip(value, axis), value)


def relative_blocks(blocks):
    dp = lax.axis_index("dp")
    return flip(flip(flip(blocks, 3, (dp & 1) != 0), 2, (dp & 2) != 0), 1, (dp & 4) != 0)


def dot_nt(a, b):
    return lax.dot_general(a, b, (((1,), (1,)), ((), ())), preferred_element_type=F32)


def dot_tn(a, b):
    return lax.dot_general(a, b, (((0,), (0,)), ((), ())), preferred_element_type=F32)


def dot_nn(a, b):
    return jnp.dot(a, b, preferred_element_type=F32)


def norm(value):
    center = value - jnp.mean(value, -1, keepdims=True)
    scale = lax.rsqrt(jnp.mean(center * center, -1, keepdims=True) + EPS)
    return center * scale, scale


def norm_back(grad, gain, unit, scale):
    scaled = grad * gain
    mean_a = jnp.mean(scaled, -1, keepdims=True)
    mean_b = jnp.mean(scaled * unit, -1, keepdims=True)
    return (scaled - mean_a - unit * mean_b) * scale


def lane_half(which):
    first = lax.broadcasted_iota(jnp.int32, (1, LANES), 1) < HEAD_DIM
    return first if which == 0 else jnp.logical_not(first)


VMEM_LIMIT = 10


def call(kernel, name, micros, outs, scratch, *operands, scalars=0, far=0, vmem=VMEM_LIMIT):
    spaces = [pltpu.SMEM] * scalars + [pl.ANY] * far + [pltpu.VMEM] * (len(operands) - scalars - far)
    return pl.pallas_call(
        kernel,
        in_specs=[pl.BlockSpec(memory_space=space) for space in spaces],
        out_specs=[pl.BlockSpec(memory_space=pltpu.VMEM)] * len(outs),
        out_shape=[jax.ShapeDtypeStruct(shape, dtype) for shape, dtype in outs],
        scratch_shapes=[pltpu.VMEM(*s) if isinstance(s, tuple) else s for s in scratch],
        compiler_params=pltpu.CompilerParams(vmem_limit_bytes=vmem * 2**20),
        cost_estimate=pl.CostEstimate(flops=int(micros * 1.1e9), bytes_accessed=0, transcendentals=0),
        name=name,
    )(*operands)


def attention_first_kernel(*refs):
    blocks, rest, w_out, scratch, sems = refs[:8], refs[8:-4], refs[-4], refs[-3:-1], refs[-1]
    copies = []
    for at, block in enumerate(blocks):
        c, i = divmod(at, 4)
        rows = block.shape[1] // 4
        for kind in range(4):
            source = block.at[:, kind * rows : (kind + 1) * rows]
            copies.append(pltpu.make_async_copy(source, w_out.at[kind, :, 2 * i + c], sems.at[at, kind]))
    for copy in copies:
        copy.start()
    for copy in copies:
        copy.wait()
    attention_forward_kernel(*rest[:5], w_out, *rest[5:], *scratch)


def attention_forward_kernel(
    in_ref, low_ref, other_ref, mark_ref, barred_ref, w_ref, qb, vb, ob, gain, shift,
    q_out, k_out, v_out, e_out, inv_out, o_out, att_out, unit_out, scale_out, mid_out, kmask, vmask,
):
    rows = in_ref.shape[0]
    wq, wk, wv, wo = (w_ref[kind].reshape(-1, w_ref.shape[-1]) for kind in range(4))
    heads = wq.shape[0] // HEAD_DIM
    zero = jnp.zeros((), LOW)
    low = low_ref[...]
    q_out[...] = (dot_nt(low, wq) + qb[...]).astype(LOW)
    for half, part in enumerate((low, other_ref[...])):
        r = slice(half * rows, (half + 1) * rows)
        k_out[r] = dot_nt(part, wk).astype(LOW)
        v_out[r] = (dot_nt(part, wv) + vb[...]).astype(LOW)
    mark = mark_ref[...]
    first = lane_half(0)
    for p in range(heads // 2):
        cols = slice(p * LANES, (p + 1) * LANES)
        keys, values = k_out[:, cols], v_out[:, cols]
        scaled = q_out[:, cols].astype(F32) * EXP2_SCALE
        high = scaled.astype(LOW)
        rest = (scaled - high.astype(F32)).astype(LOW)
        mixed = []
        for h in range(2):
            keep = lane_half(h)
            query = jnp.concatenate((jnp.where(keep, high, mark), jnp.where(keep, rest, zero)), 1)
            slot = (2 * p + h) % 4
            kmask[slot, :, :LANES] = jnp.where(keep, keys, barred_ref[...])
            kmask[slot, :, LANES:] = jnp.where(keep, keys, zero)
            vmask[slot] = jnp.where(keep, values, jnp.ones((), LOW))
            scores = dot_nt(query, kmask[slot])
            exponent = jnp.exp2(scores - jnp.max(scores, -1, keepdims=True)).astype(LOW)
            e_out[2 * p + h] = exponent
            mixed.append(dot_nn(exponent, vmask[slot]))
        inv = 1.0 / pltpu.roll(jnp.where(first, mixed[1], mixed[0]), HEAD_DIM, 1)
        attended = jnp.where(first, mixed[0], mixed[1]) * inv
        inv_out[:, cols] = inv
        o_out[:, cols] = attended
        att_out[:, cols] = attended.astype(LOW)
    unit, scale = norm(in_ref[...].astype(F32) + dot_nn(att_out[...], wo) + ob[...])
    unit_out[...] = unit
    scale_out[...] = jnp.broadcast_to(scale, scale_out.shape)
    mid_out[...] = unit * gain[...] + shift[...]


def attention_forward(layer_in, low, other, mark, barred, w, blocks=None):
    rows, width = layer_in.shape
    units = w["qb"].shape[1]
    heads = units // HEAD_DIM
    outs = [
        ((rows, units), LOW), ((2 * rows, units), LOW), ((2 * rows, units), LOW), ((heads, rows, 2 * rows), LOW),
        ((rows, units), F32), ((rows, units), F32), ((rows, units), LOW), ((rows, width), F32), ((rows, LANES), F32),
        ((rows, width), F32),
    ]
    scratch = [((4, 2 * rows, 2 * LANES), LOW), ((4, 2 * rows, LANES), LOW)]
    tail = (w["qb"], w["vb"], w["ob"], w["g1"], w["s1"])
    first = (layer_in, low, other, mark, barred)
    if blocks is None:
        return call(attention_forward_kernel, "attention_forward", 8, outs, scratch, *first, w["heads"], *tail)
    scratch.append(pltpu.SemaphoreType.DMA((8, 4)))
    outs.append(((4, 4, 8, units // 32, width), LOW))
    return call(attention_first_kernel, "attention_first", 9, outs, scratch, *blocks, *first, *tail, far=8)


GELU_A = math.sqrt(2.0 / math.pi)
GELU_B = 0.044715


def ffn_first_kernel(*refs):
    blocks, rest, w_out, sems = refs[:8], refs[8:-2], refs[-2], refs[-1]
    copies = []
    for at, block in enumerate(blocks):
        rows = block.shape[1] // 2
        for kind in range(2):
            source = block.at[:, kind * rows : (kind + 1) * rows]
            copies.append(pltpu.make_async_copy(source, w_out.at[kind, at], sems.at[at, kind]))
    for copy in copies:
        copy.start()
    for copy in copies:
        copy.wait()
    ffn_forward_kernel(rest[0], w_out, *rest[1:])


def unit_blocks(w_ref):
    count = w_ref.shape[2] * w_ref.shape[3] * 2
    for at in range(4):
        up, down = (w_ref[kind, 2 * at : 2 * at + 2].reshape(count, -1) for kind in range(2))
        yield slice(at * count, (at + 1) * count), up, down


def ffn_forward_kernel(
    mid_ref, w_ref, upb, db, gain, shift, low_out, act_out, slope_out, unit_out, scale_out, out_out, next_out
):
    middle = mid_ref[...]
    low = middle.astype(LOW)
    low_out[...] = low
    total = middle + db[...]
    for r, up, down in unit_blocks(w_ref):
        hidden = dot_nt(low, up) + upb[:, r]
        square = hidden * hidden
        bent = jnp.tanh(hidden * (GELU_A + GELU_A * GELU_B * square))
        half = 0.5 + 0.5 * bent
        active = (hidden * half).astype(LOW)
        act_out[:, r] = active
        inner = GELU_A + 3.0 * GELU_A * GELU_B * square
        slope_out[:, r] = (half + 0.5 * hidden * (1.0 - bent * bent) * inner).astype(LOW)
        total = total + dot_nn(active, down)
    unit, scale = norm(total)
    unit_out[...] = unit
    scale_out[...] = jnp.broadcast_to(scale, scale_out.shape)
    layer_out = unit * gain[...] + shift[...]
    out_out[...] = layer_out
    next_out[...] = layer_out.astype(LOW)


def ffn_forward(middle, w, blocks=None):
    rows, width = middle.shape
    units = w["upb"].shape[1]
    outs = [
        ((rows, width), LOW), ((rows, units), LOW), ((rows, units), LOW), ((rows, width), F32), ((rows, LANES), F32),
        ((rows, width), F32), ((rows, width), LOW),
    ]
    tail = (w["upb"], w["db"], w["g2"], w["s2"])
    if blocks is None:
        return call(ffn_forward_kernel, "ffn_forward", 5, outs, [], middle, w["ffn"], *tail)
    outs.append(((2, 8, 4, units // 32, width), LOW))
    scratch = [pltpu.SemaphoreType.DMA((8, 2))]
    return call(ffn_first_kernel, "ffn_first", 6, outs, scratch, *blocks, middle, *tail, far=8)


def row_sum(value):
    return jnp.sum(value, 0, keepdims=True)


def ffn_backward_kernel(
    w_ref, grad_ref, unit_two, scale_two, slope, unit_one, scale_one, heads_ref, gain_two, gain_one,
    branch_two_out, hidden_out, pre_one_out, branch_one_out, att_out, sums_out,
):
    grad = grad_ref[...].astype(F32)
    unit = unit_two[...]
    sums_out[0:1] = row_sum(grad * unit)
    sums_out[1:2] = row_sum(grad)
    grad_pre = norm_back(grad, gain_two[...], unit, scale_two[:, :1])
    branch = grad_pre.astype(LOW)
    branch_two_out[...] = branch
    sums_out[2:3] = row_sum(branch.astype(F32))
    grad_middle = grad_pre
    for r, up, down in unit_blocks(w_ref):
        hidden = (dot_nt(branch, down) * slope[:, r].astype(F32)).astype(LOW)
        hidden_out[:, r] = hidden
        grad_middle = grad_middle + dot_nn(hidden, up)
    unit = unit_one[...]
    sums_out[3:4] = row_sum(grad_middle * unit)
    sums_out[4:5] = row_sum(grad_middle)
    grad_pre = norm_back(grad_middle, gain_one[...], unit, scale_one[:, :1])
    pre_one_out[...] = grad_pre
    branch = grad_pre.astype(LOW)
    branch_one_out[...] = branch
    sums_out[5:6] = row_sum(branch.astype(F32))
    sums_out[6:8] = jnp.zeros((2, grad.shape[1]), F32)
    att_out[...] = dot_nt(branch, heads_ref[3].reshape(-1, grad.shape[1])).astype(LOW)


def ffn_backward(grad_out, kept_ffn, kept_attention, w):
    rows, width = grad_out.shape
    units = w["upb"].shape[1]
    outs = [
        ((rows, width), LOW), ((rows, units), LOW), ((rows, width), F32), ((rows, width), LOW),
        ((rows, w["qb"].shape[1]), LOW), ((8, width), F32),
    ]
    return call(
        ffn_backward_kernel, "ffn_backward", 5, outs, [], w["ffn"],
        grad_out, kept_ffn["unit"], kept_ffn["scale"], kept_ffn["slope"], kept_attention["unit"], kept_attention["scale"],
        w["heads"], w["g2"], w["g1"],
    )


def attention_backward_kernel(
    att_ref, pre_ref, q_ref, k_ref, v_ref, e_ref, inv_ref, o_ref, w_ref,
    in_out, sent_out, dq_out, dk_out, dv_out, vmask,
):
    wq, wk, wv = (w_ref[kind].reshape(-1, w_ref.shape[-1]) for kind in range(3))
    rows = att_ref.shape[0]
    heads = wq.shape[0] // HEAD_DIM
    zero = jnp.zeros((), LOW)
    first = lane_half(0)
    spare = lax.broadcasted_iota(jnp.int32, (1, LANES), 1) % HEAD_DIM
    minus = jnp.where(spare < 3, -1.0, 0.0).astype(LOW)
    for p in range(heads // 2):
        cols = slice(p * LANES, (p + 1) * LANES)
        queries, keys, values = q_ref[:, cols], k_ref[:, cols], v_ref[:, cols]
        grad = (att_ref[:, cols].astype(F32) * inv_ref[:, cols]).astype(LOW)
        dots = grad.astype(F32) * o_ref[:, cols]
        dq, dk, dv = [], [], []
        for h in range(2):
            keep = lane_half(h)
            dot = jnp.sum(jnp.where(keep, dots, 0.0), -1, keepdims=True)
            top = dot.astype(LOW)
            left = dot - top.astype(F32)
            mid = left.astype(LOW)
            end = (left - mid.astype(F32)).astype(LOW)
            pieces = jnp.where(spare == 0, top, jnp.where(spare == 1, mid, jnp.where(spare == 2, end, zero)))
            exponent = e_ref[2 * p + h]
            slot = (2 * p + h) % 4
            vmask[slot] = jnp.where(keep, values, minus)
            centered = dot_nt(jnp.where(keep, grad, pieces), vmask[slot])
            grad_scores = (exponent.astype(F32) * centered).astype(LOW)
            dq.append(dot_nn(grad_scores, keys))
            dk.append(dot_tn(grad_scores, queries))
            dv.append(dot_tn(exponent, grad))
        dq_out[:, cols] = (jnp.where(first, dq[0], dq[1]) * INV_SCALE).astype(LOW)
        dk_out[:, cols] = (jnp.where(first, dk[0], dk[1]) * INV_SCALE).astype(LOW)
        dv_out[:, cols] = jnp.where(first, dv[0], dv[1]).astype(LOW)
    dq, dk, dv = dq_out[...], dk_out[...], dv_out[...]
    sent_out[...] = (dot_nn(dk[rows:], wk) + dot_nn(dv[rows:], wv)).astype(LOW)
    in_out[...] = pre_ref[...] + dot_nn(dq, wq) + dot_nn(dk[:rows], wk) + dot_nn(dv[:rows], wv)


def attention_backward(grad_att, grad_pre, kept, w):
    rows, width = grad_pre.shape
    units = w["qb"].shape[1]
    heads = units // HEAD_DIM
    outs = [
        ((rows, width), F32), ((rows, width), LOW), ((rows, units), LOW), ((2 * rows, units), LOW), ((2 * rows, units), LOW),
    ]
    return call(
        attention_backward_kernel, "attention_backward", 12, outs,
        [((4, 2 * rows, LANES), LOW)],
        grad_att, grad_pre, kept["q"], kept["k"], kept["v"], kept["e"], kept["inv"], kept["o"], w["heads"],
    )


def both_layers(firsts, seconds):
    return sum(dot_tn(a[...], b[...]) for a, b in zip(firsts, seconds))


def ffn_grads_kernel(*refs):
    actives, branches, hiddens, middles, attendeds, ones_branches = (refs[2 * i : 2 * i + 2] for i in range(6))
    outs = refs[12:]
    rows, units = actives[0].shape
    step = units // 8
    ur = step // 4
    hr = attendeds[0].shape[1] // 32
    one = jnp.ones((rows, LANES), LOW)
    out_grad = both_layers(attendeds, ones_branches).astype(LOW)
    for at in range(8):
        c, i = divmod(at, 4)
        out = outs[c].at[i]
        cols = slice(at * step, (at + 1) * step)
        down = both_layers([a.at[:, cols] for a in actives], branches).astype(LOW)
        up = both_layers([h.at[:, cols] for h in hiddens], middles).astype(LOW)
        bias = sum(dot_tn(h[:, cols], one) for h in hiddens).astype(LOW)
        for j in range(4):
            out[j, :ur] = down[j * ur : (j + 1) * ur]
            out[j, ur : 2 * ur] = up[j * ur : (j + 1) * ur]
            head = j * LANES + (2 * i + c) * hr
            out[j, 2 * ur : 2 * ur + hr] = out_grad[head : head + hr]
            for g in range(4):
                first = j * ur + g * (ur // 4)
                out[j, 2 * ur + hr :, g * LANES : (g + 1) * LANES] = bias[first : first + ur // 4]


def ffn_grads(pairs):
    rows, units = pairs[0][0].shape
    width = pairs[1][0].shape[1]
    ur, hr = units // 32, pairs[4][0].shape[1] // 32
    out = ((4, 4, 2 * ur + hr + ur // 4, width), LOW)
    return call(ffn_grads_kernel, "ffn_grads", 7, [out, out], [], *[v for pair in pairs for v in pair])


def head_grads_kernel(eighth_ref, *refs):
    dqs, dks, dvs, lows, others, sums = (refs[2 * i : 2 * i + 2] for i in range(6))
    *outs, shared = refs[12:]
    shared[...] = sums[0][...] + sums[1][...]
    upper = lax.broadcasted_iota(jnp.int32, (16, 1), 0) < 8
    rows, units = dqs[0].shape
    hr = units // 32
    one = jnp.ones((rows, LANES), LOW)

    def halves(grads):
        own = [g.at[:rows] for g in grads]
        return own, [g.at[rows:] for g in grads]

    dk_own, dk_other = halves(dks)
    dv_own, dv_other = halves(dvs)
    grads = [
        both_layers(dqs, lows),
        both_layers(dk_own + dk_other, lows + others),
        both_layers(dv_own + dv_other, lows + others),
    ]
    grads = [g.astype(LOW) for g in grads]
    biases = [sum(dot_tn(g[...], one) for g in part).astype(LOW) for part in (dqs, dv_own + dv_other)]
    for at in range(8):
        c, i = divmod(at, 4)
        line = shared[pl.ds(eighth_ref[0] ^ (2 * i + c), 1)]
        line = jnp.where(upper, line[:, : 2 * LANES], line[:, 2 * LANES :]).astype(LOW)
        for j in range(4):
            out = outs[c].at[i, j]
            first = j * LANES + (2 * i + c) * hr
            for kind in range(3):
                out[kind * hr : (kind + 1) * hr] = grads[kind][first : first + hr]
            for kind in range(2):
                out[3 * hr :, kind * LANES : (kind + 1) * LANES] = biases[kind][first : first + hr]
            out[3 * hr :, 2 * LANES :] = line


def head_grads(pairs, eighth):
    units = pairs[0][0].shape[1]
    width = pairs[3][0].shape[1]
    out = ((4, 4, 4 * (units // 32), width), LOW)
    return call(head_grads_kernel, "head_grads", 5, [out, out], [((8, width), F32)], eighth, *[v for pair in pairs for v in pair], scalars=1)


def first_row(column):
    return column.T[:1]


def finish_kernel(ur, hr, eighth_ref, *refs):
    blocks, (down_out, up_out, out_out, up_bias) = refs[:8], refs[8:12]
    outs, biases, shared, (up_all, up_bias_all, *scratch) = refs[12:15], refs[15:17], refs[17], refs[18:]
    head = 2 * ur + hr + ur // 4
    for at, block in enumerate(blocks):
        c, i = divmod(at, 4)
        slot = eighth_ref[0] ^ (2 * i + c)
        units = pl.ds(pl.multiple_of(slot * ur, ur), ur)
        down_out[units] = block[:ur].astype(F32)
        up_all[units] = block[ur : 2 * ur].astype(F32)
        out_out[pl.ds(pl.multiple_of(slot * hr, hr), hr)] = block[2 * ur : 2 * ur + hr].astype(F32)
        for g in range(4):
            some = pl.ds(pl.multiple_of(slot * ur + g * (ur // 4), ur // 4), ur // 4)
            up_bias_all[some] = block[2 * ur + hr : head, g * LANES : (g + 1) * LANES].astype(F32)
        units = pl.ds(pl.multiple_of(slot * hr, hr), hr)
        for kind in range(3):
            scratch[kind][units] = block[head + kind * hr : head + (kind + 1) * hr].astype(F32)
        for kind in range(2):
            scratch[3 + kind][units] = block[head + 3 * hr :, kind * LANES : (kind + 1) * LANES].astype(F32)
        line = block[head + 3 * hr :, 2 * LANES :].astype(F32)
        shared[pl.ds(slot, 1)] = jnp.concatenate((line[:1], line[8:9]), 1)
    up_out[...] = up_all[...].T
    up_bias[...] = first_row(up_bias_all[...])
    for kind in range(3):
        outs[kind][...] = scratch[kind][...].T
    for kind in range(2):
        biases[kind][...] = first_row(scratch[3 + kind][...])


def finish(own, ur, hr, eighth):
    blocks = spread(own)
    width = own.shape[1]
    outs = [((8 * ur, width), F32), ((width, 8 * ur), F32), ((8 * hr, width), F32), ((1, 8 * ur), F32)]
    outs += [((width, 8 * hr), F32)] * 3 + [((1, 8 * hr), F32)] * 2 + [((8, width), F32)]
    scratch = [((8 * ur, width), F32), ((8 * ur, LANES), F32)]
    scratch += [((8 * hr, width), F32)] * 3 + [((8 * hr, LANES), F32)] * 2
    return call(functools.partial(finish_kernel, ur, hr), "finish", 3, outs, scratch, eighth, *blocks, scalars=1)


def per_device(
    inputs, segment_ids, query_weight, query_bias, key_weight, value_weight, value_bias, out_weight, out_bias,
    first_gain, first_shift, up_weight, up_bias, down_weight, down_bias, second_gain, second_shift, cotangent,
):
    rows, width = inputs.shape
    dp, tensor = lax.axis_index("dp"), lax.axis_index("tensor")
    core, eighth = dp % 2, dp % 8
    shard_heads, shard_units = query_weight.shape[1], up_weight.shape[1]
    hr, ur = shard_heads // 8, shard_units // 8

    def columns(weight, count):
        return lax.dynamic_slice_in_dim(weight, eighth * count, count, 1).T

    def own_rows(weight, count):
        return lax.dynamic_slice_in_dim(weight, eighth * count, count, 0)

    first_in = regroup(inputs)
    flat = jnp.concatenate((query_bias, value_bias, up_bias))
    top = lax.reduce_precision(flat, 8, 7)
    mid = lax.reduce_precision(flat - top, 8, 7)
    flat = jnp.concatenate((top, mid, flat - top - mid)).astype(LOW)
    count = flat.shape[0]
    flat = jnp.pad(flat, (0, -count % (16 * width))).reshape(-1, width)
    heads_piece = jnp.concatenate(
        [columns(v, hr) for v in (query_weight, key_weight, value_weight)] + [own_rows(out_weight, hr), flat]
    )
    ffn_piece = jnp.concatenate((columns(up_weight, ur), own_rows(down_weight, ur)))
    shards = jnp.stack([heads_piece] + [swap_tensor(heads_piece, step) for step in (1, 2, 3)])
    heads_own = spread_plane(shards[:, : 4 * hr])
    ffn_own = spread_plane(join_shards(ffn_piece))
    heads_own = lax.optimization_barrier(heads_own)
    head_blocks = heads_own + [swap_dp(block, 1) for block in heads_own]
    flat = shards[:, 4 * hr :].reshape(4, -1)[:, :count].astype(F32)
    flat = jnp.sum(flat.reshape(4, 3, -1), 1)
    seq = lax.dynamic_slice_in_dim(segment_ids, (tensor // 2) * LEN, LEN)
    seq = jnp.where(core == tensor % 2, seq, swap_dp(seq, 1))
    labels_own = lax.dynamic_slice_in_dim(seq, core * rows, rows)
    labels_all = jnp.concatenate((labels_own, lax.dynamic_slice_in_dim(seq, (1 - core) * rows, rows)))
    code = jnp.arange(LANES) % HEAD_DIM - 1
    mark = (labels_own[:, None] == code).astype(LOW)
    barred = jnp.where(labels_all[:, None] == code, 0.0, BARRED).astype(LOW)

    def bias(start, count):
        return relative_blocks(flat[:, start : start + count].reshape(4, 2, 2, 2, -1))

    w = {
        "qb": bias(0, shard_heads).reshape(1, -1), "vb": bias(shard_heads, shard_heads).reshape(1, -1),
        "upb": bias(2 * shard_heads, shard_units).reshape(4, 4, 2, ur).transpose(2, 1, 0, 3).reshape(1, -1),
        "ob": out_bias[None], "g1": first_gain[None], "s1": first_shift[None], "db": down_bias[None],
        "g2": second_gain[None], "s2": second_shift[None],
    }

    kept = []
    layer_in, low = first_in, first_in
    for position in range(2):
        other = swap_dp(low, 1)
        made = attention_forward(layer_in, low, other, mark, barred, w, None if position else head_blocks)
        q, k, v, e, inv, o, attended, unit_one, scale_one, middle = made[:10]
        if position == 0:
            w["heads"] = made[10]
            middle, cotangent, *ffn_own = lax.optimization_barrier((middle, cotangent, *ffn_own))
            ffn_blocks = ffn_own + [swap_dp(block, 1) for block in ffn_own]
        made = ffn_forward(middle, w, None if position else ffn_blocks)
        middle_low, active, slope, unit_two, scale_two, layer_out, next_low = made[:7]
        if position == 0:
            w["ffn"] = made[7]
        attention = {"q": q, "k": k, "v": v, "e": e, "inv": inv, "o": o, "unit": unit_one, "scale": scale_one}
        ffn = {"slope": slope, "unit": unit_two, "scale": scale_two}
        kept.append((attention, ffn, low, other, attended, middle_low, active))
        layer_in, low = layer_out, next_low
    result = regroup(low)

    grad_flow = regroup(cotangent)
    ffn_pairs, head_pairs = [], []
    for position in (1, 0):
        attention, ffn, low, other, attended, middle_low, active = kept[position]
        branch_two, grad_hidden, grad_pre, branch_one, grad_att, six = ffn_backward(grad_flow, ffn, attention, w)
        ffn_pairs.append((active, branch_two, grad_hidden, middle_low, attended, branch_one))
        if position == 0:
            near, near_sent, far, far_sent = pair_halves(*ffn_grads(list(zip(*ffn_pairs))))
            grad_att, near_sent, far_sent = lax.optimization_barrier((grad_att, near_sent, far_sent))
            near_got, far_got = swap_dp(near_sent, 2), swap_dp(far_sent, 4)
        grad_in, sent, dq, dk, dv = attention_backward(grad_att, grad_pre, attention, w)
        if position == 1:
            grad_in, result = lax.optimization_barrier((grad_in, result))
        if position == 0:
            dq, sent, near_got, far_got = lax.optimization_barrier((dq, sent, near_got, far_got))
            (near, near_sent), (far, far_sent) = add_halves(near, near_got), add_halves(far, far_got)
            dq, near_sent, far_sent = lax.optimization_barrier((dq, near_sent, far_sent))
            near_got, far_got = swap_dp(near_sent, 4), swap_dp(far_sent, 2)
        grad_flow = grad_in + swap_dp(sent, 1).astype(F32)
        head_pairs.append((dq, dk, dv, low, other, six))
    at = jnp.reshape(eighth, (1,)).astype(jnp.int32)
    keep, send = head_grads(list(zip(*head_pairs)), at)
    near_got, far_got, keep, send = lax.optimization_barrier((near_got, far_got, keep, send))
    ffn_parts = add_shards(near, near_got, far, far_got)
    near, near_sent, far, far_sent = pair_halves(keep, send)
    near_got, far_got = swap_dp(near_sent, 2), swap_dp(far_sent, 4)
    ffn_own = reduce_shards(ffn_parts)
    (near, near_sent), (far, far_sent) = add_halves(near, near_got), add_halves(far, far_got)
    near_got, far_got = swap_dp(near_sent, 4), swap_dp(far_sent, 2)
    head_own = reduce_shards(add_shards(near, near_got, far, far_got))
    own = jnp.concatenate((ffn_own, head_own))
    own, grad_low = lax.optimization_barrier((own, grad_flow.astype(LOW)))
    input_grad = regroup(grad_low).astype(F32)
    (
        down_grad, up_grad, out_grad, up_bias_grad, q_grad, k_grad, v_grad, q_bias_grad, v_bias_grad, shared,
    ) = finish(own, ur, hr, at)
    return (
        result, input_grad, q_grad, q_bias_grad[0], k_grad, v_grad, v_bias_grad[0], out_grad, shared[5], shared[3], shared[4],
        up_grad, up_bias_grad[0], down_grad, shared[2], shared[0], shared[1],
    )


def solution(mesh):
    split = P(("dp", "tensor"), None)
    columns, rows, part = P(None, "tensor"), P("tensor", None), P("tensor")
    return jax.shard_map(
        per_device,
        mesh=mesh,
        in_specs=(
            split, P("dp"), columns, part, columns, columns, part, rows, P(), P(), P(), columns, part, rows, P(), P(),
            P(), split,
        ),
        out_specs=(
            split, split, columns, part, columns, columns, part, rows, P(), P(), P(), columns, part, rows, P(), P(), P(),
        ),
        check_vma=False,
    )
```

time: 255 us -> 229 us (0.90)
  starting transfers between devices: 92.3 us -> 64 us
  Pallas kernels: 74.6 us -> 84 us
  waiting for transfers between devices: 51.7 us -> 42.8 us
    ppermute x44 -> x36, starting transfers between devices: 58.4 us -> 35.2 us  [swap_dp(): return lax.ppermute(value, 'dp', [(i, i ^ bits) for i in range(count)])]
    ppermute x4, waiting for transfers between devices: 0.01 us -> 11.1 us  [regroup(): moved = lax.ppermute(block, ('dp', 'tensor'), pairs)]
    ppermute x16 -> x11, waiting for transfers between devices: 16.6 us -> 6.3 us  [swap_tensor(): return lax.ppermute(value, 'tensor', [(i, i ^ step) for i in range(count)])]
    ppermute x44 -> x36, waiting for transfers between devices: 35.1 us -> 25.4 us  [swap_dp(): return lax.ppermute(value, 'dp', [(i, i ^ bits) for i in range(count)])]
    pallas_call x12 -> x11, Pallas kernels: 74.6 us -> 84 us  [call(): pl.pallas_call(kernel, in_specs=[pl.BlockSpec(memory_space=space) for spa...]
    unnamed x78 -> x97, local copies, waits for them, and re-layouts: 13.5 us -> 20.3 us
    reshape x8, local copies, waits for them, and re-layouts: 4.69 us -> 0.56 us  [the longest x3 0.27 us: bias(): return relative_blocks(flat[:, start:start + count].reshape(4, 2, 2, 2, -1))]
    ppermute x16 -> x11, starting transfers between devices: 20.7 us -> 17.8 us  [swap_tensor(): return lax.ppermute(value, 'tensor', [(i, i ^ step) for i in range(count)])]
  transfers between devices with their start and end apart: 64 -> 51, of which waited for: 17 -> 18; matrix products, arithmetic and copies ran while one was open for 6% -> 3% of each run, Pallas kernels for 12% -> 22%
where the time goes in v3:
time: 229 us; the launch traced here: 225 us
  Pallas kernels  84 us (37%)
  starting transfers between devices  64 us (28%)
  waiting for transfers between devices  42.8 us (19%)
  local copies, waits for them, and re-layouts  26.9 us (12%)
  other arithmetic  5.51 us (2%)
    pallas_call x11, Pallas kernels, call(): pl.pallas_call(kernel, in_specs=[pl.BlockSpec(memory_space=space) for spa...  84 us
    ppermute x36, starting transfers between devices, swap_dp(): return lax.ppermute(value, 'dp', [(i, i ^ bits) for i in range(count)])  35.2 us
    ppermute x36, waiting for transfers between devices, swap_dp(): return lax.ppermute(value, 'dp', [(i, i ^ bits) for i in range(count)])  25.4 us
    unnamed x97, local copies, waits for them, and re-layouts  20.3 us
    ppermute x11, starting transfers between devices, swap_tensor(): return lax.ppermute(value, 'tensor', [(i, i ^ step) for i in range(count)])  17.8 us
    ppermute x4, waiting for transfers between devices, regroup(): moved = lax.ppermute(block, ('dp', 'tensor'), pairs)  11.1 us
    ppermute x4, starting transfers between devices, regroup(): moved = lax.ppermute(block, ('dp', 'tensor'), pairs)  11 us
    ppermute x11, waiting for transfers between devices, swap_tensor(): return lax.ppermute(value, 'tensor', [(i, i ^ step) for i in range(count)])  6.3 us
  transfers between devices with their start and end apart: 51, of which 18 were waited for; matrix products, arithmetic and copies ran while one was open for 3% of the time, Pallas kernels for 22%

profile of v3, /device:TPU:1, one launch (start us, length us, event | category | flops | bytes accessed | tf_op | source)
XLA Modules:
  0.0 225.0 jit_solution(9551824385923088112)
XLA Ops:
  6.0 4.2 %collective-permute-start.2 = (bf16[80,512]{1,0:T(8,128)(2,1)S(1)}, bf16[80,512]{1,0:T(8,128)(2,1)S(1)}, u32[]{:S(2)}, u32[]{:S(2)}) collective-permute-start(bf16[80,512]{1,0:T(8,128)(2,1)S(1)} %constant_dynamic-update-slice_fusion.1), channel_id=1, source_target_pairs={{0,3},{1,2},{2,1},{3,0},{4,7},{5,6},{6,5},{7,4},{8,11},{9,10},{10,... | collective-permute-start | bytes 245768 | tf_op jit(solution)/shard_map/ppermute | solution.py:29
  15.7 3.8 %collective-permute-start.10 = (bf16[512,512]{1,0:T(8,128)(2,1)}, bf16[512,512]{1,0:T(8,128)(2,1)S(1)}, u32[]{:S(2)}, u32[]{:S(2)}) collective-permute-start(bf16[512,512]{1,0:T(8,128)(2,1)} %param.18), channel_id=1, source_target_pairs={{1,4},{3,6},{4,1},{6,3},{9,12},{11,14},{12,9},{14,11},{17,20},{19,... | collective-permute-start | bytes 1572872 | tf_op jit(solution)/shard_map/ppermute | solution.py:42
  24.3 6.1 %collective-permute-done.10 = bf16[512,512]{1,0:T(8,128)(2,1)S(1)} collective-permute-done((bf16[512,512]{1,0:T(8,128)(2,1)}, bf16[512,512]{1,0:T(8,128)(2,1)S(1)}, u32[]{:S(2)}, u32[]{:S(2)}) %collective-permute-start.10) | collective-permute-done | bytes 524320 | tf_op jit(solution)/shard_map/ppermute | solution.py:42
  31.3 2.6 %collective-permute-done.4.refs_2_ = bf16[4,64,512]{2,1,0:T(8,128)(2,1)} collective-permute-done((bf16[4,64,512]{2,1,0:T(8,128)(2,1)S(1)}, bf16[4,64,512]{2,1,0:T(8,128)(2,1)}, u32[]{:S(2)}, u32[]{:S(2)}) %collective-permute-start.4) | collective-permute-done | bytes 262176 | tf_op jit(solution)/shard_map/ppermute | solution.py:24
  39.8 10.0 %attention_first.1 = (bf16[512,512]{1,0:T(8,128)(2,1)S(1)}, bf16[1024,512]{1,0:T(8,128)(2,1)S(1)}, bf16[1024,512]{1,0:T(8,128)(2,1)S(1)}, bf16[8,512,1024]{2,1,0...) custom-call(bf16[4,64,512]{2,1,0:T(8,128)(2,1)S(1)} %slice.288.refs_, ...), custom_call_target="tpu_custom_call" | custom-call | flops 9900000256 | tf_op jit(solution)/shard_map/attention_first/pallas_call | solution.py:140
  52.0 3.3 %copy-done.18 = bf16[8,512,1024]{2,1,0:T(8,128)(2,1)} copy-done((bf16[8,512,1024]{2,1,0:T(8,128)(2,1)}, bf16[8,512,1024]{2,1,0:T(8,128)(2,1)S(1)}, u32[]{:S(2)}) %copy-start.18) | copy-done | bytes 8388632
  71.1 6.6 %ffn_first.1 = (bf16[512,512]{1,0:T(8,128)(2,1)S(1)}, bf16[512,2048]{1,0:T(8,128)(2,1)S(1)}, bf16[512,2048]{1,0:T(8,128)(2,1)S(1)}, f32[512,512]{1,0:T(8,128)S(1...) custom-call(bf16[4,128,512]{2,1,0:T(8,128)(2,1)S(1)} %pad_maximum_fu, ...), custom_call_target="tpu_custom_call" | custom-call | flops 6600000000 | tf_op jit(solution)/shard_map/ffn_first/pallas_call | solution.py:140
  79.7 8.4 %attention_forward.1 = (bf16[512,512]{1,0:T(8,128)(2,1)S(1)}, bf16[1024,512]{1,0:T(8,128)(2,1)S(1)}, bf16[1024,512]{1,0:T(8,128)(2,1)S(1)}, bf16[8,512,1024]{2,1...) custom-call(f32[512,512]{1,0:T(8,128)S(1)} %get-tuple-element.128.in, ...), custom_call_target="tpu_custom_call" | custom-call | flops 8800000000 | tf_op jit(solution)/shard_map/attention_forward/pallas_call | solution.py:140
  88.2 16.3 %ffn_forward.1 = (bf16[512,512]{1,0:T(8,128)(2,1)S(1)}, bf16[512,2048]{1,0:T(8,128)(2,1)S(1)}, bf16[512,2048]{1,0:T(8,128)(2,1)S(1)}, f32[512,512]{1,0:T(8,128)S...) custom-call(f32[512,512]{1,0:T(8,128)S(1)} %get-tuple-element.131.mid_ref, ...), custom_call_target="tpu_custom_call" | custom-call | flops 5500000256 | tf_op jit(solution)/shard_map/ffn_forward/pallas_call | solution.py:140
  106.9 3.6 %ffn_backward.2 = (bf16[512,512]{1,0:T(8,128)(2,1)S(1)}, bf16[512,2048]{1,0:T(8,128)(2,1)S(1)}, f32[512,512]{1,0:T(8,128)S(1)}, bf16[512,512]{1,0:T(8,128)(2,1)S...) custom-call(bf16[2,8,4,64,512]{4,3,2,1,0:T(8,128)(2,1)S(1)} %get-tuple-element.126.w_ref, ...), custom_call_target="tpu_custom_call" | custom-call | flops 5500000256 | tf_op jit(solution)/shard_map/ffn_backward/pallas_call | solution.py:140
  110.5 11.7 %attention_backward.2 = (f32[512,512]{1,0:T(8,128)S(1)}, bf16[512,512]{1,0:T(8,128)(2,1)S(1)}, bf16[512,512]{1,0:T(8,128)(2,1)S(1)}, bf16[1024,512]{1,0:T(8,128)(2,1)S(1)}, bf16[1024,512]{1,0:T(8,128)(2,1)S(1)}) custom-call(bf16[512,512]{1,0:T(8,128)(2,1)S(1)} %get-tuple-element.137.att_ref, f32[512,512]{1,0:T(8,128)S(1)} %get-tuple-element.138.pre_ref, ...), custom_call_target="tpu_custom_call" | custom-call | flops 13200000000 | tf_op jit(solution)/shard_map/attention_backward/pallas_call | solution.py:140
  124.4 3.6 %ffn_backward.3 = (bf16[512,512]{1,0:T(8,128)(2,1)S(1)}, bf16[512,2048]{1,0:T(8,128)(2,1)S(1)}, f32[512,512]{1,0:T(8,128)S(1)}, bf16[512,512]{1,0:T(8,128)(2,1)S...) custom-call(bf16[2,8,4,64,512]{4,3,2,1,0:T(8,128)(2,1)S(1)} %get-tuple-element.126.w_ref, ...), custom_call_target="tpu_custom_call" | custom-call | flops 5500000256 | tf_op jit(solution)/shard_map/ffn_backward/pallas_call | solution.py:140
  128.0 6.2 %ffn_grads.1 = (bf16[4,4,160,512]{3,2,1,0:T(8,128)(2,1)S(1)}, bf16[4,4,160,512]{3,2,1,0:T(8,128)(2,1)S(1)}) custom-call(bf16[512,2048]{1,0:T(8,128)(2,1)S(1)} %get-tuple-element.148.refs_0_, bf16[512,2048]{1,0:T(8,128)(2,1)S(1)} %get-tuple-element.149.refs_1_, bf16[512,512]{1,0:T(8,128)(2,1)S(1)} %get-tuple-element.150.refs_2_, ...), custom_call_target="tpu_custom_call" | custom-call | flops 7699999744 | tf_op jit(solution)/shard_map/ffn_grads/pallas_call | solution.py:140
  134.4 4.8 %collective-permute-done.26 = bf16[4,4,160,512]{3,2,1,0:T(8,128)(2,1)S(1)} collective-permute-done((bf16[4,4,160,512]{3,2,1,0:T(8,128)(2,1)S(1)}, bf16[4,4,160,512]{3,2,1,0:T(8,128)(2,1)S(1)}, u32[]{:S(2)}, u32[]{:S(2)}) %collective-permute-start.26) | collective-permute-done | bytes 2621472 | tf_op jit(solution)/shard_map/ppermute | solution.py:24
  141.7 11.4 %attention_backward.3 = (f32[512,512]{1,0:T(8,128)S(1)}, bf16[512,512]{1,0:T(8,128)(2,1)S(1)}, bf16[512,512]{1,0:T(8,128)(2,1)S(1)}, bf16[1024,512]{1,0:T(8,128)(2,1)S(1)}, bf16[1024,512]{1,0:T(8,128)(2,1)S(1)}) custom-call(bf16[512,512]{1,0:T(8,128)(2,1)S(1)} %get-tuple-element.170.att_ref, f32[512,512]{1,0:T(8,128)S(1)} %get-tuple-element.171.pre_ref, ...), custom_call_target="tpu_custom_call" | custom-call | flops 13200000000 | tf_op jit(solution)/shard_map/attention_backward/pallas_call | solution.py:140
  153.1 2.9 %collective-permute-done.27 = bf16[2,2,160,512]{3,2,1,0:T(8,128)(2,1)S(1)} collective-permute-done((bf16[2,2,160,512]{3,2,1,0:T(8,128)(2,1)S(1)}, bf16[2,2,160,512]{3,2,1,0:T(8,128)(2,1)S(1)}, u32[]{:S(2)}, u32[]{:S(2)}) %collective-permute-start.27) | collective-permute-done | bytes 655392 | tf_op jit(solution)/shard_map/ppermute | solution.py:24
  158.8 4.0 %head_grads.1 = (bf16[4,4,64,512]{3,2,1,0:T(8,128)(2,1)S(1)}, bf16[4,4,64,512]{3,2,1,0:T(8,128)(2,1)S(1)}) custom-call(s32[1]{0:T(128)} %bitcast.22.eighth_ref, bf16[512,512]{1,0:T(8,128)(2,1)S(1)} %get-tuple-element.187.refs_0_, bf16[512,512]{1,0:T(8,128)(2,1)S(1)} %get-tuple-element.188.refs_1_, bf16[1024,512]{1,0:T(8,128)(2,1)S(1)} %get-tuple-element.189.refs_2_, ...), custom_call_target="tpu_custom_call" | custom-call | flops 5500000256 | tf_op jit(solution)/shard_map/head_grads/pallas_call | solution.py:140
  175.2 3.0 %collective-permute-done.35 = bf16[2,2,64,512]{3,2,1,0:T(8,128)(2,1)S(1)} collective-permute-done((bf16[2,2,64,512]{3,2,1,0:T(8,128)(2,1)S(1)}, bf16[2,2,64,512]{3,2,1,0:T(8,128)(2,1)S(1)}, u32[]{:S(2)}, u32[]{:S(2)}) %collective-permute-start.35) | collective-permute-done | bytes 262176 | tf_op jit(solution)/shard_map/ppermute | solution.py:24
  180.6 3.6 %collective-permute-done.33 = bf16[160,512]{1,0:T(8,128)(2,1)S(1)} collective-permute-done((bf16[160,512]{1,0:T(8,128)(2,1)S(1)}, bf16[160,512]{1,0:T(8,128)(2,1)S(1)}, u32[]{:S(2)}, u32[]{:S(2)}) %collective-permute-start.33) | collective-permute-done | bytes 163872 | tf_op jit(solution)/shard_map/ppermute | solution.py:29
  188.4 4.8 %collective-permute-start.37 = (bf16[64,512]{1,0:T(8,128)(2,1)S(1)}, bf16[64,512]{1,0:T(8,128)(2,1)S(1)}, u32[]{:S(2)}, u32[]{:S(2)}) collective-permute-start(bf16[64,512]{1,0:T(8,128)(2,1)S(1)} %fusion.23), channel_id=1, source_target_pairs={{0,1},{1,0},{2,3},{3,2},{4,5},{5,4},{6,7},{7,6},{8,9},{9,8},{10,11... | collective-permute-start | bytes 196616 | tf_op jit(solution)/shard_map/ppermute | solution.py:29
  196.1 2.6 %collective-permute-done.40 = bf16[64,512]{1,0:T(8,128)(2,1)S(1)} collective-permute-done((bf16[64,512]{1,0:T(8,128)(2,1)S(1)}, bf16[64,512]{1,0:T(8,128)(2,1)S(1)}, u32[]{:S(2)}, u32[]{:S(2)}) %collective-permute-start.40) | collective-permute-done | bytes 65568 | tf_op jit(solution)/shard_map/ppermute | solution.py:29
  201.8 5.2 %collective-permute-start.47 = (bf16[224,512]{1,0:T(8,128)(2,1)S(1)}, bf16[224,512]{1,0:T(8,128)(2,1)S(1)}, u32[]{:S(2)}, u32[]{:S(2)}) collective-permute-start(bf16[224,512]{1,0:T(8,128)(2,1)S(1)} %pad_maximum_fusion.7.refs_0_), channel_id=1, source_target_pairs={{0,4},{4,0},{8,12},{12,8},{16,20},{20,16},{24,28},{28,24},{1,5},{5... | collective-permute-start | bytes 688136 | tf_op jit(solution)/shard_map/ppermute | solution.py:24
  207.0 3.7 %collective-permute-start.50 = (bf16[224,512]{1,0:T(8,128)(2,1)S(1)}, bf16[224,512]{1,0:T(8,128)(2,1)S(1)}, u32[]{:S(2)}, u32[]{:S(2)}) collective-permute-start(bf16[224,512]{1,0:T(8,128)(2,1)S(1)} %collective-permute-done.46.refs_3_), channel_id=1, source_target_pairs={{0,4},{4,0},{8,12},{12,8},{16,20},{20,16},{24,28},{28,24},{1,5},{5... | collective-permute-start | bytes 688136 | tf_op jit(solution)/shard_map/ppermute | solution.py:24
  218.8 5.0 %collective-permute-done.43 = bf16[512,512]{1,0:T(8,128)(2,1)S(1)} collective-permute-done((bf16[512,512]{1,0:T(8,128)(2,1)S(1)}, bf16[512,512]{1,0:T(8,128)(2,1)S(1)}, u32[]{:S(2)}, u32[]{:S(2)}) %collective-permute-start.43) | collective-permute-done | bytes 524320 | tf_op jit(solution)/shard_map/ppermute | solution.py:42
  (257 shorter events, 85.8 us)
Async XLA Ops:
  6.0 14.0 %collective-permute-start.2 = (bf16[80,512]{1,0:T(8,128)(2,1)S(1)}, bf16[80,512]{1,0:T(8,128)(2,1)S(1)}, u32[]{:S(2)}, u32[]{:S(2)}) collective-permute-start(bf16[80,512]{1,0:T(8,128)(2,1)S(1)} %constant_dynamic-update-slice_fusion.1), channel_id=1, source_target_pairs={{0,3},{1,2},{2,1},{3,0},{4,7},{5,6},{6,5},{7,4},{8,11},{9,10},{10,... | collective-permute-start | bytes 245768 | tf_op jit(solution)/shard_map/ppermute | solution.py:29
  10.2 9.8 %collective-permute-start.1 = (bf16[80,512]{1,0:T(8,128)(2,1)S(1)}, bf16[80,512]{1,0:T(8,128)(2,1)S(1)}, u32[]{:S(2)}, u32[]{:S(2)}) collective-permute-start(bf16[80,512]{1,0:T(8,128)(2,1)S(1)} %constant_dynamic-update-slice_fusion.1), channel_id=1, source_target_pairs={{0,2},{1,3},{2,0},{3,1},{4,6},{5,7},{6,4},{7,5},{8,10},{9,11},{10,... | collective-permute-start | bytes 245768 | tf_op jit(solution)/shard_map/ppermute | solution.py:29
  10.2 9.8 %collective-permute-start = (bf16[80,512]{1,0:T(8,128)(2,1)S(1)}, bf16[80,512]{1,0:T(8,128)(2,1)S(1)}, u32[]{:S(2)}, u32[]{:S(2)}) collective-permute-start(bf16[80,512]{1,0:T(8,128)(2,1)S(1)} %constant_dynamic-update-slice_fusion.1), channel_id=1, source_target_pairs={{0,1},{1,0},{2,3},{3,2},{4,5},{5,4},{6,7},{7,6},{8,9},{9,8},{10,11... | collective-permute-start | bytes 245768 | tf_op jit(solution)/shard_map/ppermute | solution.py:29
  13.6 10.0 %collective-permute-start.13 = (bf16[128,512]{1,0:T(8,128)(2,1)S(1)}, bf16[128,512]{1,0:T(8,128)(2,1)S(1)}, u32[]{:S(2)}, u32[]{:S(2)}) collective-permute-start(bf16[128,512]{1,0:T(8,128)(2,1)S(1)} %get-tuple-element.240), channel_id=1, source_target_pairs={{0,2},{1,3},{2,0},{3,1},{4,6},{5,7},{6,4},{7,5},{8,10},{9,11},{10,... | collective-permute-start | bytes 393224 | tf_op jit(solution)/shard_map/ppermute | solution.py:29
  15.7 14.7 %collective-permute-start.10 = (bf16[512,512]{1,0:T(8,128)(2,1)}, bf16[512,512]{1,0:T(8,128)(2,1)S(1)}, u32[]{:S(2)}, u32[]{:S(2)}) collective-permute-start(bf16[512,512]{1,0:T(8,128)(2,1)} %param.18), channel_id=1, source_target_pairs={{1,4},{3,6},{4,1},{6,3},{9,12},{11,14},{12,9},{14,11},{17,20},{19,... | collective-permute-start | bytes 1572872 | tf_op jit(solution)/shard_map/ppermute | solution.py:42
  20.3 11.0 %collective-permute-start.5 = (bf16[4,64,512]{2,1,0:T(8,128)(2,1)S(1)}, bf16[4,64,512]{2,1,0:T(8,128)(2,1)S(1)}, u32[]{:S(2)}, u32[]{:S(2)}) collective-permute-start(bf16[4,64,512]{2,1,0:T(8,128)(2,1)S(1)} %slice.288.refs_0_), channel_id=1, source_target_pairs={{0,24},{4,28},{8,16},{12,20},{16,8},{20,12},{24,0},{28,4},{1,25},{... | collective-permute-start | bytes 786440 | tf_op jit(solution)/shard_map/ppermute | solution.py:24
  22.5 11.4 %collective-permute-start.4 = (bf16[4,64,512]{2,1,0:T(8,128)(2,1)S(1)}, bf16[4,64,512]{2,1,0:T(8,128)(2,1)}, u32[]{:S(2)}, u32[]{:S(2)}) collective-permute-start(bf16[4,64,512]{2,1,0:T(8,128)(2,1)S(1)} %slice.288.refs_0_), channel_id=1, source_target_pairs={{0,16},{4,20},{8,24},{12,28},{16,0},{20,4},{24,8},{28,12},{1,17},{... | collective-permute-start | bytes 786440 | tf_op jit(solution)/shard_map/ppermute | solution.py:24
  22.7 11.2 %collective-permute-start.3 = (bf16[4,64,512]{2,1,0:T(8,128)(2,1)S(1)}, bf16[4,64,512]{2,1,0:T(8,128)(2,1)S(1)}, u32[]{:S(2)}, u32[]{:S(2)}) collective-permute-start(bf16[4,64,512]{2,1,0:T(8,128)(2,1)S(1)} %slice.288.refs_0_), channel_id=1, source_target_pairs={{0,8},{4,12},{8,0},{12,4},{16,24},{20,28},{24,16},{28,20},{1,9},{5... | collective-permute-start | bytes 786440 | tf_op jit(solution)/shard_map/ppermute | solution.py:24
  24.3 10.6 %collective-permute-start.14 = (bf16[2,128,512]{2,1,0:T(8,128)(2,1)}, bf16[2,128,512]{2,1,0:T(8,128)(2,1)S(1)}, u32[]{:S(2)}, u32[]{:S(2)}) collective-permute-start(bf16[2,128,512]{2,1,0:T(8,128)(2,1)} %pad_maximum_fusion.4), channel_id=1, source_target_pairs={{0,1},{1,0},{2,3},{3,2},{4,5},{5,4},{6,7},{7,6},{8,9},{9,8},{10,11... | collective-permute-start | bytes 786440 | tf_op jit(solution)/shard_map/ppermute | solution.py:29
  35.5 27.1 %collective-permute-start.17 = (bf16[4,128,512]{2,1,0:T(8,128)(2,1)S(1)}, bf16[4,128,512]{2,1,0:T(8,128)(2,1)S(1)}, u32[]{:S(2)}, u32[]{:S(2)}) collective-permute-start(bf16[4,128,512]{2,1,0:T(8,128)(2,1)S(1)} %pad_maximum_fusion.2.refs_0_), channel_id=1, source_target_pairs={{0,24},{4,28},{8,16},{12,20},{16,8},{20,12},{24,0},{28,4},{1,25},{... | collective-permute-start | bytes 1572872 | tf_op jit(solution)/shard_map/ppermute | solution.py:24
  37.2 25.4 %collective-permute-start.16 = (bf16[4,128,512]{2,1,0:T(8,128)(2,1)S(1)}, bf16[4,128,512]{2,1,0:T(8,128)(2,1)S(1)}, u32[]{:S(2)}, u32[]{:S(2)}) collective-permute-start(bf16[4,128,512]{2,1,0:T(8,128)(2,1)S(1)} %pad_maximum_fusion.2.refs_0_), channel_id=1, source_target_pairs={{0,16},{4,20},{8,24},{12,28},{16,0},{20,4},{24,8},{28,12},{1,17},{... | collective-permute-start | bytes 1572872 | tf_op jit(solution)/shard_map/ppermute | solution.py:24
  37.8 24.9 %collective-permute-start.15 = (bf16[4,128,512]{2,1,0:T(8,128)(2,1)S(1)}, bf16[4,128,512]{2,1,0:T(8,128)(2,1)}, u32[]{:S(2)}, u32[]{:S(2)}) collective-permute-start(bf16[4,128,512]{2,1,0:T(8,128)(2,1)S(1)} %pad_maximum_fusion.2.refs_0_), channel_id=1, source_target_pairs={{0,8},{4,12},{8,0},{12,4},{16,24},{20,28},{24,16},{28,20},{1,9},{5... | collective-permute-start | bytes 1572872 | tf_op jit(solution)/shard_map/ppermute | solution.py:24
  64.6 13.5 %collective-permute-start.22 = (bf16[512,512]{1,0:T(8,128)(2,1)}, bf16[512,512]{1,0:T(8,128)(2,1)S(1)}, u32[]{:S(2)}, u32[]{:S(2)}) collective-permute-start(bf16[512,512]{1,0:T(8,128)(2,1)} %param.35), channel_id=1, source_target_pairs={{1,4},{3,6},{4,1},{6,3},{9,12},{11,14},{12,9},{14,11},{17,20},{19,... | collective-permute-start | bytes 1572872 | tf_op jit(solution)/shard_map/ppermute | solution.py:42
  104.5 17.8 %collective-permute-start.24 = (bf16[512,512]{1,0:T(8,128)(2,1)S(1)}, bf16[512,512]{1,0:T(8,128)(2,1)S(1)}, u32[]{:S(2)}, u32[]{:S(2)}) collective-permute-start(bf16[512,512]{1,0:T(8,128)(2,1)S(1)} %get-tuple-element.146), channel_id=1, source_target_pairs={{1,4},{3,6},{4,1},{6,3},{9,12},{11,14},{12,9},{14,11},{17,20},{19,... | collective-permute-start | bytes 1572872 | tf_op jit(solution)/shard_map/ppermute | solution.py:42
  139.7 16.3 %collective-permute-start.27 = (bf16[2,2,160,512]{3,2,1,0:T(8,128)(2,1)S(1)}, bf16[2,2,160,512]{3,2,1,0:T(8,128)(2,1)S(1)}, u32[]{:S(2)}, u32[]{:S(2)}) collective-permute-start(bf16[2,2,160,512]{3,2,1,0:T(8,128)(2,1)S(1)} %pad_maximum_fusion), channel_id=1, source_target_pairs={{0,8},{4,12},{8,0},{12,4},{16,24},{20,28},{24,16},{28,20},{1,9},{5... | collective-permute-start | bytes 1966088 | tf_op jit(solution)/shard_map/ppermute | solution.py:24
  140.8 15.9 %collective-permute-start.28 = (bf16[2,2,160,512]{3,2,1,0:T(8,128)(2,1)S(1)}, bf16[2,2,160,512]{3,2,1,0:T(8,128)(2,1)S(1)}, u32[]{:S(2)}, u32[]{:S(2)}) collective-permute-start(bf16[2,2,160,512]{3,2,1,0:T(8,128)(2,1)S(1)} %pad_maximum_fusion.1), channel_id=1, source_target_pairs={{0,16},{4,20},{8,24},{12,28},{16,0},{20,4},{24,8},{28,12},{1,17},{... | collective-permute-start | bytes 1966088 | tf_op jit(solution)/shard_map/ppermute | solution.py:24
  171.4 9.2 %collective-permute-start.31 = (bf16[160,512]{1,0:T(8,128)(2,1)S(1)}, bf16[160,512]{1,0:T(8,128)(2,1)S(1)}, u32[]{:S(2)}, u32[]{:S(2)}) collective-permute-start(bf16[160,512]{1,0:T(8,128)(2,1)S(1)} %fusion.10), channel_id=1, source_target_pairs={{0,1},{1,0},{2,3},{3,2},{4,5},{5,4},{6,7},{7,6},{8,9},{9,8},{10,11... | collective-permute-start | bytes 491528 | tf_op jit(solution)/shard_map/ppermute | solution.py:29
  173.0 11.3 %collective-permute-start.33 = (bf16[160,512]{1,0:T(8,128)(2,1)S(1)}, bf16[160,512]{1,0:T(8,128)(2,1)S(1)}, u32[]{:S(2)}, u32[]{:S(2)}) collective-permute-start(bf16[160,512]{1,0:T(8,128)(2,1)S(1)} %get-tuple-element.234), channel_id=1, source_target_pairs={{0,3},{1,2},{2,1},{3,0},{4,7},{5,6},{6,5},{7,4},{8,11},{9,10},{10,... | collective-permute-start | bytes 491528 | tf_op jit(solution)/shard_map/ppermute | solution.py:29
  179.2 16.8 %collective-permute-start.42 = (bf16[512,512]{1,0:T(8,128)(2,1)S(1)}, bf16[512,512]{1,0:T(8,128)(2,1)S(1)}, u32[]{:S(2)}, u32[]{:S(2)}) collective-permute-start(bf16[512,512]{1,0:T(8,128)(2,1)S(1)} %get-tuple-element.202), channel_id=1, source_target_pairs={{0,4},{4,0},{8,12},{12,8},{16,20},{20,16},{24,28},{28,24},{1,5},{5... | collective-permute-start | bytes 1572872 | tf_op jit(solution)/shard_map/ppermute | solution.py:24
  201.4 9.3 %collective-permute-start.45 = (bf16[224,512]{1,0:T(8,128)(2,1)S(1)}, bf16[224,512]{1,0:T(8,128)(2,1)S(1)}, u32[]{:S(2)}, u32[]{:S(2)}) collective-permute-start(bf16[224,512]{1,0:T(8,128)(2,1)S(1)} %pad_maximum_fusion.7.refs_0_), channel_id=1, source_target_pairs={{0,16},{4,20},{8,24},{12,28},{16,0},{20,4},{24,8},{28,12},{1,17},{... | collective-permute-start | bytes 688136 | tf_op jit(solution)/shard_map/ppermute | solution.py:24
  201.4 11.7 %collective-permute-start.44 = (bf16[224,512]{1,0:T(8,128)(2,1)S(1)}, bf16[224,512]{1,0:T(8,128)(2,1)S(1)}, u32[]{:S(2)}, u32[]{:S(2)}) collective-permute-start(bf16[224,512]{1,0:T(8,128)(2,1)S(1)} %pad_maximum_fusion.7.refs_0_), channel_id=1, source_target_pairs={{0,8},{4,12},{8,0},{12,4},{16,24},{20,28},{24,16},{28,20},{1,9},{5... | collective-permute-start | bytes 688136 | tf_op jit(solution)/shard_map/ppermute | solution.py:24
  201.8 14.1 %collective-permute-start.47 = (bf16[224,512]{1,0:T(8,128)(2,1)S(1)}, bf16[224,512]{1,0:T(8,128)(2,1)S(1)}, u32[]{:S(2)}, u32[]{:S(2)}) collective-permute-start(bf16[224,512]{1,0:T(8,128)(2,1)S(1)} %pad_maximum_fusion.7.refs_0_), channel_id=1, source_target_pairs={{0,4},{4,0},{8,12},{12,8},{16,20},{20,16},{24,28},{28,24},{1,5},{5... | collective-permute-start | bytes 688136 | tf_op jit(solution)/shard_map/ppermute | solution.py:24
  207.0 8.9 %collective-permute-start.50 = (bf16[224,512]{1,0:T(8,128)(2,1)S(1)}, bf16[224,512]{1,0:T(8,128)(2,1)S(1)}, u32[]{:S(2)}, u32[]{:S(2)}) collective-permute-start(bf16[224,512]{1,0:T(8,128)(2,1)S(1)} %collective-permute-done.46.refs_3_), channel_id=1, source_target_pairs={{0,4},{4,0},{8,12},{12,8},{16,20},{20,16},{24,28},{28,24},{1,5},{5... | collective-permute-start | bytes 688136 | tf_op jit(solution)/shard_map/ppermute | solution.py:24
  213.3 10.5 %collective-permute-start.43 = (bf16[512,512]{1,0:T(8,128)(2,1)S(1)}, bf16[512,512]{1,0:T(8,128)(2,1)S(1)}, u32[]{:S(2)}, u32[]{:S(2)}) collective-permute-start(bf16[512,512]{1,0:T(8,128)(2,1)S(1)} %add_convert_fusion), channel_id=1, source_target_pairs={{1,4},{3,6},{4,1},{6,3},{9,12},{11,14},{12,9},{14,11},{17,20},{19,... | collective-permute-start | bytes 1572872 | tf_op jit(solution)/shard_map/ppermute | solution.py:42
  (70 other events, 421.1 us)

commit v4 on v3

--- a/solution.py
+++ b/solution.py
@@ -66,9 +66,7 @@
     return total
 
 
-def pair_halves(keep, send):
-    other = swap_dp(send, 1)
-
+def pair_halves(keep, other):
     def pair(first, second, shards):
         return jnp.stack([sum_parts((keep[i, shards], other[i, shards])).astype(LOW) for i in (first, second)])
 
@@ -84,8 +82,12 @@
     return [sum_parts((a[j], b[j])).astype(LOW) for a, b in ((near, near_got), (far, far_got)) for j in range(2)]
 
 
-def reduce_shards(parts):
-    total = sum_parts([parts[0]] + [swap_tensor(parts[j], j) for j in (1, 2, 3)])
+def swap_shards(parts):
+    return [parts[0]] + [swap_tensor(parts[j], j) for j in (1, 2, 3)]
+
+
+def sum_shards(parts):
+    total = sum_parts(parts)
     bits = 8
     while bits < lax.axis_size("dp"):
         total = total + swap_dp(total.astype(LOW), bits).astype(F32)
@@ -132,10 +134,13 @@
     return first if which == 0 else jnp.logical_not(first)
 
 
-VMEM_LIMIT = 10
-
-
-def call(kernel, name, micros, outs, scratch, *operands, scalars=0, far=0, vmem=VMEM_LIMIT):
+VMEM_MIB = {
+    "attention_first": 10, "attention_forward": 10, "ffn_first": 5, "ffn_forward": 5, "ffn_backward": 4, "ffn_grads": 3,
+    "attention_backward": 6, "last_backward": 10, "finish": 7,
+}
+
+
+def call(kernel, name, micros, outs, scratch, *operands, scalars=0, far=0):
     spaces = [pltpu.SMEM] * scalars + [pl.ANY] * far + [pltpu.VMEM] * (len(operands) - scalars - far)
     return pl.pallas_call(
         kernel,
@@ -143,7 +148,7 @@
         out_specs=[pl.BlockSpec(memory_space=pltpu.VMEM)] * len(outs),
         out_shape=[jax.ShapeDtypeStruct(shape, dtype) for shape, dtype in outs],
         scratch_shapes=[pltpu.VMEM(*s) if isinstance(s, tuple) else s for s in scratch],
-        compiler_params=pltpu.CompilerParams(vmem_limit_bytes=vmem * 2**20),
+        compiler_params=pltpu.CompilerParams(vmem_limit_bytes=VMEM_MIB[name] * 2**20),
         cost_estimate=pl.CostEstimate(flops=int(micros * 1.1e9), bytes_accessed=0, transcendentals=0),
         name=name,
     )(*operands)
@@ -401,43 +406,40 @@
     return sum(dot_tn(a[...], b[...]) for a, b in zip(firsts, seconds))
 
 
-def ffn_grads_kernel(*refs):
+def ffn_grads_kernel(c, *refs):
     actives, branches, hiddens, middles, attendeds, ones_branches = (refs[2 * i : 2 * i + 2] for i in range(6))
-    outs = refs[12:]
+    out, bias_out = refs[12:]
     rows, units = actives[0].shape
     step = units // 8
     ur = step // 4
     hr = attendeds[0].shape[1] // 32
     one = jnp.ones((rows, LANES), LOW)
     out_grad = both_layers(attendeds, ones_branches).astype(LOW)
-    for at in range(8):
-        c, i = divmod(at, 4)
-        out = outs[c].at[i]
+    for i in range(4):
+        at = 4 * c + i
         cols = slice(at * step, (at + 1) * step)
         down = both_layers([a.at[:, cols] for a in actives], branches).astype(LOW)
         up = both_layers([h.at[:, cols] for h in hiddens], middles).astype(LOW)
-        bias = sum(dot_tn(h[:, cols], one) for h in hiddens).astype(LOW)
+        bias_out[i * step : (i + 1) * step] = sum(dot_tn(h[:, cols], one) for h in hiddens).astype(LOW)
         for j in range(4):
-            out[j, :ur] = down[j * ur : (j + 1) * ur]
-            out[j, ur : 2 * ur] = up[j * ur : (j + 1) * ur]
+            out[i, j, :ur] = down[j * ur : (j + 1) * ur]
+            out[i, j, ur : 2 * ur] = up[j * ur : (j + 1) * ur]
             head = j * LANES + (2 * i + c) * hr
-            out[j, 2 * ur : 2 * ur + hr] = out_grad[head : head + hr]
-            for g in range(4):
-                first = j * ur + g * (ur // 4)
-                out[j, 2 * ur + hr :, g * LANES : (g + 1) * LANES] = bias[first : first + ur // 4]
-
-
-def ffn_grads(pairs):
+            out[i, j, 2 * ur :] = out_grad[head : head + hr]
+
+
+def ffn_grads(pairs, c):
     rows, units = pairs[0][0].shape
     width = pairs[1][0].shape[1]
     ur, hr = units // 32, pairs[4][0].shape[1] // 32
-    out = ((4, 4, 2 * ur + hr + ur // 4, width), LOW)
-    return call(ffn_grads_kernel, "ffn_grads", 7, [out, out], [], *[v for pair in pairs for v in pair])
+    outs = [((4, 4, 2 * ur + hr, width), LOW), ((units // 2, LANES), LOW)]
+    return call(functools.partial(ffn_grads_kernel, c), "ffn_grads", 3, outs, [], *[v for pair in pairs for v in pair])
 
 
 def head_grads_kernel(eighth_ref, *refs):
     dqs, dks, dvs, lows, others, sums = (refs[2 * i : 2 * i + 2] for i in range(6))
-    *outs, shared = refs[12:]
+    up_biases, (keep, send, shared) = refs[12:14], refs[14:]
+    lane = lax.broadcasted_iota(jnp.int32, (1, LANES), 1) // (LANES // 4)
     shared[...] = sums[0][...] + sums[1][...]
     upper = lax.broadcasted_iota(jnp.int32, (16, 1), 0) < 8
     rows, units = dqs[0].shape
@@ -462,20 +464,38 @@
         line = shared[pl.ds(eighth_ref[0] ^ (2 * i + c), 1)]
         line = jnp.where(upper, line[:, : 2 * LANES], line[:, 2 * LANES :]).astype(LOW)
         for j in range(4):
-            out = outs[c].at[i, j]
+            out = keep.at[i, j] if c == 0 else send.at[4 * i + j]
             first = j * LANES + (2 * i + c) * hr
             for kind in range(3):
                 out[kind * hr : (kind + 1) * hr] = grads[kind][first : first + hr]
-            for kind in range(2):
-                out[3 * hr :, kind * LANES : (kind + 1) * LANES] = biases[kind][first : first + hr]
+            q, v = (bias[first : first + hr] for bias in biases)
+            up_bias = up_biases[c]
+            first = (4 * i + j) * (up_bias.shape[0] // 16)
+            u = [up_bias[first + g * hr : first + (g + 1) * hr] for g in range(4)]
+            out[3 * hr :, :LANES] = jnp.where(lane < 1, q, jnp.where(lane < 2, v, jnp.where(lane < 3, u[0], u[1])))
+            out[3 * hr :, LANES : 2 * LANES] = jnp.where(lane < 1, u[2], u[3])
             out[3 * hr :, 2 * LANES :] = line
 
 
-def head_grads(pairs, eighth):
-    units = pairs[0][0].shape[1]
-    width = pairs[3][0].shape[1]
-    out = ((4, 4, 4 * (units // 32), width), LOW)
-    return call(head_grads_kernel, "head_grads", 5, [out, out], [((8, width), F32)], eighth, *[v for pair in pairs for v in pair], scalars=1)
+def last_backward_kernel(eighth_ref, *refs):
+    given, (dq_two, dk_two, dv_two), lows, others, sums = refs[:9], refs[9:12], refs[12:14], refs[14:16], refs[16:18]
+    up_biases, (in_out, keep, send, dq, dk, dv, sent_out, vmask, shared) = refs[18:20], refs[20:]
+    attention_backward_kernel(*given, in_out, sent_out, dq, dk, dv, vmask)
+    head_grads_kernel(eighth_ref, dq_two, dq, dk_two, dk, dv_two, dv, *lows, *others, *sums, *up_biases, keep, send, shared)
+    send[16:] = sent_out[...].reshape(-1, *send.shape[1:])
+
+
+def last_backward(grad_att, grad_pre, kept, w, pairs, eighth):
+    rows, width = grad_pre.shape
+    units = w["qb"].shape[1]
+    block = 4 * (units // 32)
+    outs = [((rows, width), F32), ((4, 4, block, width), LOW), ((16 + rows // block, block, width), LOW)]
+    scratch = [((rows, units), LOW), ((2 * rows, units), LOW), ((2 * rows, units), LOW), ((rows, width), LOW)]
+    scratch += [((4, 2 * rows, LANES), LOW), ((8, width), F32)]
+    return call(
+        last_backward_kernel, "last_backward", 16, outs, scratch, eighth, grad_att, grad_pre,
+        kept["q"], kept["k"], kept["v"], kept["e"], kept["inv"], kept["o"], w["heads"], *pairs, scalars=1,
+    )
 
 
 def first_row(column):
@@ -485,7 +505,7 @@
 def finish_kernel(ur, hr, eighth_ref, *refs):
     blocks, (down_out, up_out, out_out, up_bias) = refs[:8], refs[8:12]
     outs, biases, shared, (up_all, up_bias_all, *scratch) = refs[12:15], refs[15:17], refs[17], refs[18:]
-    head = 2 * ur + hr + ur // 4
+    head = 2 * ur + hr
     for at, block in enumerate(blocks):
         c, i = divmod(at, 4)
         slot = eighth_ref[0] ^ (2 * i + c)
@@ -493,14 +513,18 @@
         down_out[units] = block[:ur].astype(F32)
         up_all[units] = block[ur : 2 * ur].astype(F32)
         out_out[pl.ds(pl.multiple_of(slot * hr, hr), hr)] = block[2 * ur : 2 * ur + hr].astype(F32)
+        columns = [
+            jnp.broadcast_to(block[head + 3 * hr :, at : at + 1].astype(F32), (hr, LANES))
+            for at in range(0, 6 * (LANES // 4), LANES // 4)
+        ]
         for g in range(4):
-            some = pl.ds(pl.multiple_of(slot * ur + g * (ur // 4), ur // 4), ur // 4)
-            up_bias_all[some] = block[2 * ur + hr : head, g * LANES : (g + 1) * LANES].astype(F32)
+            some = pl.ds(pl.multiple_of(slot * ur + g * hr, hr), hr)
+            up_bias_all[some] = columns[2 + g]
         units = pl.ds(pl.multiple_of(slot * hr, hr), hr)
         for kind in range(3):
             scratch[kind][units] = block[head + kind * hr : head + (kind + 1) * hr].astype(F32)
         for kind in range(2):
-            scratch[3 + kind][units] = block[head + 3 * hr :, kind * LANES : (kind + 1) * LANES].astype(F32)
+            scratch[3 + kind][units] = columns[kind]
         line = block[head + 3 * hr :, 2 * LANES :].astype(F32)
         shared[pl.ds(slot, 1)] = jnp.concatenate((line[:1], line[8:9]), 1)
     up_out[...] = up_all[...].T
@@ -551,7 +575,7 @@
     shards = jnp.stack([heads_piece] + [swap_tensor(heads_piece, step) for step in (1, 2, 3)])
     heads_own = spread_plane(shards[:, : 4 * hr])
     ffn_own = spread_plane(join_shards(ffn_piece))
-    heads_own = lax.optimization_barrier(heads_own)
+    first_in, *heads_own = lax.optimization_barrier((first_in, *heads_own))
     head_blocks = heads_own + [swap_dp(block, 1) for block in heads_own]
     flat = shards[:, 4 * hr :].reshape(4, -1)[:, :count].astype(F32)
     flat = jnp.sum(flat.reshape(4, 3, -1), 1)
@@ -587,44 +611,51 @@
         middle_low, active, slope, unit_two, scale_two, layer_out, next_low = made[:7]
         if position == 0:
             w["ffn"] = made[7]
-        attention = {"q": q, "k": k, "v": v, "e": e, "inv": inv, "o": o, "unit": unit_one, "scale": scale_one}
+        attention = {"q": q, "k": k, "v": v, "e": e, "inv": inv, "o": o, "unit": unit_one, "scale": scale_one, "att": attended}
         ffn = {"slope": slope, "unit": unit_two, "scale": scale_two}
-        kept.append((attention, ffn, low, other, attended, middle_low, active))
+        kept.append((attention, ffn, low, other, middle_low, active))
         layer_in, low = layer_out, next_low
     result = regroup(low)
 
     grad_flow = regroup(cotangent)
-    ffn_pairs, head_pairs = [], []
-    for position in (1, 0):
-        attention, ffn, low, other, attended, middle_low, active = kept[position]
-        branch_two, grad_hidden, grad_pre, branch_one, grad_att, six = ffn_backward(grad_flow, ffn, attention, w)
-        ffn_pairs.append((active, branch_two, grad_hidden, middle_low, attended, branch_one))
-        if position == 0:
-            near, near_sent, far, far_sent = pair_halves(*ffn_grads(list(zip(*ffn_pairs))))
-            grad_att, near_sent, far_sent = lax.optimization_barrier((grad_att, near_sent, far_sent))
-            near_got, far_got = swap_dp(near_sent, 2), swap_dp(far_sent, 4)
-        grad_in, sent, dq, dk, dv = attention_backward(grad_att, grad_pre, attention, w)
-        if position == 1:
-            grad_in, result = lax.optimization_barrier((grad_in, result))
-        if position == 0:
-            dq, sent, near_got, far_got = lax.optimization_barrier((dq, sent, near_got, far_got))
-            (near, near_sent), (far, far_sent) = add_halves(near, near_got), add_halves(far, far_got)
-            dq, near_sent, far_sent = lax.optimization_barrier((dq, near_sent, far_sent))
-            near_got, far_got = swap_dp(near_sent, 4), swap_dp(far_sent, 2)
-        grad_flow = grad_in + swap_dp(sent, 1).astype(F32)
-        head_pairs.append((dq, dk, dv, low, other, six))
     at = jnp.reshape(eighth, (1,)).astype(jnp.int32)
-    keep, send = head_grads(list(zip(*head_pairs)), at)
-    near_got, far_got, keep, send = lax.optimization_barrier((near_got, far_got, keep, send))
-    ffn_parts = add_shards(near, near_got, far, far_got)
-    near, near_sent, far, far_sent = pair_halves(keep, send)
+    attention_two, ffn, low_two, other_two, middle_low, active = kept[1]
+    branch_two, grad_hidden, grad_pre, branch_one, grad_att, six_two = ffn_backward(grad_flow, ffn, attention_two, w)
+    pairs_two = (active, branch_two, grad_hidden, middle_low, attention_two["att"], branch_one)
+    grad_in, sent, dq, dk, dv = attention_backward(grad_att, grad_pre, attention_two, w)
+    grad_in, result = lax.optimization_barrier((grad_in, result))
+    grad_flow = grad_in + swap_dp(sent, 1).astype(F32)
+
+    attention, ffn, low, low_other, middle_low, active = kept[0]
+    branch_two, grad_hidden, grad_pre, branch_one, grad_att, six = ffn_backward(grad_flow, ffn, attention, w)
+    pairs_one = (active, branch_two, grad_hidden, middle_low, attention["att"], branch_one)
+    ffn_pairs = list(zip(pairs_two, pairs_one))
+    send, other_columns = ffn_grads(ffn_pairs, 1)
+    other = swap_dp(send, 1)
+    keep, own_columns = ffn_grads(ffn_pairs, 0)
+    near, near_sent, far, far_sent = pair_halves(keep, other)
+    grad_att, near_sent, far_sent = lax.optimization_barrier((grad_att, near_sent, far_sent))
     near_got, far_got = swap_dp(near_sent, 2), swap_dp(far_sent, 4)
-    ffn_own = reduce_shards(ffn_parts)
+    grad_in, keep, send = last_backward(
+        grad_att, grad_pre, attention, w,
+        (dq, dk, dv, low_two, low, other_two, low_other, six_two, six, own_columns, other_columns), at,
+    )
+    keep, send, near_got, far_got = lax.optimization_barrier((keep, send, near_got, far_got))
     (near, near_sent), (far, far_sent) = add_halves(near, near_got), add_halves(far, far_got)
+    near_sent, far_sent, send = lax.optimization_barrier((near_sent, far_sent, send))
     near_got, far_got = swap_dp(near_sent, 4), swap_dp(far_sent, 2)
-    head_own = reduce_shards(add_shards(near, near_got, far, far_got))
+    other = swap_dp(send, 1)
+    grad_low = (grad_in + other[16:].reshape(rows, width).astype(F32)).astype(LOW)
+    near_head, near_sent, far_head, far_sent = pair_halves(keep, other[:16].reshape(keep.shape))
+    near_head_got, far_head_got = lax.optimization_barrier((swap_dp(near_sent, 2), swap_dp(far_sent, 4)))
+    (near_head, near_sent), (far_head, far_sent) = add_halves(near_head, near_head_got), add_halves(far_head, far_head_got)
+    near_head_got, far_head_got = swap_dp(near_sent, 4), swap_dp(far_sent, 2)
+    ffn_parts = swap_shards(add_shards(near, near_got, far, far_got))
+    ffn_parts = lax.optimization_barrier((*ffn_parts, near_head_got, far_head_got))[:4]
+    ffn_own = sum_shards(ffn_parts)
+    head_own = sum_shards(swap_shards(add_shards(near_head, near_head_got, far_head, far_head_got)))
     own = jnp.concatenate((ffn_own, head_own))
-    own, grad_low = lax.optimization_barrier((own, grad_flow.astype(LOW)))
+    own, grad_low = lax.optimization_barrier((own, grad_low))
     input_grad = regroup(grad_low).astype(F32)
     (
         down_grad, up_grad, out_grad, up_bias_grad, q_grad, k_grad, v_grad, q_bias_grad, v_bias_grad, shared,

time: 229 us -> 218 us (0.952)
  waiting for transfers between devices: 42.8 us -> 32.7 us
  starting transfers between devices: 64 us -> 56.9 us
  local copies, waits for them, and re-layouts: 26.9 us -> 30.2 us
    ppermute x36 -> x35, waiting for transfers between devices: 25.4 us -> 18.5 us  [swap_dp(): return lax.ppermute(value, 'dp', [(i, i ^ bits) for i in range(count)])]
    ppermute x11, starting transfers between devices: 17.8 us -> 13.1 us  [swap_tensor(): return lax.ppermute(value, 'tensor', [(i, i ^ step) for i in range(count)])]
    ppermute x36 -> x35, starting transfers between devices: 35.2 us -> 31 us  [swap_dp(): return lax.ppermute(value, 'dp', [(i, i ^ bits) for i in range(count)])]
    ppermute x4, waiting for transfers between devices: 11.1 us -> 8.51 us  [regroup(): moved = lax.ppermute(block, ('dp', 'tensor'), pairs)]
    unnamed x97 -> x103, local copies, waits for them, and re-layouts: 20.3 us -> 21.3 us
  transfers between devices with their start and end apart: 51 -> 50, of which waited for: 18 -> 13; matrix products, arithmetic and copies ran while one was open for 3% -> 5% of each run, Pallas kernels for 22% -> 25%
where the time goes in v4:
time: 218 us; the launch traced here: 214 us
  Pallas kernels  85.8 us (39%)
  starting transfers between devices  56.9 us (26%)
  waiting for transfers between devices  32.7 us (15%)
  local copies, waits for them, and re-layouts  30.2 us (14%)
  other arithmetic  6.57 us (3%)
    pallas_call x11, Pallas kernels, call(): pl.pallas_call(kernel, in_specs=[pl.BlockSpec(memory_space=space) for spa...  85.8 us
    ppermute x35, starting transfers between devices, swap_dp(): return lax.ppermute(value, 'dp', [(i, i ^ bits) for i in range(count)])  31 us
    unnamed x103, local copies, waits for them, and re-layouts  21.3 us
    ppermute x35, waiting for transfers between devices, swap_dp(): return lax.ppermute(value, 'dp', [(i, i ^ bits) for i in range(count)])  18.5 us
    ppermute x11, starting transfers between devices, swap_tensor(): return lax.ppermute(value, 'tensor', [(i, i ^ step) for i in range(count)])  13.1 us
    ppermute x4, starting transfers between devices, regroup(): moved = lax.ppermute(block, ('dp', 'tensor'), pairs)  12.8 us
    ppermute x4, waiting for transfers between devices, regroup(): moved = lax.ppermute(block, ('dp', 'tensor'), pairs)  8.51 us
    ppermute x11, waiting for transfers between devices, swap_tensor(): return lax.ppermute(value, 'tensor', [(i, i ^ step) for i in range(count)])  5.73 us
  transfers between devices with their start and end apart: 50, of which 13 were waited for; matrix products, arithmetic and copies ran while one was open for 5% of the time, Pallas kernels for 25%

profile of v4, /device:TPU:1, one launch (start us, length us, event | category | flops | bytes accessed | tf_op | source)
XLA Modules:
  0.0 214.1 jit_solution(7552973575720992299)
XLA Ops:
  6.0 4.2 %collective-permute-start.3 = (bf16[80,512]{1,0:T(8,128)(2,1)S(1)}, bf16[80,512]{1,0:T(8,128)(2,1)S(1)}, u32[]{:S(2)}, u32[]{:S(2)}) collective-permute-start(bf16[80,512]{1,0:T(8,128)(2,1)S(1)} %constant_dynamic-update-slice_fusion.1), channel_id=1, source_target_pairs={{0,3},{1,2},{2,1},{3,0},{4,7},{5,6},{6,5},{7,4},{8,11},{9,10},{10,... | collective-permute-start | bytes 245768 | tf_op jit(solution)/shard_map/ppermute | solution.py:29
  15.7 3.8 %collective-permute-start = (bf16[512,512]{1,0:T(8,128)(2,1)S(1)}, bf16[512,512]{1,0:T(8,128)(2,1)}, u32[]{:S(2)}, u32[]{:S(2)}) collective-permute-start(bf16[512,512]{1,0:T(8,128)(2,1)S(1)} %copy-done.38), channel_id=1, source_target_pairs={{1,4},{3,6},{4,1},{6,3},{9,12},{11,14},{12,9},{14,11},{17,20},{19,... | collective-permute-start | bytes 1572872 | tf_op jit(solution)/shard_map/ppermute | solution.py:42
  24.9 4.4 %collective-permute-done = bf16[512,512]{1,0:T(8,128)(2,1)} collective-permute-done((bf16[512,512]{1,0:T(8,128)(2,1)S(1)}, bf16[512,512]{1,0:T(8,128)(2,1)}, u32[]{:S(2)}, u32[]{:S(2)}) %collective-permute-start) | collective-permute-done | bytes 524320 | tf_op jit(solution)/shard_map/ppermute | solution.py:42
  30.4 3.5 %collective-permute-done.5.refs_2_ = bf16[4,64,512]{2,1,0:T(8,128)(2,1)S(1)} collective-permute-done((bf16[4,64,512]{2,1,0:T(8,128)(2,1)S(1)}, bf16[4,64,512]{2,1,0:T(8,128)(2,1)S(1)}, u32[]{:S(2)}, u32[]{:S(2)}) %collective-permute-start.5) | collective-permute-done | bytes 262176 | tf_op jit(solution)/shard_map/ppermute | solution.py:24
  43.9 9.7 %attention_first.1 = (bf16[512,512]{1,0:T(8,128)(2,1)S(1)}, bf16[1024,512]{1,0:T(8,128)(2,1)S(1)}, bf16[1024,512]{1,0:T(8,128)(2,1)S(1)}, bf16[8,512,1024]{2,1,0...) custom-call(bf16[4,64,512]{2,1,0:T(8,128)(2,1)S(1)} %slice.296.refs_, ...), custom_call_target="tpu_custom_call" | custom-call | flops 9900000256 | tf_op jit(solution)/shard_map/attention_first/pallas_call | solution.py:145
  55.9 3.3 %copy-done.20 = bf16[8,512,1024]{2,1,0:T(8,128)(2,1)} copy-done((bf16[8,512,1024]{2,1,0:T(8,128)(2,1)}, bf16[8,512,1024]{2,1,0:T(8,128)(2,1)S(1)}, u32[]{:S(2)}) %copy-start.20) | copy-done | bytes 8388632
  67.5 2.8 %collective-permute-start.22 = (bf16[512,512]{1,0:T(8,128)(2,1)}, bf16[512,512]{1,0:T(8,128)(2,1)S(1)}, u32[]{:S(2)}, u32[]{:S(2)}) collective-permute-start(bf16[512,512]{1,0:T(8,128)(2,1)} %param.35), channel_id=1, source_target_pairs={{1,4},{3,6},{4,1},{6,3},{9,12},{11,14},{12,9},{14,11},{17,20},{19,... | collective-permute-start | bytes 1572872 | tf_op jit(solution)/shard_map/ppermute | solution.py:42
  74.2 6.8 %ffn_first.1 = (bf16[512,512]{1,0:T(8,128)(2,1)S(1)}, bf16[512,2048]{1,0:T(8,128)(2,1)S(1)}, bf16[512,2048]{1,0:T(8,128)(2,1)S(1)}, f32[512,512]{1,0:T(8,128)S(1...) custom-call(bf16[4,128,512]{2,1,0:T(8,128)(2,1)S(1)} %pad_maximum_fu, ...), custom_call_target="tpu_custom_call" | custom-call | flops 6600000000 | tf_op jit(solution)/shard_map/ffn_first/pallas_call | solution.py:145
  82.9 8.5 %attention_forward.1 = (bf16[512,512]{1,0:T(8,128)(2,1)S(1)}, bf16[1024,512]{1,0:T(8,128)(2,1)S(1)}, bf16[1024,512]{1,0:T(8,128)(2,1)S(1)}, bf16[8,512,1024]{2,1...) custom-call(f32[512,512]{1,0:T(8,128)S(1)} %get-tuple-element.130.in, ...), custom_call_target="tpu_custom_call" | custom-call | flops 8800000000 | tf_op jit(solution)/shard_map/attention_forward/pallas_call | solution.py:145
  91.5 16.4 %ffn_forward.1 = (bf16[512,512]{1,0:T(8,128)(2,1)S(1)}, bf16[512,2048]{1,0:T(8,128)(2,1)S(1)}, bf16[512,2048]{1,0:T(8,128)(2,1)S(1)}, f32[512,512]{1,0:T(8,128)S...) custom-call(f32[512,512]{1,0:T(8,128)S(1)} %get-tuple-element.133.mid_ref, ...), custom_call_target="tpu_custom_call" | custom-call | flops 5500000256 | tf_op jit(solution)/shard_map/ffn_forward/pallas_call | solution.py:145
  110.6 3.7 %ffn_backward.2 = (bf16[512,512]{1,0:T(8,128)(2,1)S(1)}, bf16[512,2048]{1,0:T(8,128)(2,1)S(1)}, f32[512,512]{1,0:T(8,128)S(1)}, bf16[512,512]{1,0:T(8,128)(2,1)S...) custom-call(bf16[2,8,4,64,512]{4,3,2,1,0:T(8,128)(2,1)S(1)} %get-tuple-element.128.w_ref, ...), custom_call_target="tpu_custom_call" | custom-call | flops 5500000256 | tf_op jit(solution)/shard_map/ffn_backward/pallas_call | solution.py:145
  114.3 11.9 %attention_backward.1 = (f32[512,512]{1,0:T(8,128)S(1)}, bf16[512,512]{1,0:T(8,128)(2,1)S(1)}, bf16[512,512]{1,0:T(8,128)(2,1)S(1)}, bf16[1024,512]{1,0:T(8,128)(2,1)S(1)}, bf16[1024,512]{1,0:T(8,128)(2,1)S(1)}) custom-call(bf16[512,512]{1,0:T(8,128)(2,1)S(1)} %get-tuple-element.139.att_ref, f32[512,512]{1,0:T(8,128)S(1)} %get-tuple-element.140.pre_ref, ...), custom_call_target="tpu_custom_call" | custom-call | flops 13200000000 | tf_op jit(solution)/shard_map/attention_backward/pallas_call | solution.py:145
  128.4 3.6 %ffn_backward.3 = (bf16[512,512]{1,0:T(8,128)(2,1)S(1)}, bf16[512,2048]{1,0:T(8,128)(2,1)S(1)}, f32[512,512]{1,0:T(8,128)S(1)}, bf16[512,512]{1,0:T(8,128)(2,1)S...) custom-call(bf16[2,8,4,64,512]{4,3,2,1,0:T(8,128)(2,1)S(1)} %get-tuple-element.128.w_ref, ...), custom_call_target="tpu_custom_call" | custom-call | flops 5500000256 | tf_op jit(solution)/shard_map/ffn_backward/pallas_call | solution.py:145
  132.0 3.5 %ffn_grads.3 = (bf16[4,4,144,512]{3,2,1,0:T(8,128)(2,1)S(1)}, bf16[1024,128]{1,0:T(8,128)(2,1)S(1)}) custom-call(bf16[512,2048]{1,0:T(8,128)(2,1)S(1)} %get-tuple-element.150.refs_0_, bf16[512,2048]{1,0:T(8,128)(2,1)S(1)} %get-tuple-element.151.refs_1_, bf16[512,512]{1,0:T(8,128)(2,1)S(1)} %get-tuple-element.152.refs_2_, ...), custom_call_target="tpu_custom_call" | custom-call | flops 3300000000 | tf_op jit(solution)/shard_map/ffn_grads/pallas_call | solution.py:145
  135.8 3.5 %ffn_grads.2 = (bf16[4,4,144,512]{3,2,1,0:T(8,128)(2,1)S(1)}, bf16[1024,128]{1,0:T(8,128)(2,1)S(1)}) custom-call(bf16[512,2048]{1,0:T(8,128)(2,1)S(1)} %get-tuple-element.150.refs_0_, bf16[512,2048]{1,0:T(8,128)(2,1)S(1)} %get-tuple-element.151.refs_1_, bf16[512,512]{1,0:T(8,128)(2,1)S(1)} %get-tuple-element.152.refs_2_, ...), custom_call_target="tpu_custom_call" | custom-call | flops 3300000000 | tf_op jit(solution)/shard_map/ffn_grads/pallas_call | solution.py:145
  142.6 16.0 %last_backward.1 = (f32[512,512]{1,0:T(8,128)S(1)}, bf16[4,4,64,512]{3,2,1,0:T(8,128)(2,1)S(1)}, bf16[24,64,512]{2,1,0:T(8,128)(2,1)S(1)}) custom-call(s32[1]{0:T(128)} %bitcast.19.eighth_ref, bf16[512,512]{1,0:T(8,128)(2,1)S(1)} %get-tuple-element.172.refs_0_, f32[512,512]{1,0:T(8,128)S(1)} %get-tuple-element.173.refs_1_, bf16[512,512]{1,0:T(8,128)(2,1)S(1)} %copy-done.36, ...), custom_call_target="tpu_custom_call" | custom-call | flops 17600000000 | tf_op jit(solution)/shard_map/last_backward/pallas_call | solution.py:145
  164.9 3.7 %collective-permute-done.29 = bf16[2,144,512]{2,1,0:T(8,128)(2,1)S(1)} collective-permute-done((bf16[2,144,512]{2,1,0:T(8,128)(2,1)S(1)}, bf16[2,144,512]{2,1,0:T(8,128)(2,1)S(1)}, u32[]{:S(2)}, u32[]{:S(2)}) %collective-permute-start.29) | collective-permute-done | bytes 294944 | tf_op jit(solution)/shard_map/ppermute | solution.py:24
  171.5 3.2 %collective-permute-done.35 = bf16[2,2,64,512]{3,2,1,0:T(8,128)(2,1)S(1)} collective-permute-done((bf16[2,2,64,512]{3,2,1,0:T(8,128)(2,1)S(1)}, bf16[2,2,64,512]{3,2,1,0:T(8,128)(2,1)S(1)}, u32[]{:S(2)}, u32[]{:S(2)}) %collective-permute-start.35) | collective-permute-done | bytes 262176 | tf_op jit(solution)/shard_map/ppermute | solution.py:24
  180.0 3.1 %collective-permute-done.32 = bf16[144,512]{1,0:T(8,128)(2,1)S(1)} collective-permute-done((bf16[144,512]{1,0:T(8,128)(2,1)S(1)}, bf16[144,512]{1,0:T(8,128)(2,1)S(1)}, u32[]{:S(2)}, u32[]{:S(2)}) %collective-permute-start.32) | collective-permute-done | bytes 147488 | tf_op jit(solution)/shard_map/ppermute | solution.py:29
  183.2 2.7 %collective-permute-start.41 = (bf16[64,512]{1,0:T(8,128)(2,1)S(1)}, bf16[64,512]{1,0:T(8,128)(2,1)S(1)}, u32[]{:S(2)}, u32[]{:S(2)}) collective-permute-start(bf16[64,512]{1,0:T(8,128)(2,1)S(1)} %get-tuple-element.242), channel_id=1, source_target_pairs={{0,3},{1,2},{2,1},{3,0},{4,7},{5,6},{6,5},{7,4},{8,11},{9,10},{10,... | collective-permute-start | bytes 196616 | tf_op jit(solution)/shard_map/ppermute | solution.py:29
  191.5 4.4 %collective-permute-start.46 = (bf16[208,512]{1,0:T(8,128)(2,1)S(1)}, bf16[208,512]{1,0:T(8,128)(2,1)S(1)}, u32[]{:S(2)}, u32[]{:S(2)}) collective-permute-start(bf16[208,512]{1,0:T(8,128)(2,1)S(1)} %pad_maximum_fusion.7.refs_0_), channel_id=1, source_target_pairs={{0,4},{4,0},{8,12},{12,8},{16,20},{20,16},{24,28},{28,24},{1,5},{5... | collective-permute-start | bytes 638984 | tf_op jit(solution)/shard_map/ppermute | solution.py:24
  195.9 3.9 %collective-permute-start.49 = (bf16[208,512]{1,0:T(8,128)(2,1)S(1)}, bf16[208,512]{1,0:T(8,128)(2,1)S(1)}, u32[]{:S(2)}, u32[]{:S(2)}) collective-permute-start(bf16[208,512]{1,0:T(8,128)(2,1)S(1)} %collective-permute-done.45.refs_3_), channel_id=1, source_target_pairs={{0,4},{4,0},{8,12},{12,8},{16,20},{20,16},{24,28},{28,24},{1,5},{5... | collective-permute-start | bytes 638984 | tf_op jit(solution)/shard_map/ppermute | solution.py:24
  202.3 3.5 %collective-permute-start.42 = (bf16[512,512]{1,0:T(8,128)(2,1)S(1)}, bf16[512,512]{1,0:T(8,128)(2,1)S(1)}, u32[]{:S(2)}, u32[]{:S(2)}) collective-permute-start(bf16[512,512]{1,0:T(8,128)(2,1)S(1)} %fusion), channel_id=1, source_target_pairs={{1,4},{3,6},{4,1},{6,3},{9,12},{11,14},{12,9},{14,11},{17,20},{19,... | collective-permute-start | bytes 1572872 | tf_op jit(solution)/shard_map/ppermute | solution.py:42
  208.7 4.1 %collective-permute-done.42 = bf16[512,512]{1,0:T(8,128)(2,1)S(1)} collective-permute-done((bf16[512,512]{1,0:T(8,128)(2,1)S(1)}, bf16[512,512]{1,0:T(8,128)(2,1)S(1)}, u32[]{:S(2)}, u32[]{:S(2)}) %collective-permute-start.42) | collective-permute-done | bytes 524320 | tf_op jit(solution)/shard_map/ppermute | solution.py:42
  (263 shorter events, 77.9 us)
Async XLA Ops:
  6.0 14.0 %collective-permute-start.3 = (bf16[80,512]{1,0:T(8,128)(2,1)S(1)}, bf16[80,512]{1,0:T(8,128)(2,1)S(1)}, u32[]{:S(2)}, u32[]{:S(2)}) collective-permute-start(bf16[80,512]{1,0:T(8,128)(2,1)S(1)} %constant_dynamic-update-slice_fusion.1), channel_id=1, source_target_pairs={{0,3},{1,2},{2,1},{3,0},{4,7},{5,6},{6,5},{7,4},{8,11},{9,10},{10,... | collective-permute-start | bytes 245768 | tf_op jit(solution)/shard_map/ppermute | solution.py:29
  13.5 10.6 %collective-permute-start.13 = (bf16[128,512]{1,0:T(8,128)(2,1)S(1)}, bf16[128,512]{1,0:T(8,128)(2,1)S(1)}, u32[]{:S(2)}, u32[]{:S(2)}) collective-permute-start(bf16[128,512]{1,0:T(8,128)(2,1)S(1)} %get-tuple-element.246), channel_id=1, source_target_pairs={{0,2},{1,3},{2,0},{3,1},{4,6},{5,7},{6,4},{7,5},{8,10},{9,11},{10,... | collective-permute-start | bytes 393224 | tf_op jit(solution)/shard_map/ppermute | solution.py:29
  15.7 13.6 %collective-permute-start = (bf16[512,512]{1,0:T(8,128)(2,1)S(1)}, bf16[512,512]{1,0:T(8,128)(2,1)}, u32[]{:S(2)}, u32[]{:S(2)}) collective-permute-start(bf16[512,512]{1,0:T(8,128)(2,1)S(1)} %copy-done.38), channel_id=1, source_target_pairs={{1,4},{3,6},{4,1},{6,3},{9,12},{11,14},{12,9},{14,11},{17,20},{19,... | collective-permute-start | bytes 1572872 | tf_op jit(solution)/shard_map/ppermute | solution.py:42
  20.3 10.1 %collective-permute-start.6 = (bf16[4,64,512]{2,1,0:T(8,128)(2,1)S(1)}, bf16[4,64,512]{2,1,0:T(8,128)(2,1)S(1)}, u32[]{:S(2)}, u32[]{:S(2)}) collective-permute-start(bf16[4,64,512]{2,1,0:T(8,128)(2,1)S(1)} %slice.296.refs_0_), channel_id=1, source_target_pairs={{0,24},{4,28},{8,16},{12,20},{16,8},{20,12},{24,0},{28,4},{1,25},{... | collective-permute-start | bytes 786440 | tf_op jit(solution)/shard_map/ppermute | solution.py:24
  22.5 11.4 %collective-permute-start.5 = (bf16[4,64,512]{2,1,0:T(8,128)(2,1)S(1)}, bf16[4,64,512]{2,1,0:T(8,128)(2,1)S(1)}, u32[]{:S(2)}, u32[]{:S(2)}) collective-permute-start(bf16[4,64,512]{2,1,0:T(8,128)(2,1)S(1)} %slice.296.refs_0_), channel_id=1, source_target_pairs={{0,16},{4,20},{8,24},{12,28},{16,0},{20,4},{24,8},{28,12},{1,17},{... | collective-permute-start | bytes 786440 | tf_op jit(solution)/shard_map/ppermute | solution.py:24
  22.7 11.2 %collective-permute-start.4 = (bf16[4,64,512]{2,1,0:T(8,128)(2,1)S(1)}, bf16[4,64,512]{2,1,0:T(8,128)(2,1)S(1)}, u32[]{:S(2)}, u32[]{:S(2)}) collective-permute-start(bf16[4,64,512]{2,1,0:T(8,128)(2,1)S(1)} %slice.296.refs_0_), channel_id=1, source_target_pairs={{0,8},{4,12},{8,0},{12,4},{16,24},{20,28},{24,16},{28,20},{1,9},{5... | collective-permute-start | bytes 786440 | tf_op jit(solution)/shard_map/ppermute | solution.py:24
  24.9 11.6 %collective-permute-start.14 = (bf16[2,128,512]{2,1,0:T(8,128)(2,1)}, bf16[2,128,512]{2,1,0:T(8,128)(2,1)S(1)}, u32[]{:S(2)}, u32[]{:S(2)}) collective-permute-start(bf16[2,128,512]{2,1,0:T(8,128)(2,1)} %pad_maximum_fusion.4), channel_id=1, source_target_pairs={{0,1},{1,0},{2,3},{3,2},{4,5},{5,4},{6,7},{7,6},{8,9},{9,8},{10,11... | collective-permute-start | bytes 786440 | tf_op jit(solution)/shard_map/ppermute | solution.py:29
  38.5 27.1 %collective-permute-start.17 = (bf16[4,128,512]{2,1,0:T(8,128)(2,1)S(1)}, bf16[4,128,512]{2,1,0:T(8,128)(2,1)S(1)}, u32[]{:S(2)}, u32[]{:S(2)}) collective-permute-start(bf16[4,128,512]{2,1,0:T(8,128)(2,1)S(1)} %pad_maximum_fusion.2.refs_0_), channel_id=1, source_target_pairs={{0,24},{4,28},{8,16},{12,20},{16,8},{20,12},{24,0},{28,4},{1,25},{... | collective-permute-start | bytes 1572872 | tf_op jit(solution)/shard_map/ppermute | solution.py:24
  40.1 25.5 %collective-permute-start.16 = (bf16[4,128,512]{2,1,0:T(8,128)(2,1)S(1)}, bf16[4,128,512]{2,1,0:T(8,128)(2,1)}, u32[]{:S(2)}, u32[]{:S(2)}) collective-permute-start(bf16[4,128,512]{2,1,0:T(8,128)(2,1)S(1)} %pad_maximum_fusion.2.refs_0_), channel_id=1, source_target_pairs={{0,16},{4,20},{8,24},{12,28},{16,0},{20,4},{24,8},{28,12},{1,17},{... | collective-permute-start | bytes 1572872 | tf_op jit(solution)/shard_map/ppermute | solution.py:24
  40.8 24.8 %collective-permute-start.15 = (bf16[4,128,512]{2,1,0:T(8,128)(2,1)S(1)}, bf16[4,128,512]{2,1,0:T(8,128)(2,1)}, u32[]{:S(2)}, u32[]{:S(2)}) collective-permute-start(bf16[4,128,512]{2,1,0:T(8,128)(2,1)S(1)} %pad_maximum_fusion.2.refs_0_), channel_id=1, source_target_pairs={{0,8},{4,12},{8,0},{12,4},{16,24},{20,28},{24,16},{28,20},{1,9},{5... | collective-permute-start | bytes 1572872 | tf_op jit(solution)/shard_map/ppermute | solution.py:24
  67.5 13.9 %collective-permute-start.22 = (bf16[512,512]{1,0:T(8,128)(2,1)}, bf16[512,512]{1,0:T(8,128)(2,1)S(1)}, u32[]{:S(2)}, u32[]{:S(2)}) collective-permute-start(bf16[512,512]{1,0:T(8,128)(2,1)} %param.35), channel_id=1, source_target_pairs={{1,4},{3,6},{4,1},{6,3},{9,12},{11,14},{12,9},{14,11},{17,20},{19,... | collective-permute-start | bytes 1572872 | tf_op jit(solution)/shard_map/ppermute | solution.py:42
  107.9 18.4 %collective-permute-start.24 = (bf16[512,512]{1,0:T(8,128)(2,1)S(1)}, bf16[512,512]{1,0:T(8,128)(2,1)S(1)}, u32[]{:S(2)}, u32[]{:S(2)}) collective-permute-start(bf16[512,512]{1,0:T(8,128)(2,1)S(1)} %get-tuple-element.148), channel_id=1, source_target_pairs={{1,4},{3,6},{4,1},{6,3},{9,12},{11,14},{12,9},{14,11},{17,20},{19,... | collective-permute-start | bytes 1572872 | tf_op jit(solution)/shard_map/ppermute | solution.py:42
  140.7 18.0 %collective-permute-start.27 = (bf16[2,2,144,512]{3,2,1,0:T(8,128)(2,1)S(1)}, bf16[2,2,144,512]{3,2,1,0:T(8,128)(2,1)S(1)}, u32[]{:S(2)}, u32[]{:S(2)}) collective-permute-start(bf16[2,2,144,512]{3,2,1,0:T(8,128)(2,1)S(1)} %pad_maximum_fusion), channel_id=1, source_target_pairs={{0,8},{4,12},{8,0},{12,4},{16,24},{20,28},{24,16},{28,20},{1,9},{5... | collective-permute-start | bytes 1769480 | tf_op jit(solution)/shard_map/ppermute | solution.py:24
  142.0 16.7 %collective-permute-start.28 = (bf16[2,2,144,512]{3,2,1,0:T(8,128)(2,1)S(1)}, bf16[2,2,144,512]{3,2,1,0:T(8,128)(2,1)S(1)}, u32[]{:S(2)}, u32[]{:S(2)}) collective-permute-start(bf16[2,2,144,512]{3,2,1,0:T(8,128)(2,1)S(1)} %pad_maximum_fusion.1), channel_id=1, source_target_pairs={{0,16},{4,20},{8,24},{12,28},{16,0},{20,4},{24,8},{28,12},{1,17},{... | collective-permute-start | bytes 1769480 | tf_op jit(solution)/shard_map/ppermute | solution.py:24
  163.3 11.4 %collective-permute-start.35 = (bf16[2,2,64,512]{3,2,1,0:T(8,128)(2,1)S(1)}, bf16[2,2,64,512]{3,2,1,0:T(8,128)(2,1)S(1)}, u32[]{:S(2)}, u32[]{:S(2)}) collective-permute-start(bf16[2,2,64,512]{3,2,1,0:T(8,128)(2,1)S(1)} %pad_maximum_fusion.5), channel_id=1, source_target_pairs={{0,8},{4,12},{8,0},{12,4},{16,24},{20,28},{24,16},{28,20},{1,9},{5... | collective-permute-start | bytes 786440 | tf_op jit(solution)/shard_map/ppermute | solution.py:24
  164.3 10.4 %collective-permute-start.36 = (bf16[2,2,64,512]{3,2,1,0:T(8,128)(2,1)S(1)}, bf16[2,2,64,512]{3,2,1,0:T(8,128)(2,1)S(1)}, u32[]{:S(2)}, u32[]{:S(2)}) collective-permute-start(bf16[2,2,64,512]{3,2,1,0:T(8,128)(2,1)S(1)} %pad_maximum_fusion.6), channel_id=1, source_target_pairs={{0,16},{4,20},{8,24},{12,28},{16,0},{20,4},{24,8},{28,12},{1,17},{... | collective-permute-start | bytes 786440 | tf_op jit(solution)/shard_map/ppermute | solution.py:24
  168.6 11.4 %collective-permute-start.30 = (bf16[144,512]{1,0:T(8,128)(2,1)S(1)}, bf16[144,512]{1,0:T(8,128)(2,1)S(1)}, u32[]{:S(2)}, u32[]{:S(2)}) collective-permute-start(bf16[144,512]{1,0:T(8,128)(2,1)S(1)} %get-tuple-element.239), channel_id=1, source_target_pairs={{0,1},{1,0},{2,3},{3,2},{4,5},{5,4},{6,7},{7,6},{8,9},{9,8},{10,11... | collective-permute-start | bytes 442376 | tf_op jit(solution)/shard_map/ppermute | solution.py:29
  170.0 10.0 %collective-permute-start.33 = (bf16[144,512]{1,0:T(8,128)(2,1)S(1)}, bf16[144,512]{1,0:T(8,128)(2,1)S(1)}, u32[]{:S(2)}, u32[]{:S(2)}) collective-permute-start(bf16[144,512]{1,0:T(8,128)(2,1)S(1)} %get-tuple-element.237), channel_id=1, source_target_pairs={{0,3},{1,2},{2,1},{3,0},{4,7},{5,6},{6,5},{7,4},{8,11},{9,10},{10,... | collective-permute-start | bytes 442376 | tf_op jit(solution)/shard_map/ppermute | solution.py:29
  170.2 12.9 %collective-permute-start.32 = (bf16[144,512]{1,0:T(8,128)(2,1)S(1)}, bf16[144,512]{1,0:T(8,128)(2,1)S(1)}, u32[]{:S(2)}, u32[]{:S(2)}) collective-permute-start(bf16[144,512]{1,0:T(8,128)(2,1)S(1)} %get-tuple-element.238), channel_id=1, source_target_pairs={{0,2},{1,3},{2,0},{3,1},{4,6},{5,7},{6,4},{7,5},{8,10},{9,11},{10,... | collective-permute-start | bytes 442376 | tf_op jit(solution)/shard_map/ppermute | solution.py:29
  189.5 10.2 %collective-permute-start.44 = (bf16[208,512]{1,0:T(8,128)(2,1)S(1)}, bf16[208,512]{1,0:T(8,128)(2,1)S(1)}, u32[]{:S(2)}, u32[]{:S(2)}) collective-permute-start(bf16[208,512]{1,0:T(8,128)(2,1)S(1)} %pad_maximum_fusion.7.refs_0_), channel_id=1, source_target_pairs={{0,16},{4,20},{8,24},{12,28},{16,0},{20,4},{24,8},{28,12},{1,17},{... | collective-permute-start | bytes 638984 | tf_op jit(solution)/shard_map/ppermute | solution.py:24
  190.9 10.8 %collective-permute-start.43 = (bf16[208,512]{1,0:T(8,128)(2,1)S(1)}, bf16[208,512]{1,0:T(8,128)(2,1)S(1)}, u32[]{:S(2)}, u32[]{:S(2)}) collective-permute-start(bf16[208,512]{1,0:T(8,128)(2,1)S(1)} %pad_maximum_fusion.7.refs_0_), channel_id=1, source_target_pairs={{0,8},{4,12},{8,0},{12,4},{16,24},{20,28},{24,16},{28,20},{1,9},{5... | collective-permute-start | bytes 638984 | tf_op jit(solution)/shard_map/ppermute | solution.py:24
  191.5 14.4 %collective-permute-start.46 = (bf16[208,512]{1,0:T(8,128)(2,1)S(1)}, bf16[208,512]{1,0:T(8,128)(2,1)S(1)}, u32[]{:S(2)}, u32[]{:S(2)}) collective-permute-start(bf16[208,512]{1,0:T(8,128)(2,1)S(1)} %pad_maximum_fusion.7.refs_0_), channel_id=1, source_target_pairs={{0,4},{4,0},{8,12},{12,8},{16,20},{20,16},{24,28},{28,24},{1,5},{5... | collective-permute-start | bytes 638984 | tf_op jit(solution)/shard_map/ppermute | solution.py:24
  195.9 10.0 %collective-permute-start.49 = (bf16[208,512]{1,0:T(8,128)(2,1)S(1)}, bf16[208,512]{1,0:T(8,128)(2,1)S(1)}, u32[]{:S(2)}, u32[]{:S(2)}) collective-permute-start(bf16[208,512]{1,0:T(8,128)(2,1)S(1)} %collective-permute-done.45.refs_3_), channel_id=1, source_target_pairs={{0,4},{4,0},{8,12},{12,8},{16,20},{20,16},{24,28},{28,24},{1,5},{5... | collective-permute-start | bytes 638984 | tf_op jit(solution)/shard_map/ppermute | solution.py:24
  202.3 10.5 %collective-permute-start.42 = (bf16[512,512]{1,0:T(8,128)(2,1)S(1)}, bf16[512,512]{1,0:T(8,128)(2,1)S(1)}, u32[]{:S(2)}, u32[]{:S(2)}) collective-permute-start(bf16[512,512]{1,0:T(8,128)(2,1)S(1)} %fusion), channel_id=1, source_target_pairs={{1,4},{3,6},{4,1},{6,3},{9,12},{11,14},{12,9},{14,11},{17,20},{19,... | collective-permute-start | bytes 1572872 | tf_op jit(solution)/shard_map/ppermute | solution.py:42
  (73 other events, 420.5 us)

commit v5 on v4

--- a/solution.py
+++ b/solution.py
@@ -52,11 +52,6 @@
 
 def spread_plane(block):
     return [block] + [swap_dp(block, bits) for bits in (2, 4, 6)]
-
-
-def spread(block):
-    own = spread_plane(block)
-    return own + [swap_dp(block, 1) for block in own]
 
 
 def sum_parts(parts):
@@ -535,9 +530,8 @@
         biases[kind][...] = first_row(scratch[3 + kind][...])
 
 
-def finish(own, ur, hr, eighth):
-    blocks = spread(own)
-    width = own.shape[1]
+def finish(blocks, ur, hr, eighth):
+    width = blocks[0].shape[1]
     outs = [((8 * ur, width), F32), ((width, 8 * ur), F32), ((8 * hr, width), F32), ((1, 8 * ur), F32)]
     outs += [((width, 8 * hr), F32)] * 3 + [((1, 8 * hr), F32)] * 2 + [((8, width), F32)]
     scratch = [((8 * ur, width), F32), ((8 * ur, LANES), F32)]
@@ -656,10 +650,14 @@
     head_own = sum_shards(swap_shards(add_shards(near_head, near_head_got, far_head, far_head_got)))
     own = jnp.concatenate((ffn_own, head_own))
     own, grad_low = lax.optimization_barrier((own, grad_low))
-    input_grad = regroup(grad_low).astype(F32)
+    own, *others = spread_plane(own)
+    own, *others, input_grad = lax.optimization_barrier((own, *others, regroup(grad_low)))
+    input_grad = input_grad.astype(F32)
+    plane = [own] + others
+    blocks = plane + [swap_dp(block, 1) for block in plane]
     (
         down_grad, up_grad, out_grad, up_bias_grad, q_grad, k_grad, v_grad, q_bias_grad, v_bias_grad, shared,
-    ) = finish(own, ur, hr, at)
+    ) = finish(blocks, ur, hr, at)
     return (
         result, input_grad, q_grad, q_bias_grad[0], k_grad, v_grad, v_bias_grad[0], out_grad, shared[5], shared[3], shared[4],
         up_grad, up_bias_grad[0], down_grad, shared[2], shared[0], shared[1],

time: 218 us -> 216 us (level)
  starting transfers between devices: 56.9 us -> 49.9 us
  waiting for transfers between devices: 32.7 us -> 37.3 us
    ppermute x35, starting transfers between devices: 31 us -> 21.2 us  [swap_dp(): return lax.ppermute(value, 'dp', [(i, i ^ bits) for i in range(count)])]
    ppermute x35, waiting for transfers between devices: 18.5 us -> 22.8 us  [swap_dp(): return lax.ppermute(value, 'dp', [(i, i ^ bits) for i in range(count)])]
    ppermute x4, starting transfers between devices: 12.8 us -> 15.6 us  [regroup(): moved = lax.ppermute(block, ('dp', 'tensor'), pairs)]
  transfers between devices with their start and end apart: 50 -> 50, of which waited for: 13 -> 16; matrix products, arithmetic and copies ran while one was open for 5% -> 5% of each run, Pallas kernels for 25% -> 24%
where the time goes in v5:
time: 216 us; the launch traced here: 212 us
  Pallas kernels  85.8 us (40%)
  starting transfers between devices  49.9 us (23%)
  waiting for transfers between devices  37.3 us (17%)
  local copies, waits for them, and re-layouts  30.2 us (14%)
  other arithmetic  6.69 us (3%)
    pallas_call x11, Pallas kernels, call(): pl.pallas_call(kernel, in_specs=[pl.BlockSpec(memory_space=space) for spa...  85.8 us
    ppermute x35, waiting for transfers between devices, swap_dp(): return lax.ppermute(value, 'dp', [(i, i ^ bits) for i in range(count)])  22.8 us
    unnamed x103, local copies, waits for them, and re-layouts  21.3 us
    ppermute x35, starting transfers between devices, swap_dp(): return lax.ppermute(value, 'dp', [(i, i ^ bits) for i in range(count)])  21.2 us
    ppermute x4, starting transfers between devices, regroup(): moved = lax.ppermute(block, ('dp', 'tensor'), pairs)  15.6 us
    ppermute x11, starting transfers between devices, swap_tensor(): return lax.ppermute(value, 'tensor', [(i, i ^ step) for i in range(count)])  13.1 us
    ppermute x4, waiting for transfers between devices, regroup(): moved = lax.ppermute(block, ('dp', 'tensor'), pairs)  8.83 us
    ppermute x11, waiting for transfers between devices, swap_tensor(): return lax.ppermute(value, 'tensor', [(i, i ^ step) for i in range(count)])  5.73 us
  transfers between devices with their start and end apart: 50, of which 16 were waited for; matrix products, arithmetic and copies ran while one was open for 5% of the time, Pallas kernels for 24%

profile of v5, /device:TPU:1, one launch (start us, length us, event | category | flops | bytes accessed | tf_op | source)
XLA Modules:
  0.0 211.6 jit_solution(4652105949310427603)
XLA Ops:
  6.0 4.2 %collective-permute-start.3 = (bf16[80,512]{1,0:T(8,128)(2,1)S(1)}, bf16[80,512]{1,0:T(8,128)(2,1)S(1)}, u32[]{:S(2)}, u32[]{:S(2)}) collective-permute-start(bf16[80,512]{1,0:T(8,128)(2,1)S(1)} %constant_dynamic-update-slice_fusion.1), channel_id=1, source_target_pairs={{0,3},{1,2},{2,1},{3,0},{4,7},{5,6},{6,5},{7,4},{8,11},{9,10},{10,... | collective-permute-start | bytes 245768 | tf_op jit(solution)/shard_map/ppermute | solution.py:29
  15.7 3.8 %collective-permute-start = (bf16[512,512]{1,0:T(8,128)(2,1)S(1)}, bf16[512,512]{1,0:T(8,128)(2,1)}, u32[]{:S(2)}, u32[]{:S(2)}) collective-permute-start(bf16[512,512]{1,0:T(8,128)(2,1)S(1)} %copy-done.38), channel_id=1, source_target_pairs={{1,4},{3,6},{4,1},{6,3},{9,12},{11,14},{12,9},{14,11},{17,20},{19,... | collective-permute-start | bytes 1572872 | tf_op jit(solution)/shard_map/ppermute | solution.py:42
  24.9 4.4 %collective-permute-done = bf16[512,512]{1,0:T(8,128)(2,1)} collective-permute-done((bf16[512,512]{1,0:T(8,128)(2,1)S(1)}, bf16[512,512]{1,0:T(8,128)(2,1)}, u32[]{:S(2)}, u32[]{:S(2)}) %collective-permute-start) | collective-permute-done | bytes 524320 | tf_op jit(solution)/shard_map/ppermute | solution.py:42
  30.4 3.5 %collective-permute-done.5.refs_2_ = bf16[4,64,512]{2,1,0:T(8,128)(2,1)S(1)} collective-permute-done((bf16[4,64,512]{2,1,0:T(8,128)(2,1)S(1)}, bf16[4,64,512]{2,1,0:T(8,128)(2,1)S(1)}, u32[]{:S(2)}, u32[]{:S(2)}) %collective-permute-start.5) | collective-permute-done | bytes 262176 | tf_op jit(solution)/shard_map/ppermute | solution.py:24
  43.9 9.7 %attention_first.1 = (bf16[512,512]{1,0:T(8,128)(2,1)S(1)}, bf16[1024,512]{1,0:T(8,128)(2,1)S(1)}, bf16[1024,512]{1,0:T(8,128)(2,1)S(1)}, bf16[8,512,1024]{2,1,0...) custom-call(bf16[4,64,512]{2,1,0:T(8,128)(2,1)S(1)} %slice.296.refs_, ...), custom_call_target="tpu_custom_call" | custom-call | flops 9900000256 | tf_op jit(solution)/shard_map/attention_first/pallas_call | solution.py:140
  55.9 3.3 %copy-done.20 = bf16[8,512,1024]{2,1,0:T(8,128)(2,1)} copy-done((bf16[8,512,1024]{2,1,0:T(8,128)(2,1)}, bf16[8,512,1024]{2,1,0:T(8,128)(2,1)S(1)}, u32[]{:S(2)}) %copy-start.20) | copy-done | bytes 8388632
  67.5 2.8 %collective-permute-start.22 = (bf16[512,512]{1,0:T(8,128)(2,1)}, bf16[512,512]{1,0:T(8,128)(2,1)S(1)}, u32[]{:S(2)}, u32[]{:S(2)}) collective-permute-start(bf16[512,512]{1,0:T(8,128)(2,1)} %param.35), channel_id=1, source_target_pairs={{1,4},{3,6},{4,1},{6,3},{9,12},{11,14},{12,9},{14,11},{17,20},{19,... | collective-permute-start | bytes 1572872 | tf_op jit(solution)/shard_map/ppermute | solution.py:42
  74.2 6.8 %ffn_first.1 = (bf16[512,512]{1,0:T(8,128)(2,1)S(1)}, bf16[512,2048]{1,0:T(8,128)(2,1)S(1)}, bf16[512,2048]{1,0:T(8,128)(2,1)S(1)}, f32[512,512]{1,0:T(8,128)S(1...) custom-call(bf16[4,128,512]{2,1,0:T(8,128)(2,1)S(1)} %pad_maximum_fu, ...), custom_call_target="tpu_custom_call" | custom-call | flops 6600000000 | tf_op jit(solution)/shard_map/ffn_first/pallas_call | solution.py:140
  82.9 8.5 %attention_forward.1 = (bf16[512,512]{1,0:T(8,128)(2,1)S(1)}, bf16[1024,512]{1,0:T(8,128)(2,1)S(1)}, bf16[1024,512]{1,0:T(8,128)(2,1)S(1)}, bf16[8,512,1024]{2,1...) custom-call(f32[512,512]{1,0:T(8,128)S(1)} %get-tuple-element.135.in, ...), custom_call_target="tpu_custom_call" | custom-call | flops 8800000000 | tf_op jit(solution)/shard_map/attention_forward/pallas_call | solution.py:140
  91.5 16.4 %ffn_forward.1 = (bf16[512,512]{1,0:T(8,128)(2,1)S(1)}, bf16[512,2048]{1,0:T(8,128)(2,1)S(1)}, bf16[512,2048]{1,0:T(8,128)(2,1)S(1)}, f32[512,512]{1,0:T(8,128)S...) custom-call(f32[512,512]{1,0:T(8,128)S(1)} %get-tuple-element.138.mid_ref, ...), custom_call_target="tpu_custom_call" | custom-call | flops 5500000256 | tf_op jit(solution)/shard_map/ffn_forward/pallas_call | solution.py:140
  107.9 2.7 %collective-permute-start.24 = (bf16[512,512]{1,0:T(8,128)(2,1)S(1)}, bf16[512,512]{1,0:T(8,128)(2,1)S(1)}, u32[]{:S(2)}, u32[]{:S(2)}) collective-permute-start(bf16[512,512]{1,0:T(8,128)(2,1)S(1)} %get-tuple-element.153), channel_id=1, source_target_pairs={{1,4},{3,6},{4,1},{6,3},{9,12},{11,14},{12,9},{14,11},{17,20},{19,... | collective-permute-start | bytes 1572872 | tf_op jit(solution)/shard_map/ppermute | solution.py:42
  110.6 3.7 %ffn_backward.2 = (bf16[512,512]{1,0:T(8,128)(2,1)S(1)}, bf16[512,2048]{1,0:T(8,128)(2,1)S(1)}, f32[512,512]{1,0:T(8,128)S(1)}, bf16[512,512]{1,0:T(8,128)(2,1)S...) custom-call(bf16[2,8,4,64,512]{4,3,2,1,0:T(8,128)(2,1)S(1)} %get-tuple-element.133.w_ref, ...), custom_call_target="tpu_custom_call" | custom-call | flops 5500000256 | tf_op jit(solution)/shard_map/ffn_backward/pallas_call | solution.py:140
  114.3 11.9 %attention_backward.1 = (f32[512,512]{1,0:T(8,128)S(1)}, bf16[512,512]{1,0:T(8,128)(2,1)S(1)}, bf16[512,512]{1,0:T(8,128)(2,1)S(1)}, bf16[1024,512]{1,0:T(8,128)(2,1)S(1)}, bf16[1024,512]{1,0:T(8,128)(2,1)S(1)}) custom-call(bf16[512,512]{1,0:T(8,128)(2,1)S(1)} %get-tuple-element.144.att_ref, f32[512,512]{1,0:T(8,128)S(1)} %get-tuple-element.145.pre_ref, ...), custom_call_target="tpu_custom_call" | custom-call | flops 13200000000 | tf_op jit(solution)/shard_map/attention_backward/pallas_call | solution.py:140
  128.4 3.6 %ffn_backward.3 = (bf16[512,512]{1,0:T(8,128)(2,1)S(1)}, bf16[512,2048]{1,0:T(8,128)(2,1)S(1)}, f32[512,512]{1,0:T(8,128)S(1)}, bf16[512,512]{1,0:T(8,128)(2,1)S...) custom-call(bf16[2,8,4,64,512]{4,3,2,1,0:T(8,128)(2,1)S(1)} %get-tuple-element.133.w_ref, ...), custom_call_target="tpu_custom_call" | custom-call | flops 5500000256 | tf_op jit(solution)/shard_map/ffn_backward/pallas_call | solution.py:140
  132.0 3.5 %ffn_grads.3 = (bf16[4,4,144,512]{3,2,1,0:T(8,128)(2,1)S(1)}, bf16[1024,128]{1,0:T(8,128)(2,1)S(1)}) custom-call(bf16[512,2048]{1,0:T(8,128)(2,1)S(1)} %get-tuple-element.155.refs_0_, bf16[512,2048]{1,0:T(8,128)(2,1)S(1)} %get-tuple-element.156.refs_1_, bf16[512,512]{1,0:T(8,128)(2,1)S(1)} %get-tuple-element.157.refs_2_, ...), custom_call_target="tpu_custom_call" | custom-call | flops 3300000000 | tf_op jit(solution)/shard_map/ffn_grads/pallas_call | solution.py:140
  135.8 3.5 %ffn_grads.2 = (bf16[4,4,144,512]{3,2,1,0:T(8,128)(2,1)S(1)}, bf16[1024,128]{1,0:T(8,128)(2,1)S(1)}) custom-call(bf16[512,2048]{1,0:T(8,128)(2,1)S(1)} %get-tuple-element.155.refs_0_, bf16[512,2048]{1,0:T(8,128)(2,1)S(1)} %get-tuple-element.156.refs_1_, bf16[512,512]{1,0:T(8,128)(2,1)S(1)} %get-tuple-element.157.refs_2_, ...), custom_call_target="tpu_custom_call" | custom-call | flops 3300000000 | tf_op jit(solution)/shard_map/ffn_grads/pallas_call | solution.py:140
  142.6 16.0 %last_backward.1 = (f32[512,512]{1,0:T(8,128)S(1)}, bf16[4,4,64,512]{3,2,1,0:T(8,128)(2,1)S(1)}, bf16[24,64,512]{2,1,0:T(8,128)(2,1)S(1)}) custom-call(s32[1]{0:T(128)} %bitcast.19.eighth_ref, bf16[512,512]{1,0:T(8,128)(2,1)S(1)} %get-tuple-element.177.refs_0_, f32[512,512]{1,0:T(8,128)S(1)} %get-tuple-element.178.refs_1_, bf16[512,512]{1,0:T(8,128)(2,1)S(1)} %copy-done.36, ...), custom_call_target="tpu_custom_call" | custom-call | flops 17600000000 | tf_op jit(solution)/shard_map/last_backward/pallas_call | solution.py:140
  164.9 3.7 %collective-permute-done.29 = bf16[2,144,512]{2,1,0:T(8,128)(2,1)S(1)} collective-permute-done((bf16[2,144,512]{2,1,0:T(8,128)(2,1)S(1)}, bf16[2,144,512]{2,1,0:T(8,128)(2,1)S(1)}, u32[]{:S(2)}, u32[]{:S(2)}) %collective-permute-start.29) | collective-permute-done | bytes 294944 | tf_op jit(solution)/shard_map/ppermute | solution.py:24
  171.5 3.2 %collective-permute-done.35 = bf16[2,2,64,512]{3,2,1,0:T(8,128)(2,1)S(1)} collective-permute-done((bf16[2,2,64,512]{3,2,1,0:T(8,128)(2,1)S(1)}, bf16[2,2,64,512]{3,2,1,0:T(8,128)(2,1)S(1)}, u32[]{:S(2)}, u32[]{:S(2)}) %collective-permute-start.35) | collective-permute-done | bytes 262176 | tf_op jit(solution)/shard_map/ppermute | solution.py:24
  180.0 3.1 %collective-permute-done.32 = bf16[144,512]{1,0:T(8,128)(2,1)S(1)} collective-permute-done((bf16[144,512]{1,0:T(8,128)(2,1)S(1)}, bf16[144,512]{1,0:T(8,128)(2,1)S(1)}, u32[]{:S(2)}, u32[]{:S(2)}) %collective-permute-start.32) | collective-permute-done | bytes 147488 | tf_op jit(solution)/shard_map/ppermute | solution.py:29
  183.2 2.7 %collective-permute-start.41 = (bf16[64,512]{1,0:T(8,128)(2,1)S(1)}, bf16[64,512]{1,0:T(8,128)(2,1)S(1)}, u32[]{:S(2)}, u32[]{:S(2)}) collective-permute-start(bf16[64,512]{1,0:T(8,128)(2,1)S(1)} %get-tuple-element.252), channel_id=1, source_target_pairs={{0,3},{1,2},{2,1},{3,0},{4,7},{5,6},{6,5},{7,4},{8,11},{9,10},{10,... | collective-permute-start | bytes 196616 | tf_op jit(solution)/shard_map/ppermute | solution.py:29
  188.7 6.3 %collective-permute-start.45 = (bf16[512,512]{1,0:T(8,128)(2,1)S(1)}, bf16[512,512]{1,0:T(8,128)(2,1)S(1)}, u32[]{:S(2)}, u32[]{:S(2)}) collective-permute-start(bf16[512,512]{1,0:T(8,128)(2,1)S(1)} %fusion), channel_id=1, source_target_pairs={{1,4},{3,6},{4,1},{6,3},{9,12},{11,14},{12,9},{14,11},{17,20},{19,... | collective-permute-start | bytes 1572872 | tf_op jit(solution)/shard_map/ppermute | solution.py:42
  197.7 4.4 %collective-permute-done.45 = bf16[512,512]{1,0:T(8,128)(2,1)S(1)} collective-permute-done((bf16[512,512]{1,0:T(8,128)(2,1)S(1)}, bf16[512,512]{1,0:T(8,128)(2,1)S(1)}, u32[]{:S(2)}, u32[]{:S(2)}) %collective-permute-start.45) | collective-permute-done | bytes 524320 | tf_op jit(solution)/shard_map/ppermute | solution.py:42
  203.1 3.1 %collective-permute-done.43.refs_2_ = bf16[208,512]{1,0:T(8,128)(2,1)S(1)} collective-permute-done((bf16[208,512]{1,0:T(8,128)(2,1)S(1)}, bf16[208,512]{1,0:T(8,128)(2,1)S(1)}, u32[]{:S(2)}, u32[]{:S(2)}) %collective-permute-start.43) | collective-permute-done | bytes 213024 | tf_op jit(solution)/shard_map/ppermute | solution.py:24
  (264 shorter events, 75.0 us)
Async XLA Ops:
  6.0 14.0 %collective-permute-start.3 = (bf16[80,512]{1,0:T(8,128)(2,1)S(1)}, bf16[80,512]{1,0:T(8,128)(2,1)S(1)}, u32[]{:S(2)}, u32[]{:S(2)}) collective-permute-start(bf16[80,512]{1,0:T(8,128)(2,1)S(1)} %constant_dynamic-update-slice_fusion.1), channel_id=1, source_target_pairs={{0,3},{1,2},{2,1},{3,0},{4,7},{5,6},{6,5},{7,4},{8,11},{9,10},{10,... | collective-permute-start | bytes 245768 | tf_op jit(solution)/shard_map/ppermute | solution.py:29
  10.2 9.8 %collective-permute-start.2 = (bf16[80,512]{1,0:T(8,128)(2,1)S(1)}, bf16[80,512]{1,0:T(8,128)(2,1)S(1)}, u32[]{:S(2)}, u32[]{:S(2)}) collective-permute-start(bf16[80,512]{1,0:T(8,128)(2,1)S(1)} %constant_dynamic-update-slice_fusion.1), channel_id=1, source_target_pairs={{0,2},{1,3},{2,0},{3,1},{4,6},{5,7},{6,4},{7,5},{8,10},{9,11},{10,... | collective-permute-start | bytes 245768 | tf_op jit(solution)/shard_map/ppermute | solution.py:29
  10.2 9.9 %collective-permute-start.1 = (bf16[80,512]{1,0:T(8,128)(2,1)S(1)}, bf16[80,512]{1,0:T(8,128)(2,1)S(1)}, u32[]{:S(2)}, u32[]{:S(2)}) collective-permute-start(bf16[80,512]{1,0:T(8,128)(2,1)S(1)} %constant_dynamic-update-slice_fusion.1), channel_id=1, source_target_pairs={{0,1},{1,0},{2,3},{3,2},{4,5},{5,4},{6,7},{7,6},{8,9},{9,8},{10,11... | collective-permute-start | bytes 245768 | tf_op jit(solution)/shard_map/ppermute | solution.py:29
  13.5 10.6 %collective-permute-start.13 = (bf16[128,512]{1,0:T(8,128)(2,1)S(1)}, bf16[128,512]{1,0:T(8,128)(2,1)S(1)}, u32[]{:S(2)}, u32[]{:S(2)}) collective-permute-start(bf16[128,512]{1,0:T(8,128)(2,1)S(1)} %get-tuple-element.256), channel_id=1, source_target_pairs={{0,2},{1,3},{2,0},{3,1},{4,6},{5,7},{6,4},{7,5},{8,10},{9,11},{10,... | collective-permute-start | bytes 393224 | tf_op jit(solution)/shard_map/ppermute | solution.py:29
  15.7 13.6 %collective-permute-start = (bf16[512,512]{1,0:T(8,128)(2,1)S(1)}, bf16[512,512]{1,0:T(8,128)(2,1)}, u32[]{:S(2)}, u32[]{:S(2)}) collective-permute-start(bf16[512,512]{1,0:T(8,128)(2,1)S(1)} %copy-done.38), channel_id=1, source_target_pairs={{1,4},{3,6},{4,1},{6,3},{9,12},{11,14},{12,9},{14,11},{17,20},{19,... | collective-permute-start | bytes 1572872 | tf_op jit(solution)/shard_map/ppermute | solution.py:42
  20.3 10.1 %collective-permute-start.6 = (bf16[4,64,512]{2,1,0:T(8,128)(2,1)S(1)}, bf16[4,64,512]{2,1,0:T(8,128)(2,1)S(1)}, u32[]{:S(2)}, u32[]{:S(2)}) collective-permute-start(bf16[4,64,512]{2,1,0:T(8,128)(2,1)S(1)} %slice.296.refs_0_), channel_id=1, source_target_pairs={{0,24},{4,28},{8,16},{12,20},{16,8},{20,12},{24,0},{28,4},{1,25},{... | collective-permute-start | bytes 786440 | tf_op jit(solution)/shard_map/ppermute | solution.py:24
  22.5 11.4 %collective-permute-start.5 = (bf16[4,64,512]{2,1,0:T(8,128)(2,1)S(1)}, bf16[4,64,512]{2,1,0:T(8,128)(2,1)S(1)}, u32[]{:S(2)}, u32[]{:S(2)}) collective-permute-start(bf16[4,64,512]{2,1,0:T(8,128)(2,1)S(1)} %slice.296.refs_0_), channel_id=1, source_target_pairs={{0,16},{4,20},{8,24},{12,28},{16,0},{20,4},{24,8},{28,12},{1,17},{... | collective-permute-start | bytes 786440 | tf_op jit(solution)/shard_map/ppermute | solution.py:24
  22.7 11.2 %collective-permute-start.4 = (bf16[4,64,512]{2,1,0:T(8,128)(2,1)S(1)}, bf16[4,64,512]{2,1,0:T(8,128)(2,1)S(1)}, u32[]{:S(2)}, u32[]{:S(2)}) collective-permute-start(bf16[4,64,512]{2,1,0:T(8,128)(2,1)S(1)} %slice.296.refs_0_), channel_id=1, source_target_pairs={{0,8},{4,12},{8,0},{12,4},{16,24},{20,28},{24,16},{28,20},{1,9},{5... | collective-permute-start | bytes 786440 | tf_op jit(solution)/shard_map/ppermute | solution.py:24
  24.9 11.6 %collective-permute-start.14 = (bf16[2,128,512]{2,1,0:T(8,128)(2,1)}, bf16[2,128,512]{2,1,0:T(8,128)(2,1)S(1)}, u32[]{:S(2)}, u32[]{:S(2)}) collective-permute-start(bf16[2,128,512]{2,1,0:T(8,128)(2,1)} %pad_maximum_fusion.4), channel_id=1, source_target_pairs={{0,1},{1,0},{2,3},{3,2},{4,5},{5,4},{6,7},{7,6},{8,9},{9,8},{10,11... | collective-permute-start | bytes 786440 | tf_op jit(solution)/shard_map/ppermute | solution.py:29
  38.5 27.1 %collective-permute-start.17 = (bf16[4,128,512]{2,1,0:T(8,128)(2,1)S(1)}, bf16[4,128,512]{2,1,0:T(8,128)(2,1)S(1)}, u32[]{:S(2)}, u32[]{:S(2)}) collective-permute-start(bf16[4,128,512]{2,1,0:T(8,128)(2,1)S(1)} %pad_maximum_fusion.2.refs_0_), channel_id=1, source_target_pairs={{0,24},{4,28},{8,16},{12,20},{16,8},{20,12},{24,0},{28,4},{1,25},{... | collective-permute-start | bytes 1572872 | tf_op jit(solution)/shard_map/ppermute | solution.py:24
  40.1 25.5 %collective-permute-start.16 = (bf16[4,128,512]{2,1,0:T(8,128)(2,1)S(1)}, bf16[4,128,512]{2,1,0:T(8,128)(2,1)}, u32[]{:S(2)}, u32[]{:S(2)}) collective-permute-start(bf16[4,128,512]{2,1,0:T(8,128)(2,1)S(1)} %pad_maximum_fusion.2.refs_0_), channel_id=1, source_target_pairs={{0,16},{4,20},{8,24},{12,28},{16,0},{20,4},{24,8},{28,12},{1,17},{... | collective-permute-start | bytes 1572872 | tf_op jit(solution)/shard_map/ppermute | solution.py:24
  40.8 24.8 %collective-permute-start.15 = (bf16[4,128,512]{2,1,0:T(8,128)(2,1)S(1)}, bf16[4,128,512]{2,1,0:T(8,128)(2,1)}, u32[]{:S(2)}, u32[]{:S(2)}) collective-permute-start(bf16[4,128,512]{2,1,0:T(8,128)(2,1)S(1)} %pad_maximum_fusion.2.refs_0_), channel_id=1, source_target_pairs={{0,8},{4,12},{8,0},{12,4},{16,24},{20,28},{24,16},{28,20},{1,9},{5... | collective-permute-start | bytes 1572872 | tf_op jit(solution)/shard_map/ppermute | solution.py:24
  67.5 13.9 %collective-permute-start.22 = (bf16[512,512]{1,0:T(8,128)(2,1)}, bf16[512,512]{1,0:T(8,128)(2,1)S(1)}, u32[]{:S(2)}, u32[]{:S(2)}) collective-permute-start(bf16[512,512]{1,0:T(8,128)(2,1)} %param.35), channel_id=1, source_target_pairs={{1,4},{3,6},{4,1},{6,3},{9,12},{11,14},{12,9},{14,11},{17,20},{19,... | collective-permute-start | bytes 1572872 | tf_op jit(solution)/shard_map/ppermute | solution.py:42
  107.9 18.4 %collective-permute-start.24 = (bf16[512,512]{1,0:T(8,128)(2,1)S(1)}, bf16[512,512]{1,0:T(8,128)(2,1)S(1)}, u32[]{:S(2)}, u32[]{:S(2)}) collective-permute-start(bf16[512,512]{1,0:T(8,128)(2,1)S(1)} %get-tuple-element.153), channel_id=1, source_target_pairs={{1,4},{3,6},{4,1},{6,3},{9,12},{11,14},{12,9},{14,11},{17,20},{19,... | collective-permute-start | bytes 1572872 | tf_op jit(solution)/shard_map/ppermute | solution.py:42
  140.7 18.0 %collective-permute-start.27 = (bf16[2,2,144,512]{3,2,1,0:T(8,128)(2,1)S(1)}, bf16[2,2,144,512]{3,2,1,0:T(8,128)(2,1)S(1)}, u32[]{:S(2)}, u32[]{:S(2)}) collective-permute-start(bf16[2,2,144,512]{3,2,1,0:T(8,128)(2,1)S(1)} %pad_maximum_fusion), channel_id=1, source_target_pairs={{0,8},{4,12},{8,0},{12,4},{16,24},{20,28},{24,16},{28,20},{1,9},{5... | collective-permute-start | bytes 1769480 | tf_op jit(solution)/shard_map/ppermute | solution.py:24
  142.0 16.7 %collective-permute-start.28 = (bf16[2,2,144,512]{3,2,1,0:T(8,128)(2,1)S(1)}, bf16[2,2,144,512]{3,2,1,0:T(8,128)(2,1)S(1)}, u32[]{:S(2)}, u32[]{:S(2)}) collective-permute-start(bf16[2,2,144,512]{3,2,1,0:T(8,128)(2,1)S(1)} %pad_maximum_fusion.1), channel_id=1, source_target_pairs={{0,16},{4,20},{8,24},{12,28},{16,0},{20,4},{24,8},{28,12},{1,17},{... | collective-permute-start | bytes 1769480 | tf_op jit(solution)/shard_map/ppermute | solution.py:24
  163.3 11.4 %collective-permute-start.35 = (bf16[2,2,64,512]{3,2,1,0:T(8,128)(2,1)S(1)}, bf16[2,2,64,512]{3,2,1,0:T(8,128)(2,1)S(1)}, u32[]{:S(2)}, u32[]{:S(2)}) collective-permute-start(bf16[2,2,64,512]{3,2,1,0:T(8,128)(2,1)S(1)} %pad_maximum_fusion.5), channel_id=1, source_target_pairs={{0,8},{4,12},{8,0},{12,4},{16,24},{20,28},{24,16},{28,20},{1,9},{5... | collective-permute-start | bytes 786440 | tf_op jit(solution)/shard_map/ppermute | solution.py:24
  164.3 10.4 %collective-permute-start.36 = (bf16[2,2,64,512]{3,2,1,0:T(8,128)(2,1)S(1)}, bf16[2,2,64,512]{3,2,1,0:T(8,128)(2,1)S(1)}, u32[]{:S(2)}, u32[]{:S(2)}) collective-permute-start(bf16[2,2,64,512]{3,2,1,0:T(8,128)(2,1)S(1)} %pad_maximum_fusion.6), channel_id=1, source_target_pairs={{0,16},{4,20},{8,24},{12,28},{16,0},{20,4},{24,8},{28,12},{1,17},{... | collective-permute-start | bytes 786440 | tf_op jit(solution)/shard_map/ppermute | solution.py:24
  168.6 11.4 %collective-permute-start.30 = (bf16[144,512]{1,0:T(8,128)(2,1)S(1)}, bf16[144,512]{1,0:T(8,128)(2,1)S(1)}, u32[]{:S(2)}, u32[]{:S(2)}) collective-permute-start(bf16[144,512]{1,0:T(8,128)(2,1)S(1)} %get-tuple-element.249), channel_id=1, source_target_pairs={{0,1},{1,0},{2,3},{3,2},{4,5},{5,4},{6,7},{7,6},{8,9},{9,8},{10,11... | collective-permute-start | bytes 442376 | tf_op jit(solution)/shard_map/ppermute | solution.py:29
  170.0 10.0 %collective-permute-start.33 = (bf16[144,512]{1,0:T(8,128)(2,1)S(1)}, bf16[144,512]{1,0:T(8,128)(2,1)S(1)}, u32[]{:S(2)}, u32[]{:S(2)}) collective-permute-start(bf16[144,512]{1,0:T(8,128)(2,1)S(1)} %get-tuple-element.247), channel_id=1, source_target_pairs={{0,3},{1,2},{2,1},{3,0},{4,7},{5,6},{6,5},{7,4},{8,11},{9,10},{10,... | collective-permute-start | bytes 442376 | tf_op jit(solution)/shard_map/ppermute | solution.py:29
  170.2 12.9 %collective-permute-start.32 = (bf16[144,512]{1,0:T(8,128)(2,1)S(1)}, bf16[144,512]{1,0:T(8,128)(2,1)S(1)}, u32[]{:S(2)}, u32[]{:S(2)}) collective-permute-start(bf16[144,512]{1,0:T(8,128)(2,1)S(1)} %get-tuple-element.248), channel_id=1, source_target_pairs={{0,2},{1,3},{2,0},{3,1},{4,6},{5,7},{6,4},{7,5},{8,10},{9,11},{10,... | collective-permute-start | bytes 442376 | tf_op jit(solution)/shard_map/ppermute | solution.py:29
  188.7 13.4 %collective-permute-start.45 = (bf16[512,512]{1,0:T(8,128)(2,1)S(1)}, bf16[512,512]{1,0:T(8,128)(2,1)S(1)}, u32[]{:S(2)}, u32[]{:S(2)}) collective-permute-start(bf16[512,512]{1,0:T(8,128)(2,1)S(1)} %fusion), channel_id=1, source_target_pairs={{1,4},{3,6},{4,1},{6,3},{9,12},{11,14},{12,9},{14,11},{17,20},{19,... | collective-permute-start | bytes 1572872 | tf_op jit(solution)/shard_map/ppermute | solution.py:42
  195.9 10.2 %collective-permute-start.43 = (bf16[208,512]{1,0:T(8,128)(2,1)S(1)}, bf16[208,512]{1,0:T(8,128)(2,1)S(1)}, u32[]{:S(2)}, u32[]{:S(2)}) collective-permute-start(bf16[208,512]{1,0:T(8,128)(2,1)S(1)} %pad_maximum_fusion.7.refs_0_), channel_id=1, source_target_pairs={{0,16},{4,20},{8,24},{12,28},{16,0},{20,4},{24,8},{28,12},{1,17},{... | collective-permute-start | bytes 638984 | tf_op jit(solution)/shard_map/ppermute | solution.py:24
  197.0 9.1 %collective-permute-start.42 = (bf16[208,512]{1,0:T(8,128)(2,1)S(1)}, bf16[208,512]{1,0:T(8,128)(2,1)S(1)}, u32[]{:S(2)}, u32[]{:S(2)}) collective-permute-start(bf16[208,512]{1,0:T(8,128)(2,1)S(1)} %pad_maximum_fusion.7.refs_0_), channel_id=1, source_target_pairs={{0,8},{4,12},{8,0},{12,4},{16,24},{20,28},{24,16},{28,20},{1,9},{5... | collective-permute-start | bytes 638984 | tf_op jit(solution)/shard_map/ppermute | solution.py:24
  (73 other events, 393.5 us)

commit v6 on v5

--- a/solution.py
+++ b/solution.py
@@ -556,7 +556,11 @@
         return lax.dynamic_slice_in_dim(weight, eighth * count, count, 0)
 
     first_in = regroup(inputs)
-    flat = jnp.concatenate((query_bias, value_bias, up_bias))
+    flat = (
+        jnp.pad(query_bias, (0, shard_heads + shard_units))
+        + jnp.pad(value_bias, (shard_heads, shard_units))
+        + jnp.pad(up_bias, (2 * shard_heads, 0))
+    )
     top = lax.reduce_precision(flat, 8, 7)
     mid = lax.reduce_precision(flat - top, 8, 7)
     flat = jnp.concatenate((top, mid, flat - top - mid)).astype(LOW)

time: 216 us -> 214 us (level)
    unnamed x103 -> x101, local copies, waits for them, and re-layouts: 21.3 us -> 19.9 us
  transfers between devices with their start and end apart: 50 -> 50, of which waited for: 16 -> 16; matrix products, arithmetic and copies ran while one was open for 5% -> 5% of each run, Pallas kernels for 24% -> 25%
where the time goes in v6:
time: 214 us; the launch traced here: 210 us
  Pallas kernels  85.8 us (40%)
  starting transfers between devices  49.9 us (23%)
  waiting for transfers between devices  37.3 us (17%)
  local copies, waits for them, and re-layouts  28.1 us (13%)
  other arithmetic  7.47 us (3%)
    pallas_call x11, Pallas kernels, call(): pl.pallas_call(kernel, in_specs=[pl.BlockSpec(memory_space=space) for spa...  85.8 us
    ppermute x35, waiting for transfers between devices, swap_dp(): return lax.ppermute(value, 'dp', [(i, i ^ bits) for i in range(count)])  22.7 us
    ppermute x35, starting transfers between devices, swap_dp(): return lax.ppermute(value, 'dp', [(i, i ^ bits) for i in range(count)])  21.2 us
    unnamed x101, local copies, waits for them, and re-layouts  19.9 us
    ppermute x4, starting transfers between devices, regroup(): moved = lax.ppermute(block, ('dp', 'tensor'), pairs)  15.6 us
    ppermute x11, starting transfers between devices, swap_tensor(): return lax.ppermute(value, 'tensor', [(i, i ^ step) for i in range(count)])  13.1 us
    ppermute x4, waiting for transfers between devices, regroup(): moved = lax.ppermute(block, ('dp', 'tensor'), pairs)  8.83 us
    ppermute x11, waiting for transfers between devices, swap_tensor(): return lax.ppermute(value, 'tensor', [(i, i ^ step) for i in range(count)])  5.73 us
  transfers between devices with their start and end apart: 50, of which 16 were waited for; matrix products, arithmetic and copies ran while one was open for 5% of the time, Pallas kernels for 25%

profile of v6, /device:TPU:1, one launch (start us, length us, event | category | flops | bytes accessed | tf_op | source)
XLA Modules:
  0.0 210.3 jit_solution(8071911249074149896)
XLA Ops:
  4.7 4.2 %collective-permute-start.3 = (bf16[80,512]{1,0:T(8,128)(2,1)S(1)}, bf16[80,512]{1,0:T(8,128)(2,1)S(1)}, u32[]{:S(2)}, u32[]{:S(2)}) collective-permute-start(bf16[80,512]{1,0:T(8,128)(2,1)S(1)} %constant_dynamic-update-slice_fusion), channel_id=1, source_target_pairs={{0,3},{1,2},{2,1},{3,0},{4,7},{5,6},{6,5},{7,4},{8,11},{9,10},{10,... | collective-permute-start | bytes 245768 | tf_op jit(solution)/shard_map/ppermute | solution.py:29
  14.4 3.8 %collective-permute-start = (bf16[512,512]{1,0:T(8,128)(2,1)S(1)}, bf16[512,512]{1,0:T(8,128)(2,1)}, u32[]{:S(2)}, u32[]{:S(2)}) collective-permute-start(bf16[512,512]{1,0:T(8,128)(2,1)S(1)} %copy-done.38), channel_id=1, source_target_pairs={{1,4},{3,6},{4,1},{6,3},{9,12},{11,14},{12,9},{14,11},{17,20},{19,... | collective-permute-start | bytes 1572872 | tf_op jit(solution)/shard_map/ppermute | solution.py:42
  23.6 4.4 %collective-permute-done = bf16[512,512]{1,0:T(8,128)(2,1)} collective-permute-done((bf16[512,512]{1,0:T(8,128)(2,1)S(1)}, bf16[512,512]{1,0:T(8,128)(2,1)}, u32[]{:S(2)}, u32[]{:S(2)}) %collective-permute-start) | collective-permute-done | bytes 524320 | tf_op jit(solution)/shard_map/ppermute | solution.py:42
  29.1 3.5 %collective-permute-done.5.refs_2_ = bf16[4,64,512]{2,1,0:T(8,128)(2,1)S(1)} collective-permute-done((bf16[4,64,512]{2,1,0:T(8,128)(2,1)S(1)}, bf16[4,64,512]{2,1,0:T(8,128)(2,1)S(1)}, u32[]{:S(2)}, u32[]{:S(2)}) %collective-permute-start.5) | collective-permute-done | bytes 262176 | tf_op jit(solution)/shard_map/ppermute | solution.py:24
  42.6 9.7 %attention_first.1 = (bf16[512,512]{1,0:T(8,128)(2,1)S(1)}, bf16[1024,512]{1,0:T(8,128)(2,1)S(1)}, bf16[1024,512]{1,0:T(8,128)(2,1)S(1)}, bf16[8,512,1024]{2,1,0...) custom-call(bf16[4,64,512]{2,1,0:T(8,128)(2,1)S(1)} %slice.296.refs_, ...), custom_call_target="tpu_custom_call" | custom-call | flops 9900000256 | tf_op jit(solution)/shard_map/attention_first/pallas_call | solution.py:140
  54.5 3.3 %copy-done.20 = bf16[8,512,1024]{2,1,0:T(8,128)(2,1)} copy-done((bf16[8,512,1024]{2,1,0:T(8,128)(2,1)}, bf16[8,512,1024]{2,1,0:T(8,128)(2,1)S(1)}, u32[]{:S(2)}) %copy-start.20) | copy-done | bytes 8388632
  66.2 2.8 %collective-permute-start.22 = (bf16[512,512]{1,0:T(8,128)(2,1)}, bf16[512,512]{1,0:T(8,128)(2,1)S(1)}, u32[]{:S(2)}, u32[]{:S(2)}) collective-permute-start(bf16[512,512]{1,0:T(8,128)(2,1)} %param.35), channel_id=1, source_target_pairs={{1,4},{3,6},{4,1},{6,3},{9,12},{11,14},{12,9},{14,11},{17,20},{19,... | collective-permute-start | bytes 1572872 | tf_op jit(solution)/shard_map/ppermute | solution.py:42
  72.8 6.8 %ffn_first.1 = (bf16[512,512]{1,0:T(8,128)(2,1)S(1)}, bf16[512,2048]{1,0:T(8,128)(2,1)S(1)}, bf16[512,2048]{1,0:T(8,128)(2,1)S(1)}, f32[512,512]{1,0:T(8,128)S(1...) custom-call(bf16[4,128,512]{2,1,0:T(8,128)(2,1)S(1)} %pad_maximum_fu, ...), custom_call_target="tpu_custom_call" | custom-call | flops 6600000000 | tf_op jit(solution)/shard_map/ffn_first/pallas_call | solution.py:140
  81.6 8.5 %attention_forward.1 = (bf16[512,512]{1,0:T(8,128)(2,1)S(1)}, bf16[1024,512]{1,0:T(8,128)(2,1)S(1)}, bf16[1024,512]{1,0:T(8,128)(2,1)S(1)}, bf16[8,512,1024]{2,1...) custom-call(f32[512,512]{1,0:T(8,128)S(1)} %get-tuple-element.135.in, ...), custom_call_target="tpu_custom_call" | custom-call | flops 8800000000 | tf_op jit(solution)/shard_map/attention_forward/pallas_call | solution.py:140
  90.2 16.4 %ffn_forward.1 = (bf16[512,512]{1,0:T(8,128)(2,1)S(1)}, bf16[512,2048]{1,0:T(8,128)(2,1)S(1)}, bf16[512,2048]{1,0:T(8,128)(2,1)S(1)}, f32[512,512]{1,0:T(8,128)S...) custom-call(f32[512,512]{1,0:T(8,128)S(1)} %get-tuple-element.138.mid_ref, ...), custom_call_target="tpu_custom_call" | custom-call | flops 5500000256 | tf_op jit(solution)/shard_map/ffn_forward/pallas_call | solution.py:140
  106.6 2.7 %collective-permute-start.24 = (bf16[512,512]{1,0:T(8,128)(2,1)S(1)}, bf16[512,512]{1,0:T(8,128)(2,1)S(1)}, u32[]{:S(2)}, u32[]{:S(2)}) collective-permute-start(bf16[512,512]{1,0:T(8,128)(2,1)S(1)} %get-tuple-element.153), channel_id=1, source_target_pairs={{1,4},{3,6},{4,1},{6,3},{9,12},{11,14},{12,9},{14,11},{17,20},{19,... | collective-permute-start | bytes 1572872 | tf_op jit(solution)/shard_map/ppermute | solution.py:42
  109.3 3.7 %ffn_backward.2 = (bf16[512,512]{1,0:T(8,128)(2,1)S(1)}, bf16[512,2048]{1,0:T(8,128)(2,1)S(1)}, f32[512,512]{1,0:T(8,128)S(1)}, bf16[512,512]{1,0:T(8,128)(2,1)S...) custom-call(bf16[2,8,4,64,512]{4,3,2,1,0:T(8,128)(2,1)S(1)} %get-tuple-element.133.w_ref, ...), custom_call_target="tpu_custom_call" | custom-call | flops 5500000256 | tf_op jit(solution)/shard_map/ffn_backward/pallas_call | solution.py:140
  113.0 11.9 %attention_backward.1 = (f32[512,512]{1,0:T(8,128)S(1)}, bf16[512,512]{1,0:T(8,128)(2,1)S(1)}, bf16[512,512]{1,0:T(8,128)(2,1)S(1)}, bf16[1024,512]{1,0:T(8,128)(2,1)S(1)}, bf16[1024,512]{1,0:T(8,128)(2,1)S(1)}) custom-call(bf16[512,512]{1,0:T(8,128)(2,1)S(1)} %get-tuple-element.144.att_ref, f32[512,512]{1,0:T(8,128)S(1)} %get-tuple-element.145.pre_ref, ...), custom_call_target="tpu_custom_call" | custom-call | flops 13200000000 | tf_op jit(solution)/shard_map/attention_backward/pallas_call | solution.py:140
  127.1 3.6 %ffn_backward.3 = (bf16[512,512]{1,0:T(8,128)(2,1)S(1)}, bf16[512,2048]{1,0:T(8,128)(2,1)S(1)}, f32[512,512]{1,0:T(8,128)S(1)}, bf16[512,512]{1,0:T(8,128)(2,1)S...) custom-call(bf16[2,8,4,64,512]{4,3,2,1,0:T(8,128)(2,1)S(1)} %get-tuple-element.133.w_ref, ...), custom_call_target="tpu_custom_call" | custom-call | flops 5500000256 | tf_op jit(solution)/shard_map/ffn_backward/pallas_call | solution.py:140
  130.7 3.5 %ffn_grads.3 = (bf16[4,4,144,512]{3,2,1,0:T(8,128)(2,1)S(1)}, bf16[1024,128]{1,0:T(8,128)(2,1)S(1)}) custom-call(bf16[512,2048]{1,0:T(8,128)(2,1)S(1)} %get-tuple-element.155.refs_0_, bf16[512,2048]{1,0:T(8,128)(2,1)S(1)} %get-tuple-element.156.refs_1_, bf16[512,512]{1,0:T(8,128)(2,1)S(1)} %get-tuple-element.157.refs_2_, ...), custom_call_target="tpu_custom_call" | custom-call | flops 3300000000 | tf_op jit(solution)/shard_map/ffn_grads/pallas_call | solution.py:140
  134.4 3.5 %ffn_grads.2 = (bf16[4,4,144,512]{3,2,1,0:T(8,128)(2,1)S(1)}, bf16[1024,128]{1,0:T(8,128)(2,1)S(1)}) custom-call(bf16[512,2048]{1,0:T(8,128)(2,1)S(1)} %get-tuple-element.155.refs_0_, bf16[512,2048]{1,0:T(8,128)(2,1)S(1)} %get-tuple-element.156.refs_1_, bf16[512,512]{1,0:T(8,128)(2,1)S(1)} %get-tuple-element.157.refs_2_, ...), custom_call_target="tpu_custom_call" | custom-call | flops 3300000000 | tf_op jit(solution)/shard_map/ffn_grads/pallas_call | solution.py:140
  141.3 16.0 %last_backward.1 = (f32[512,512]{1,0:T(8,128)S(1)}, bf16[4,4,64,512]{3,2,1,0:T(8,128)(2,1)S(1)}, bf16[24,64,512]{2,1,0:T(8,128)(2,1)S(1)}) custom-call(s32[1]{0:T(128)} %bitcast.19.eighth_ref, bf16[512,512]{1,0:T(8,128)(2,1)S(1)} %get-tuple-element.177.refs_0_, f32[512,512]{1,0:T(8,128)S(1)} %get-tuple-element.178.refs_1_, bf16[512,512]{1,0:T(8,128)(2,1)S(1)} %copy-done.36, ...), custom_call_target="tpu_custom_call" | custom-call | flops 17600000000 | tf_op jit(solution)/shard_map/last_backward/pallas_call | solution.py:140
  163.6 3.7 %collective-permute-done.29 = bf16[2,144,512]{2,1,0:T(8,128)(2,1)S(1)} collective-permute-done((bf16[2,144,512]{2,1,0:T(8,128)(2,1)S(1)}, bf16[2,144,512]{2,1,0:T(8,128)(2,1)S(1)}, u32[]{:S(2)}, u32[]{:S(2)}) %collective-permute-start.29) | collective-permute-done | bytes 294944 | tf_op jit(solution)/shard_map/ppermute | solution.py:24
  170.2 3.2 %collective-permute-done.35 = bf16[2,2,64,512]{3,2,1,0:T(8,128)(2,1)S(1)} collective-permute-done((bf16[2,2,64,512]{3,2,1,0:T(8,128)(2,1)S(1)}, bf16[2,2,64,512]{3,2,1,0:T(8,128)(2,1)S(1)}, u32[]{:S(2)}, u32[]{:S(2)}) %collective-permute-start.35) | collective-permute-done | bytes 262176 | tf_op jit(solution)/shard_map/ppermute | solution.py:24
  178.7 3.1 %collective-permute-done.32 = bf16[144,512]{1,0:T(8,128)(2,1)S(1)} collective-permute-done((bf16[144,512]{1,0:T(8,128)(2,1)S(1)}, bf16[144,512]{1,0:T(8,128)(2,1)S(1)}, u32[]{:S(2)}, u32[]{:S(2)}) %collective-permute-start.32) | collective-permute-done | bytes 147488 | tf_op jit(solution)/shard_map/ppermute | solution.py:29
  181.9 2.7 %collective-permute-start.41 = (bf16[64,512]{1,0:T(8,128)(2,1)S(1)}, bf16[64,512]{1,0:T(8,128)(2,1)S(1)}, u32[]{:S(2)}, u32[]{:S(2)}) collective-permute-start(bf16[64,512]{1,0:T(8,128)(2,1)S(1)} %get-tuple-element.252), channel_id=1, source_target_pairs={{0,3},{1,2},{2,1},{3,0},{4,7},{5,6},{6,5},{7,4},{8,11},{9,10},{10,... | collective-permute-start | bytes 196616 | tf_op jit(solution)/shard_map/ppermute | solution.py:29
  187.4 6.3 %collective-permute-start.45 = (bf16[512,512]{1,0:T(8,128)(2,1)S(1)}, bf16[512,512]{1,0:T(8,128)(2,1)S(1)}, u32[]{:S(2)}, u32[]{:S(2)}) collective-permute-start(bf16[512,512]{1,0:T(8,128)(2,1)S(1)} %fusion), channel_id=1, source_target_pairs={{1,4},{3,6},{4,1},{6,3},{9,12},{11,14},{12,9},{14,11},{17,20},{19,... | collective-permute-start | bytes 1572872 | tf_op jit(solution)/shard_map/ppermute | solution.py:42
  196.4 4.4 %collective-permute-done.45 = bf16[512,512]{1,0:T(8,128)(2,1)S(1)} collective-permute-done((bf16[512,512]{1,0:T(8,128)(2,1)S(1)}, bf16[512,512]{1,0:T(8,128)(2,1)S(1)}, u32[]{:S(2)}, u32[]{:S(2)}) %collective-permute-start.45) | collective-permute-done | bytes 524320 | tf_op jit(solution)/shard_map/ppermute | solution.py:42
  201.8 3.1 %collective-permute-done.43.refs_2_ = bf16[208,512]{1,0:T(8,128)(2,1)S(1)} collective-permute-done((bf16[208,512]{1,0:T(8,128)(2,1)S(1)}, bf16[208,512]{1,0:T(8,128)(2,1)S(1)}, u32[]{:S(2)}, u32[]{:S(2)}) %collective-permute-start.43) | collective-permute-done | bytes 213024 | tf_op jit(solution)/shard_map/ppermute | solution.py:24
  (260 shorter events, 73.7 us)
Async XLA Ops:
  4.7 14.0 %collective-permute-start.3 = (bf16[80,512]{1,0:T(8,128)(2,1)S(1)}, bf16[80,512]{1,0:T(8,128)(2,1)S(1)}, u32[]{:S(2)}, u32[]{:S(2)}) collective-permute-start(bf16[80,512]{1,0:T(8,128)(2,1)S(1)} %constant_dynamic-update-slice_fusion), channel_id=1, source_target_pairs={{0,3},{1,2},{2,1},{3,0},{4,7},{5,6},{6,5},{7,4},{8,11},{9,10},{10,... | collective-permute-start | bytes 245768 | tf_op jit(solution)/shard_map/ppermute | solution.py:29
  8.8 9.8 %collective-permute-start.2 = (bf16[80,512]{1,0:T(8,128)(2,1)S(1)}, bf16[80,512]{1,0:T(8,128)(2,1)S(1)}, u32[]{:S(2)}, u32[]{:S(2)}) collective-permute-start(bf16[80,512]{1,0:T(8,128)(2,1)S(1)} %constant_dynamic-update-slice_fusion), channel_id=1, source_target_pairs={{0,2},{1,3},{2,0},{3,1},{4,6},{5,7},{6,4},{7,5},{8,10},{9,11},{10,... | collective-permute-start | bytes 245768 | tf_op jit(solution)/shard_map/ppermute | solution.py:29
  8.9 9.9 %collective-permute-start.1 = (bf16[80,512]{1,0:T(8,128)(2,1)S(1)}, bf16[80,512]{1,0:T(8,128)(2,1)S(1)}, u32[]{:S(2)}, u32[]{:S(2)}) collective-permute-start(bf16[80,512]{1,0:T(8,128)(2,1)S(1)} %constant_dynamic-update-slice_fusion), channel_id=1, source_target_pairs={{0,1},{1,0},{2,3},{3,2},{4,5},{5,4},{6,7},{7,6},{8,9},{9,8},{10,11... | collective-permute-start | bytes 245768 | tf_op jit(solution)/shard_map/ppermute | solution.py:29
  12.2 10.6 %collective-permute-start.13 = (bf16[128,512]{1,0:T(8,128)(2,1)S(1)}, bf16[128,512]{1,0:T(8,128)(2,1)S(1)}, u32[]{:S(2)}, u32[]{:S(2)}) collective-permute-start(bf16[128,512]{1,0:T(8,128)(2,1)S(1)} %get-tuple-element.256), channel_id=1, source_target_pairs={{0,2},{1,3},{2,0},{3,1},{4,6},{5,7},{6,4},{7,5},{8,10},{9,11},{10,... | collective-permute-start | bytes 393224 | tf_op jit(solution)/shard_map/ppermute | solution.py:29
  14.4 13.6 %collective-permute-start = (bf16[512,512]{1,0:T(8,128)(2,1)S(1)}, bf16[512,512]{1,0:T(8,128)(2,1)}, u32[]{:S(2)}, u32[]{:S(2)}) collective-permute-start(bf16[512,512]{1,0:T(8,128)(2,1)S(1)} %copy-done.38), channel_id=1, source_target_pairs={{1,4},{3,6},{4,1},{6,3},{9,12},{11,14},{12,9},{14,11},{17,20},{19,... | collective-permute-start | bytes 1572872 | tf_op jit(solution)/shard_map/ppermute | solution.py:42
  19.0 10.1 %collective-permute-start.6 = (bf16[4,64,512]{2,1,0:T(8,128)(2,1)S(1)}, bf16[4,64,512]{2,1,0:T(8,128)(2,1)S(1)}, u32[]{:S(2)}, u32[]{:S(2)}) collective-permute-start(bf16[4,64,512]{2,1,0:T(8,128)(2,1)S(1)} %slice.296.refs_0_), channel_id=1, source_target_pairs={{0,24},{4,28},{8,16},{12,20},{16,8},{20,12},{24,0},{28,4},{1,25},{... | collective-permute-start | bytes 786440 | tf_op jit(solution)/shard_map/ppermute | solution.py:24
  21.2 11.4 %collective-permute-start.5 = (bf16[4,64,512]{2,1,0:T(8,128)(2,1)S(1)}, bf16[4,64,512]{2,1,0:T(8,128)(2,1)S(1)}, u32[]{:S(2)}, u32[]{:S(2)}) collective-permute-start(bf16[4,64,512]{2,1,0:T(8,128)(2,1)S(1)} %slice.296.refs_0_), channel_id=1, source_target_pairs={{0,16},{4,20},{8,24},{12,28},{16,0},{20,4},{24,8},{28,12},{1,17},{... | collective-permute-start | bytes 786440 | tf_op jit(solution)/shard_map/ppermute | solution.py:24
  21.4 11.2 %collective-permute-start.4 = (bf16[4,64,512]{2,1,0:T(8,128)(2,1)S(1)}, bf16[4,64,512]{2,1,0:T(8,128)(2,1)S(1)}, u32[]{:S(2)}, u32[]{:S(2)}) collective-permute-start(bf16[4,64,512]{2,1,0:T(8,128)(2,1)S(1)} %slice.296.refs_0_), channel_id=1, source_target_pairs={{0,8},{4,12},{8,0},{12,4},{16,24},{20,28},{24,16},{28,20},{1,9},{5... | collective-permute-start | bytes 786440 | tf_op jit(solution)/shard_map/ppermute | solution.py:24
  23.6 11.6 %collective-permute-start.14 = (bf16[2,128,512]{2,1,0:T(8,128)(2,1)}, bf16[2,128,512]{2,1,0:T(8,128)(2,1)S(1)}, u32[]{:S(2)}, u32[]{:S(2)}) collective-permute-start(bf16[2,128,512]{2,1,0:T(8,128)(2,1)} %pad_maximum_fusion.4), channel_id=1, source_target_pairs={{0,1},{1,0},{2,3},{3,2},{4,5},{5,4},{6,7},{7,6},{8,9},{9,8},{10,11... | collective-permute-start | bytes 786440 | tf_op jit(solution)/shard_map/ppermute | solution.py:29
  37.2 27.1 %collective-permute-start.17 = (bf16[4,128,512]{2,1,0:T(8,128)(2,1)S(1)}, bf16[4,128,512]{2,1,0:T(8,128)(2,1)S(1)}, u32[]{:S(2)}, u32[]{:S(2)}) collective-permute-start(bf16[4,128,512]{2,1,0:T(8,128)(2,1)S(1)} %pad_maximum_fusion.2.refs_0_), channel_id=1, source_target_pairs={{0,24},{4,28},{8,16},{12,20},{16,8},{20,12},{24,0},{28,4},{1,25},{... | collective-permute-start | bytes 1572872 | tf_op jit(solution)/shard_map/ppermute | solution.py:24
  38.8 25.5 %collective-permute-start.16 = (bf16[4,128,512]{2,1,0:T(8,128)(2,1)S(1)}, bf16[4,128,512]{2,1,0:T(8,128)(2,1)}, u32[]{:S(2)}, u32[]{:S(2)}) collective-permute-start(bf16[4,128,512]{2,1,0:T(8,128)(2,1)S(1)} %pad_maximum_fusion.2.refs_0_), channel_id=1, source_target_pairs={{0,16},{4,20},{8,24},{12,28},{16,0},{20,4},{24,8},{28,12},{1,17},{... | collective-permute-start | bytes 1572872 | tf_op jit(solution)/shard_map/ppermute | solution.py:24
  39.5 24.8 %collective-permute-start.15 = (bf16[4,128,512]{2,1,0:T(8,128)(2,1)S(1)}, bf16[4,128,512]{2,1,0:T(8,128)(2,1)}, u32[]{:S(2)}, u32[]{:S(2)}) collective-permute-start(bf16[4,128,512]{2,1,0:T(8,128)(2,1)S(1)} %pad_maximum_fusion.2.refs_0_), channel_id=1, source_target_pairs={{0,8},{4,12},{8,0},{12,4},{16,24},{20,28},{24,16},{28,20},{1,9},{5... | collective-permute-start | bytes 1572872 | tf_op jit(solution)/shard_map/ppermute | solution.py:24
  66.2 13.9 %collective-permute-start.22 = (bf16[512,512]{1,0:T(8,128)(2,1)}, bf16[512,512]{1,0:T(8,128)(2,1)S(1)}, u32[]{:S(2)}, u32[]{:S(2)}) collective-permute-start(bf16[512,512]{1,0:T(8,128)(2,1)} %param.35), channel_id=1, source_target_pairs={{1,4},{3,6},{4,1},{6,3},{9,12},{11,14},{12,9},{14,11},{17,20},{19,... | collective-permute-start | bytes 1572872 | tf_op jit(solution)/shard_map/ppermute | solution.py:42
  106.6 18.4 %collective-permute-start.24 = (bf16[512,512]{1,0:T(8,128)(2,1)S(1)}, bf16[512,512]{1,0:T(8,128)(2,1)S(1)}, u32[]{:S(2)}, u32[]{:S(2)}) collective-permute-start(bf16[512,512]{1,0:T(8,128)(2,1)S(1)} %get-tuple-element.153), channel_id=1, source_target_pairs={{1,4},{3,6},{4,1},{6,3},{9,12},{11,14},{12,9},{14,11},{17,20},{19,... | collective-permute-start | bytes 1572872 | tf_op jit(solution)/shard_map/ppermute | solution.py:42
  139.4 18.0 %collective-permute-start.27 = (bf16[2,2,144,512]{3,2,1,0:T(8,128)(2,1)S(1)}, bf16[2,2,144,512]{3,2,1,0:T(8,128)(2,1)S(1)}, u32[]{:S(2)}, u32[]{:S(2)}) collective-permute-start(bf16[2,2,144,512]{3,2,1,0:T(8,128)(2,1)S(1)} %pad_maximum_fusion), channel_id=1, source_target_pairs={{0,8},{4,12},{8,0},{12,4},{16,24},{20,28},{24,16},{28,20},{1,9},{5... | collective-permute-start | bytes 1769480 | tf_op jit(solution)/shard_map/ppermute | solution.py:24
  140.7 16.7 %collective-permute-start.28 = (bf16[2,2,144,512]{3,2,1,0:T(8,128)(2,1)S(1)}, bf16[2,2,144,512]{3,2,1,0:T(8,128)(2,1)S(1)}, u32[]{:S(2)}, u32[]{:S(2)}) collective-permute-start(bf16[2,2,144,512]{3,2,1,0:T(8,128)(2,1)S(1)} %pad_maximum_fusion.1), channel_id=1, source_target_pairs={{0,16},{4,20},{8,24},{12,28},{16,0},{20,4},{24,8},{28,12},{1,17},{... | collective-permute-start | bytes 1769480 | tf_op jit(solution)/shard_map/ppermute | solution.py:24
  162.0 11.4 %collective-permute-start.35 = (bf16[2,2,64,512]{3,2,1,0:T(8,128)(2,1)S(1)}, bf16[2,2,64,512]{3,2,1,0:T(8,128)(2,1)S(1)}, u32[]{:S(2)}, u32[]{:S(2)}) collective-permute-start(bf16[2,2,64,512]{3,2,1,0:T(8,128)(2,1)S(1)} %pad_maximum_fusion.5), channel_id=1, source_target_pairs={{0,8},{4,12},{8,0},{12,4},{16,24},{20,28},{24,16},{28,20},{1,9},{5... | collective-permute-start | bytes 786440 | tf_op jit(solution)/shard_map/ppermute | solution.py:24
  163.0 10.4 %collective-permute-start.36 = (bf16[2,2,64,512]{3,2,1,0:T(8,128)(2,1)S(1)}, bf16[2,2,64,512]{3,2,1,0:T(8,128)(2,1)S(1)}, u32[]{:S(2)}, u32[]{:S(2)}) collective-permute-start(bf16[2,2,64,512]{3,2,1,0:T(8,128)(2,1)S(1)} %pad_maximum_fusion.6), channel_id=1, source_target_pairs={{0,16},{4,20},{8,24},{12,28},{16,0},{20,4},{24,8},{28,12},{1,17},{... | collective-permute-start | bytes 786440 | tf_op jit(solution)/shard_map/ppermute | solution.py:24
  167.3 11.4 %collective-permute-start.30 = (bf16[144,512]{1,0:T(8,128)(2,1)S(1)}, bf16[144,512]{1,0:T(8,128)(2,1)S(1)}, u32[]{:S(2)}, u32[]{:S(2)}) collective-permute-start(bf16[144,512]{1,0:T(8,128)(2,1)S(1)} %get-tuple-element.249), channel_id=1, source_target_pairs={{0,1},{1,0},{2,3},{3,2},{4,5},{5,4},{6,7},{7,6},{8,9},{9,8},{10,11... | collective-permute-start | bytes 442376 | tf_op jit(solution)/shard_map/ppermute | solution.py:29
  168.7 10.0 %collective-permute-start.33 = (bf16[144,512]{1,0:T(8,128)(2,1)S(1)}, bf16[144,512]{1,0:T(8,128)(2,1)S(1)}, u32[]{:S(2)}, u32[]{:S(2)}) collective-permute-start(bf16[144,512]{1,0:T(8,128)(2,1)S(1)} %get-tuple-element.247), channel_id=1, source_target_pairs={{0,3},{1,2},{2,1},{3,0},{4,7},{5,6},{6,5},{7,4},{8,11},{9,10},{10,... | collective-permute-start | bytes 442376 | tf_op jit(solution)/shard_map/ppermute | solution.py:29
  168.9 12.9 %collective-permute-start.32 = (bf16[144,512]{1,0:T(8,128)(2,1)S(1)}, bf16[144,512]{1,0:T(8,128)(2,1)S(1)}, u32[]{:S(2)}, u32[]{:S(2)}) collective-permute-start(bf16[144,512]{1,0:T(8,128)(2,1)S(1)} %get-tuple-element.248), channel_id=1, source_target_pairs={{0,2},{1,3},{2,0},{3,1},{4,6},{5,7},{6,4},{7,5},{8,10},{9,11},{10,... | collective-permute-start | bytes 442376 | tf_op jit(solution)/shard_map/ppermute | solution.py:29
  187.4 13.4 %collective-permute-start.45 = (bf16[512,512]{1,0:T(8,128)(2,1)S(1)}, bf16[512,512]{1,0:T(8,128)(2,1)S(1)}, u32[]{:S(2)}, u32[]{:S(2)}) collective-permute-start(bf16[512,512]{1,0:T(8,128)(2,1)S(1)} %fusion), channel_id=1, source_target_pairs={{1,4},{3,6},{4,1},{6,3},{9,12},{11,14},{12,9},{14,11},{17,20},{19,... | collective-permute-start | bytes 1572872 | tf_op jit(solution)/shard_map/ppermute | solution.py:42
  194.6 10.2 %collective-permute-start.43 = (bf16[208,512]{1,0:T(8,128)(2,1)S(1)}, bf16[208,512]{1,0:T(8,128)(2,1)S(1)}, u32[]{:S(2)}, u32[]{:S(2)}) collective-permute-start(bf16[208,512]{1,0:T(8,128)(2,1)S(1)} %pad_maximum_fusion.7.refs_0_), channel_id=1, source_target_pairs={{0,16},{4,20},{8,24},{12,28},{16,0},{20,4},{24,8},{28,12},{1,17},{... | collective-permute-start | bytes 638984 | tf_op jit(solution)/shard_map/ppermute | solution.py:24
  195.7 9.2 %collective-permute-start.42 = (bf16[208,512]{1,0:T(8,128)(2,1)S(1)}, bf16[208,512]{1,0:T(8,128)(2,1)S(1)}, u32[]{:S(2)}, u32[]{:S(2)}) collective-permute-start(bf16[208,512]{1,0:T(8,128)(2,1)S(1)} %pad_maximum_fusion.7.refs_0_), channel_id=1, source_target_pairs={{0,8},{4,12},{8,0},{12,4},{16,24},{20,28},{24,16},{28,20},{1,9},{5... | collective-permute-start | bytes 638984 | tf_op jit(solution)/shard_map/ppermute | solution.py:24
  (73 other events, 389.5 us)
